TPU v7x, 256 devices: a whole 4x4x8 slice. The times are simulated.
256 devices in a mesh: row: 32 (over z, x), col: 8 (over y, core).
Axes of the slice: x: 4, y: 4, z: 8, core: 2. Of those that a mesh axis runs over, the one named last changes fastest.
Arguments:
- u_panel: bfloat16 [64, 128, 2560], P('row', None, 'col'), may hold values from -6 to 6
- v_panel: bfloat16 [64, 128, 2560], P('row', None, 'col'), may hold values from -0.125 to 0.125
- ranks: int32 [64], P('row'), may hold values from 42 to 128
- inverse_t: float32 [2560, 2560], P('row', 'col'), may hold values from -1 to 2, as said below
Outputs:
- panel_v: bfloat16 [64, 128, 2560], P('row', None, 'col')
- update_left: bfloat16 [64, 8, 8, 128, 2560], P('row', 'col')
Inputs may be any that keep to these rules, and one draw needn't show every extreme that they name: inverse_t is upper triangular with its diagonal between 1 and 2.
All inputs are finite; a program needn't handle non-finite values.
Results may differ from a plain program's by a relative error of at most 0.006.
Values may be sent and summed in bfloat16 or wider, within the bound.
No kernel may reach another device: no remote copies, remote signals or barrier semaphores. Data moves between devices by JAX's collectives and lax.ppermute only.
A program may use at most 64 MiB of HBM per device.

v0:
```python
import jax
import jax.numpy as jnp
from jax import lax
from jax.sharding import PartitionSpec as P


def local(u_panel, v_panel, ranks, inverse_t):
    tile_count, rank_slots, slice_width = v_panel.shape
    within = lax.broadcasted_iota(jnp.int32, (1, rank_slots, 1), 1) < ranks[:, None, None]
    masked = jnp.where(within, v_panel, jnp.zeros_like(v_panel))
    whole_left, whole_right = (
        lax.all_gather(u_panel, "col", axis=2, tiled=True),
        lax.all_gather(masked, "col", axis=2, tiled=True),
    )
    inverse_block = lax.all_gather(inverse_t, "row", axis=0, tiled=True)
    order = whole_right.shape[2]
    solved_part = jnp.dot(
        whole_right.reshape(tile_count * rank_slots, order).astype(jnp.float32),
        inverse_block,
        precision=lax.Precision.HIGHEST,
        preferred_element_type=jnp.float32,
    )
    solved_part = solved_part.reshape(tile_count, rank_slots, slice_width).astype(jnp.bfloat16)
    solved = lax.all_gather(solved_part, "col", axis=2, tiled=True)
    row_count = lax.axis_size("row")
    col_count = lax.axis_size("col")
    round_count = row_count // col_count
    all_slices = lax.all_gather(solved_part, "row", axis=0, tiled=True)
    shaped = all_slices.reshape(round_count, col_count, tile_count, rank_slots, slice_width)
    arrived = lax.all_to_all(shaped, "col", split_axis=1, concat_axis=4, tiled=True)
    columns = arrived.reshape(round_count * tile_count, rank_slots, order)
    core_blocks = jnp.einsum(
        "skn,qln->sqkl", solved, columns, preferred_element_type=jnp.float32
    ).astype(jnp.bfloat16)
    left_update = jnp.einsum(
        "sqkl,skn->sqln", core_blocks, whole_left, preferred_element_type=jnp.float32
    ).astype(jnp.bfloat16)
    return (solved_part, left_update[:, None])


def solution(mesh):
    placed = (P("row", None, "col"), P("row", None, "col"), P("row"), P("row", "col"))
    return jax.shard_map(
        local,
        mesh=mesh,
        in_specs=placed,
        out_specs=(P("row", None, "col"), P("row", "col", None, None, None)),
        check_vma=False,
    )
```

profile of v0, /device:TPU:1, one launch (start us, length us, event | category | flops | bytes accessed | tf_op | source)
XLA Modules:
  0.0 318.6 jit_solution(16211173470784262466)
XLA Ops:
  7.2 0.0 all-gather.6.cloned.1.call-start
  7.2 0.7 iota_compare_fusion
  7.9 1.6 broadcast_select_fusion
  9.5 0.0 all-gather.6.cloned.1.call-update
  9.6 0.0 all-gather.8.cloned.1.call-start
  9.6 0.7 all-gather.8.cloned.1.call-update
  10.3 0.0 all-gather.10.cloned.1.call-start
  10.4 31.0 %all-gather.6.cloned.1.call-done = bf16[2,128,2560]{1,2,0:T(8,128)(2,1)} async-done(((bf16[2,128,320]{1,2,0:T(8,128)(2,1)}), bf16[2,128,2560]{1,2,0:T(8,128)(2,1)}) %all-gather.6.cloned.1.call-update) | async-done | bytes 1310736 | tf_op jit(solution)/shard_map/all_gather | solution.py:13
  41.3 80.5 %all-gather.8.cloned.1.call-done = f32[2560,320]{1,0:T(8,128)} async-done(((f32[80,320]{1,0:T(8,128)}), f32[2560,320]{1,0:T(8,128)}) %all-gather.8.cloned.1.call-update) | async-done | bytes 3276816 | tf_op jit(solution)/shard_map/all_gather | solution.py:15
  121.8 6.4 %fusion.11 = bf16[2,128,320]{1,2,0:T(8,128)(2,1)} fusion(bf16[2,128,2560]{1,2,0:T(8,128)(2,1)} %all-gather.6.cloned.1.call-done, f32[2560,320]{1,0:T(8,128)} %all-gather.8.cloned.1.call-done), kind=kOutput, calls=%fused_computation.8 | convolution fusion | flops 2516664320 | bytes 4751360 | tf_op jit(solution)/shard_map/dot_general | solution.py:17
  128.3 0.0 all-gather.10.cloned.1.call-update
  128.3 82.7 %all-gather.10.cloned.1.call-done = bf16[64,128,320]{1,2,0:T(8,128)(2,1)} async-done(((bf16[2,128,320]{1,2,0:T(8,128)(2,1)}), bf16[64,128,320]{1,2,0:T(8,128)(2,1)}) %all-gather.10.cloned.1.call-update) | async-done | bytes 5242896 | tf_op jit(solution)/shard_map/all_gather | solution.py:28
  211.0 5.4 %copy.9 = bf16[4,8,2,128,320]{3,4,2,0,1:T(8,128)(2,1)} copy(bf16[4,8,2,128,320]{3,4,2,1,0:T(8,128)(2,1)} %bitcast.40) | data formatting | bytes 10485760 | tf_op jit(solution)/shard_map/reshape | solution.py:29
  216.4 7.7 %all-to-all-start = ((bf16[4,8,2,128,320]{3,4,2,0,1:T(8,128)(2,1)}), bf16[4,8,2,128,320]{3,4,2,0,1:T(8,128)(2,1)}, u32[]{:S(2)}, u32[]{:S(2)}) async-start(bf16[4,8,2,128,320]{3,4,2,0,1:T(8,128)(2,1)} %copy.9), calls=%async_computation | async-start | bytes 10485760 | tf_op jit(solution)/shard_map/all_to_all | solution.py:30
  224.1 0.0 all-gather.14.cloned.1.call-start
  224.1 0.6 all-gather.14.cloned.1.call-update
  224.6 0.0 all-gather.12.cloned.1.call-start
  224.7 0.5 all-gather.12.cloned.1.call-update
  225.2 69.5 %all-to-all-done = bf16[4,8,2,128,320]{3,4,2,0,1:T(8,128)(2,1)} async-done(((bf16[4,8,2,128,320]{3,4,2,0,1:T(8,128)(2,1)}), bf16[4,8,2,128,320]{3,4,2,0,1:T(8,128)(2,1)}, u32[]{:S(2)}, u32[]{:S(2)}) %all-to-all-start) | async-done | bytes 5242912 | tf_op jit(solution)/shard_map/all_to_all | solution.py:30
  294.8 5.3 %copy.10 = bf16[4,8,2,128,320]{3,4,1,2,0:T(8,128)(2,1)} copy(bf16[4,8,2,128,320]{3,4,2,0,1:T(8,128)(2,1)} %all-to-all-done) | data formatting | bytes 10485760 | tf_op jit(solution)/shard_map/all_to_all | solution.py:30
  300.0 0.0 all-gather.14.cloned.1.call-done
  300.0 0.0 all-gather.12.cloned.1.call-done
  300.0 12.0 %convert_bitcast_fusion = bf16[2,1,8,128,2560]{4,3,2,1,0:T(8,128)(2,1)} fusion(bf16[2,128,2560]{1,2,0:T(8,128)(2,1)} %all-gather.14.cloned.1.call-done, bf16[8,128,2560,1]{1,2,0,3:T(8,128)(2,1)} %bitcast.39, bf16[2,128,2560]{1,2,0:T(8,128)(2,1)} %all-gather.12.cloned.1.call-done), kind=kOutput, calls=%fused_computation | convolution fusion | flops 2689859584 | bytes 18350080 | tf_op jit(solution)/shard_map/sqkl,skn->sqln/dot_general | solution.py:35
Async XLA Ops:
  7.2 34.1 %all-gather.6.cloned.1.call-start = ((), (), s32[]{:S(2)}) async-start(), calls=%async_computation.1 | async-start | bytes 1474560 | tf_op jit(solution)/shard_map/all_gather | solution.py:13
  9.6 112.3 %all-gather.8.cloned.1.call-start = ((), (), s32[]{:S(2)}) async-start(), calls=%async_computation.2 | async-start | bytes 4055040 | tf_op jit(solution)/shard_map/all_gather | solution.py:15
  10.3 200.7 %all-gather.10.cloned.1.call-start = ((), (), s32[]{:S(2)}) async-start(), calls=%async_computation.3 | async-start | bytes 5406720 | tf_op jit(solution)/shard_map/all_gather | solution.py:28
  216.4 78.4 %all-to-all-start = ((bf16[4,8,2,128,320]{3,4,2,0,1:T(8,128)(2,1)}), bf16[4,8,2,128,320]{3,4,2,0,1:T(8,128)(2,1)}, u32[]{:S(2)}, u32[]{:S(2)}) async-start(bf16[4,8,2,128,320]{3,4,2,0,1:T(8,128)(2,1)} %copy.9), calls=%async_computation | async-start | bytes 10485760 | tf_op jit(solution)/shard_map/all_to_all | solution.py:30
  224.1 76.0 %all-gather.14.cloned.1.call-start = ((), (), s32[]{:S(2)}) async-start(), calls=%async_computation.5 | async-start | bytes 1474560 | tf_op jit(solution)/shard_map/all_gather | solution.py:12
  224.6 75.4 %all-gather.12.cloned.1.call-start = ((), (), s32[]{:S(2)}) async-start(), calls=%async_computation.4 | async-start | bytes 1474560 | tf_op jit(solution)/shard_map/all_gather | solution.py:24
Sparse Core Ops, SparseCore 0:
  10.4 30.8 all-gather.5
  43.9 77.9 all-gather.7
  128.4 82.5 all-gather.9
  226.4 26.8 all-gather.13
  255.5 29.9 all-gather.11
where the time goes:
time: 319 us
  waiting for transfers between devices  266 us (83%)
  matrix products  18.4 us (6%)
  between operations  13.8 us (4%)
  local copies, waits for them, and re-layouts  10.6 us (3%)
  starting transfers between devices  7.88 us (2%)
    all_gather x1, waiting for transfers between devices, local(): all_slices = lax.all_gather(solved_part, 'row', axis=0, tiled=True)  82.7 us
    all_gather x1, waiting for transfers between devices, local(): inverse_block = lax.all_gather(inverse_t, 'row', axis=0, tiled=True)  80.5 us
    all_to_all x1, waiting for transfers between devices, local(): lax.all_to_all(shaped, 'col', split_axis=1, concat_axis=4, tiled=True)  69.5 us
    all_gather x1, waiting for transfers between devices, local(): lax.all_gather(masked, 'col', axis=2, tiled=True)  31 us
    dot_general x1, matrix products, local(): jnp.einsum('sqkl,skn->sqln', core_blocks, whole_left, preferred_element_t...  12 us
    all_to_all x1, starting transfers between devices, local(): lax.all_to_all(shaped, 'col', split_axis=1, concat_axis=4, tiled=True)  7.72 us
    dot_general x1, matrix products, local(): jnp.dot(whole_right.reshape(tile_count * rank_slots, order).astype(jnp.fl...  6.42 us
  transfers between devices with their start and end apart: 6, of which 4 were waited for; matrix products, arithmetic and copies ran while one was open for 2% of the time, Pallas kernels for 0%

commit v1 on v0

v1 whole, which is shorter than its diff:
```python
import jax
import jax.numpy as jnp
from jax import lax
from jax.experimental import pallas as pl
from jax.experimental.pallas import tpu as pltpu
from jax.sharding import Mesh, PartitionSpec as P

AXES = ("z", "x", "y", "core")
SIZES = (8, 4, 4, 2)


def permute(value, target):
    pairs = []
    for z in range(8):
        for x in range(4):
            for y in range(4):
                for core in range(2):
                    goal = [p % s for p, s in zip(target(z, x, y, core), SIZES)]
                    source = ((z * 4 + x) * 4 + y) * 2 + core
                    pairs.append((source, ((goal[0] * 4 + goal[1]) * 4 + goal[2]) * 2 + goal[3]))
    return lax.ppermute(value, AXES, pairs)


def along_x(value, step):
    return permute(value, lambda z, x, y, core: (z, x + step, y, core))


def ring_of_four(value, shift, dim):
    below, above = shift(value, 1), shift(value, -1)
    half = value.shape[dim] // 2
    first = lax.slice_in_dim(below, 0, half, axis=dim)
    second = lax.slice_in_dim(above, half, value.shape[dim], axis=dim)
    across = jnp.concatenate([shift(first, 1), shift(second, -1)], axis=dim)
    return [value, above, across, below]


def along_y(value, step):
    return permute(value, lambda z, x, y, core: (z, x, y + step, core))


def along_z(value, step):
    return permute(value, lambda z, x, y, core: (z + step, x, y, core))


def ring_of_eight(value, shift):
    below, above, back = [value], [value], []
    for _ in range(3):
        below.append(shift(below[-1], 1))
        above.append(shift(above[-1], -1))
    half = value.shape[1] // 2
    first = shift(below[3][:, :half], 1)
    second = shift(above[3][:, half:], -1)
    across = jnp.concatenate([first, second], axis=1)
    return above + [across] + below[:0:-1]


def partial_kernel(place, *refs):
    rows, lines, kept, given = refs[:4], refs[4:12], refs[12], refs[13]
    kept[...] = jnp.zeros_like(kept)
    given[...] = jnp.zeros_like(given)
    z, core, mid = place[0], place[1], place[2]
    for far, line in enumerate(lines):
        at = lax.rem(z + far, 8)
        y = lax.rem(lax.div(at, 2) + 4 - mid, 4)
        mine = lax.rem(at, 2) == core
        column = jnp.concatenate([line[0], line[1]], axis=1)
        for step, row in enumerate(rows):
            block = jnp.concatenate([row[y, 0], row[y, 1]], axis=1)
            part = lax.dot_general(column, block, (((0,), (0,)), ((), ())), preferred_element_type=jnp.float32)

            @pl.when(mine)
            def _():
                kept[step] += part

            @pl.when(jnp.logical_not(mine))
            def _():
                given[step] += part


def partial_cores(rows, lines):
    place = jnp.stack([lax.axis_index(name) for name in ("z", "core", "y")]).astype(jnp.int32)
    wide = 2 * rows[0].shape[-1]
    vmem = pl.BlockSpec(memory_space=pltpu.VMEM)
    out = jax.ShapeDtypeStruct((4, wide, wide), jnp.float32)
    return pl.pallas_call(
        partial_kernel,
        out_shape=(out, out),
        in_specs=[pl.BlockSpec(memory_space=pltpu.SMEM)] + [vmem] * 12,
        out_specs=(vmem, vmem),
        compiler_params=pltpu.CompilerParams(vmem_limit_bytes=32 * 2**20),
        cost_estimate=pl.CostEstimate(flops=1400000000, bytes_accessed=6000000, transcendentals=0),
    )(place, *rows, *lines)


def apply_kernel(place, cores, left, out):
    step = pl.program_id(1)
    for tile in range(2):
        for column in range(2):
            block = cores[step, column * 128:(column + 1) * 128, tile * 128:(tile + 1) * 128]
            out[tile, 0, column] = lax.dot_general(
                block, left[tile], (((1,), (1,)), ((), ())), preferred_element_type=jnp.float32
            ).astype(out.dtype)


def apply_cores(cores, left):
    tiles, order, slots = left.shape
    place = lax.axis_index("x").astype(jnp.int32).reshape(1)
    parts = 2
    span = order // parts
    grid_spec = pltpu.PrefetchScalarGridSpec(
        num_scalar_prefetch=1,
        grid=(parts, 4),
        in_specs=[
            pl.BlockSpec(cores.shape, lambda n, step, place: (0, 0, 0)),
            pl.BlockSpec((tiles, span, slots), lambda n, step, place: (0, n, 0)),
        ],
        out_specs=pl.BlockSpec(
            (tiles, 1, 2, slots, span), lambda n, step, place: (0, 0, lax.rem(place[0] + 4 - step, 4), 0, n)
        ),
    )
    return pl.pallas_call(
        apply_kernel,
        out_shape=jax.ShapeDtypeStruct((tiles, 1, 8, slots, order), jnp.bfloat16),
        grid_spec=grid_spec,
        compiler_params=pltpu.CompilerParams(vmem_limit_bytes=32 * 2**20),
        cost_estimate=pl.CostEstimate(flops=1400000000, bytes_accessed=12000000, transcendentals=0),
    )(place, cores, left)


def local(u_panel, v_panel, ranks, inverse_t):
    tiles, slots, width = v_panel.shape
    x = lax.axis_index("x")
    within = lax.broadcasted_iota(jnp.int32, (1, 1, slots), 2) < ranks[:, None, None]
    own = jnp.swapaxes(v_panel, 1, 2)
    own = jnp.where(within, own, jnp.zeros_like(own))
    right = lax.all_gather(own, ("y", "core"), axis=1, tiled=True)
    left = lax.all_gather(jnp.swapaxes(u_panel, 1, 2), ("y", "core"), axis=1, tiled=True)

    depth = inverse_t.shape[0]
    rows = lax.broadcasted_iota(jnp.int32, inverse_t.shape, 0) + depth * (lax.axis_index("z") * 4 + x)
    cols = lax.broadcasted_iota(jnp.int32, inverse_t.shape, 1) + width * (lax.axis_index("y") * 2 + lax.axis_index("core"))
    nearest = lax.reduce_precision(inverse_t, 8, 7)
    rounded = nearest.astype(jnp.bfloat16)
    rest = jnp.where(rows == cols, inverse_t - nearest, 0.0)
    rest = jnp.sum(rest, axis=0, keepdims=True).astype(jnp.bfloat16)
    sent = jnp.concatenate([rounded, jnp.pad(rest, ((0, 15), (0, 0)))], axis=0)
    planes = lax.all_to_all(
        jnp.broadcast_to(sent[None], (8,) + sent.shape), "z", split_axis=0, concat_axis=0, tiled=True
    )
    blocks = ring_of_four(planes, along_x, 0)
    by_x = right.reshape(tiles, 8, 4, depth, slots)
    total = jnp.zeros((tiles, width, slots), jnp.float32)
    diagonal = jnp.zeros((width,), jnp.float32)
    for step, block in enumerate(blocks):
        part = lax.dynamic_index_in_dim(by_x, (x + step) % 4, axis=2, keepdims=False)
        total = total + jnp.einsum(
            "zmn,tzmk->tnk", block[:, :depth], part, preferred_element_type=jnp.float32
        )
        diagonal = diagonal + jnp.sum(block[:, depth].astype(jnp.float32), axis=0)
    total = total + diagonal[None, :, None] * own.astype(jnp.float32)
    solved = total.astype(jnp.bfloat16)

    moved = permute(
        solved,
        lambda z, x, y, core: (2 * y + x % 2, z // 2, 2 * (z % 2) + x // 2, core),
    )
    rows = ring_of_four(jnp.stack(ring_of_four(solved, along_y, 1)), along_x, 0)
    lines = ring_of_eight(moved, along_z)
    kept, given = partial_cores(rows, lines)
    given = permute(given, lambda z, x, y, core: (z, x, y, core + 1))
    cores = (kept + given).astype(jnp.bfloat16)
    pieces = [cores[0]] + [along_x(cores[step], step) for step in range(1, 4)]
    update = apply_cores(jnp.stack(pieces), left)
    return jnp.swapaxes(solved, 1, 2), update


def solution(mesh):
    fine = Mesh(mesh.devices.reshape(SIZES), AXES)
    row, col = ("z", "x"), ("y", "core")
    placed = (P(row, None, col), P(row, None, col), P(row), P(row, col))
    return jax.shard_map(
        local,
        mesh=fine,
        in_specs=placed,
        out_specs=(P(row, None, col), P(row, col, None, None, None)),
        check_vma=False,
    )
```

time: 319 us -> 175 us (0.55)
  the two profiles are of different devices: /device:TPU:1 before, /device:TPU:8 now
where the time goes in v1:
time: 175 us; the launch traced here: 174 us
  waiting for transfers between devices  64.7 us (37%)
  starting transfers between devices  38.2 us (22%)
  blocking collectives  27.2 us (16%)
  Pallas kernels  17.4 us (10%)
  between operations  14.4 us (8%)
  other arithmetic  5.07 us (3%)
  matrix products  4.23 us (2%)
  local copies, waits for them, and re-layouts  3.11 us (2%)
    ppermute x25, waiting for transfers between devices, permute(): return lax.ppermute(value, AXES, pairs)  64.6 us
    ppermute x25, starting transfers between devices, permute(): return lax.ppermute(value, AXES, pairs)  38.2 us
    all_to_all x1, blocking collectives, local(): lax.all_to_all(jnp.broadcast_to(sent[None], (8,) + sent.shape), 'z', spli...  27.2 us
    pallas_call x1, Pallas kernels, partial_cores(): pl.pallas_call(partial_kernel, out_shape=(out, out), in_specs=[pl.BlockSp...  10.5 us
    pallas_call x1, Pallas kernels, apply_cores(): pl.pallas_call(apply_kernel, out_shape=jax.ShapeDtypeStruct((tiles, 1, 8,...  6.92 us
    dot_general x4, matrix products, local(): jnp.einsum('zmn,tzmk->tnk', block[:, :depth], part, preferred_element_typ...  4.23 us
  transfers between devices with their start and end apart: 27, of which 13 were waited for; matrix products, arithmetic and copies ran while one was open for 2% of the time, Pallas kernels for 6%

profile of v1, /device:TPU:8, one launch (start us, length us, event | category | flops | bytes accessed | tf_op | source)
XLA Modules:
  0.0 174.3 jit_solution(12461654424640736777)
XLA Ops:
  7.2 0.0 all-gather.3.cloned.1.call-start
  7.2 0.7 iota_compare_fusion.1
  7.9 1.6 fusion.13
  9.5 0.0 all-gather.3.cloned.1.call-update
  9.6 0.0 all-gather.5.cloned.1.call-start
  9.6 1.0 reduce-precision_convert_fusion
  10.7 0.1 broadcast_in_dim.27
  10.7 27.2 %all_to_all.5 = bf16[8,96,320]{2,1,0:T(8,128)(2,1)S(1)} all-to-all(bf16[8,96,320]{2,1,0:T(8,128)(2,1)S(1)} %broadcast_in_dim.27), channel_id=1, replica_groups=mesh['z'=8,'x'=4,'y'=4,'core'=2] {'z'}, dimensions={0} | all-to-all | bytes 983040 | tf_op jit(solution)/shard_map/all_to_all | solution.py:147
  37.9 1.5 collective-permute-start.1
  39.4 1.7 %collective-permute-start = (bf16[8,96,320]{2,1,0:T(8,128)(2,1)S(1)}, bf16[8,96,320]{2,1,0:T(8,128)(2,1)S(1)}, u32[]{:S(2)}, u32[]{:S(2)}) collective-permute-start(bf16[8,96,320]{2,1,0:T(8,128)(2,1)S(1)} %all_to_all.5), channel_id=1, source_target_pairs={{0,24},{1,25},{2,26},{3,27},{4,28},{5,29},{6,30},{7,31},{8,0},{9,1... | collective-permute-start | bytes 1474568 | tf_op jit(solution)/shard_map/ppermute | solution.py:21
  41.1 11.3 %collective-permute-done.1 = bf16[8,96,320]{2,1,0:T(8,128)(2,1)S(1)} collective-permute-done((bf16[8,96,320]{2,1,0:T(8,128)(2,1)S(1)}, bf16[8,96,320]{2,1,0:T(8,128)(2,1)S(1)}, u32[]{:S(2)}, u32[]{:S(2)}) %collective-permute-start.1) | collective-permute-done | bytes 491552 | tf_op jit(solution)/shard_map/ppermute | solution.py:21
  52.5 0.4 collective-permute-start.2
  53.0 3.0 %collective-permute-start.3 = (bf16[4,96,320]{2,1,0:T(8,128)(2,1)S(1)}, bf16[4,96,320]{2,1,0:T(8,128)(2,1)S(1)}, u32[]{:S(2)}, u32[]{:S(2)}) collective-permute-start(bf16[4,96,320]{2,1,0:T(8,128)(2,1)S(1)} %slice.83), channel_id=1, source_target_pairs={{0,24},{1,25},{2,26},{3,27},{4,28},{5,29},{6,30},{7,31},{8,0},{9,1... | collective-permute-start | bytes 737288 | tf_op jit(solution)/shard_map/ppermute | solution.py:21
  56.0 4.5 %collective-permute-done.2 = bf16[4,96,320]{2,1,0:T(8,128)(2,1)S(1)} collective-permute-done((bf16[4,96,320]{2,1,0:T(8,128)(2,1)S(1)}, bf16[4,96,320]{2,1,0:T(8,128)(2,1)S(1)}, u32[]{:S(2)}, u32[]{:S(2)}) %collective-permute-start.2) | collective-permute-done | bytes 245792 | tf_op jit(solution)/shard_map/ppermute | solution.py:21
  60.5 0.0 collective-permute-done.3
  60.6 0.0 all-gather.3.cloned.1.call-done
  60.7 1.4 convolution_bitcast_fusion.1
  62.1 0.0 copy-start.1
  62.1 1.4 convolution_bitcast_fusion.3
  63.5 0.4 convolution_bitcast_fusion
  63.9 1.1 add_convert_fusion.1
  65.0 0.1 fusion.3
  65.1 1.7 collective-permute-start.5
  66.7 0.4 collective-permute-start.4
  67.2 3.4 %collective-permute-done.5 = bf16[2,320,128]{2,1,0:T(8,128)(2,1)S(1)} collective-permute-done((bf16[2,320,128]{2,1,0:T(8,128)(2,1)S(1)}, bf16[2,320,128]{2,1,0:T(8,128)(2,1)S(1)}, u32[]{:S(2)}, u32[]{:S(2)}) %collective-permute-start.5) | collective-permute-done | bytes 163872 | tf_op jit(solution)/shard_map/ppermute | solution.py:21
  70.6 1.6 collective-permute-start.6
  72.2 0.0 collective-permute-done.4
  72.2 1.0 collective-permute-start.7
  73.1 2.3 %collective-permute-done.6 = bf16[2,160,128]{2,1,0:T(8,128)(2,1)S(1)} collective-permute-done((bf16[2,160,128]{2,1,0:T(8,128)(2,1)S(1)}, bf16[2,160,128]{2,1,0:T(8,128)(2,1)S(1)}, u32[]{:S(2)}, u32[]{:S(2)}) %collective-permute-start.6) | collective-permute-done | bytes 81952 | tf_op jit(solution)/shard_map/ppermute | solution.py:21
  75.4 1.3 collective-permute-done.7
  76.7 0.1 pad_maximum_fusion.refs_0_
  76.8 0.8 collective-permute-start.9
  77.6 2.6 %collective-permute-start.8 = (bf16[4,2,320,128]{3,2,1,0:T(8,128)(2,1)S(1)}, bf16[4,2,320,128]{3,2,1,0:T(8,128)(2,1)S(1)}, u32[]{:S(2)}, u32[]{:S(2)}) collective-permute-start(bf16[4,2,320,128]{3,2,1,0:T(8,128)(2,1)S(1)} %pad_maximum_fusion.refs_0_), channel_id=1, source_target_pairs={{0,24},{1,25},{2,26},{3,27},{4,28},{5,29},{6,30},{7,31},{8,0},{9,1... | collective-permute-start | bytes 1966088 | tf_op jit(solution)/shard_map/ppermute | solution.py:21
  80.2 3.3 %collective-permute-start.12 = (bf16[2,320,128]{2,1,0:T(8,128)(2,1)S(1)}, bf16[2,320,128]{2,1,0:T(8,128)(2,1)S(1)}, u32[]{:S(2)}, u32[]{:S(2)}) collective-permute-start(bf16[2,320,128]{2,1,0:T(8,128)(2,1)S(1)} %fusion.3), channel_id=1, source_target_pairs={{0,0},{1,1},{2,64},{3,65},{4,128},{5,129},{6,192},{7,193},{8,32},{... | collective-permute-start | bytes 491528 | tf_op jit(solution)/shard_map/ppermute | solution.py:21
  83.5 22.1 %collective-permute-done.12.refs_4_ = bf16[2,320,128]{2,1,0:T(8,128)(2,1)S(1)} collective-permute-done((bf16[2,320,128]{2,1,0:T(8,128)(2,1)S(1)}, bf16[2,320,128]{2,1,0:T(8,128)(2,1)S(1)}, u32[]{:S(2)}, u32[]{:S(2)}) %collective-permute-start.12) | collective-permute-done | bytes 163872 | tf_op jit(solution)/shard_map/ppermute | solution.py:21
  105.6 0.0 collective-permute-start.16
  105.6 3.2 %collective-permute-start.13 = (bf16[2,320,128]{2,1,0:T(8,128)(2,1)S(1)}, bf16[2,320,128]{2,1,0:T(8,128)(2,1)S(1)}, u32[]{:S(2)}, u32[]{:S(2)}) collective-permute-start(bf16[2,320,128]{2,1,0:T(8,128)(2,1)S(1)} %collective-permute-done.12.refs_4_), channel_id=1, source_target_pairs={{0,224},{1,225},{2,226},{3,227},{4,228},{5,229},{6,230},{7,231},{8... | collective-permute-start | bytes 491528 | tf_op jit(solution)/shard_map/ppermute | solution.py:21
  108.8 3.3 %collective-permute-done.16.refs_11_ = bf16[2,320,128]{2,1,0:T(8,128)(2,1)S(1)} collective-permute-done((bf16[2,320,128]{2,1,0:T(8,128)(2,1)S(1)}, bf16[2,320,128]{2,1,0:T(8,128)(2,1)S(1)}, u32[]{:S(2)}, u32[]{:S(2)}) %collective-permute-start.16) | collective-permute-done | bytes 163872 | tf_op jit(solution)/shard_map/ppermute | solution.py:21
  112.1 0.0 collective-permute-start.17
  112.1 3.2 %collective-permute-start.14 = (bf16[2,320,128]{2,1,0:T(8,128)(2,1)S(1)}, bf16[2,320,128]{2,1,0:T(8,128)(2,1)S(1)}, u32[]{:S(2)}, u32[]{:S(2)}) collective-permute-start(bf16[2,320,128]{2,1,0:T(8,128)(2,1)S(1)} %collective-permute-done.13.refs_5_), channel_id=1, source_target_pairs={{0,224},{1,225},{2,226},{3,227},{4,228},{5,229},{6,230},{7,231},{8... | collective-permute-start | bytes 491528 | tf_op jit(solution)/shard_map/ppermute | solution.py:21
  115.3 3.3 %collective-permute-done.17.refs_10_ = bf16[2,320,128]{2,1,0:T(8,128)(2,1)S(1)} collective-permute-done((bf16[2,320,128]{2,1,0:T(8,128)(2,1)S(1)}, bf16[2,320,128]{2,1,0:T(8,128)(2,1)S(1)}, u32[]{:S(2)}, u32[]{:S(2)}) %collective-permute-start.17) | collective-permute-done | bytes 163872 | tf_op jit(solution)/shard_map/ppermute | solution.py:21
  118.6 3.2 %collective-permute-start.15 = (bf16[2,320,128]{2,1,0:T(8,128)(2,1)S(1)}, bf16[2,320,128]{2,1,0:T(8,128)(2,1)S(1)}, u32[]{:S(2)}, u32[]{:S(2)}) collective-permute-start(bf16[2,320,128]{2,1,0:T(8,128)(2,1)S(1)} %collective-permute-done.14.refs_6_), channel_id=1, source_target_pairs={{0,224},{1,225},{2,226},{3,227},{4,228},{5,229},{6,230},{7,231},{8... | collective-permute-start | bytes 491528 | tf_op jit(solution)/shard_map/ppermute | solution.py:21
  121.9 0.8 slice.92
  122.6 0.7 slice.93
  123.4 3.2 %collective-permute-start.11 = (bf16[2,2,320,128]{3,2,1,0:T(8,128)(2,1)}, bf16[2,2,320,128]{3,2,1,0:T(8,128)(2,1)}, u32[]{:S(2)}, u32[]{:S(2)}) collective-permute-start(bf16[2,2,320,128]{3,2,1,0:T(8,128)(2,1)} %slice.93), channel_id=1, source_target_pairs={{0,24},{1,25},{2,26},{3,27},{4,28},{5,29},{6,30},{7,31},{8,0},{9,1... | collective-permute-start | bytes 983048 | tf_op jit(solution)/shard_map/ppermute | solution.py:21
  126.6 0.0 all-gather.5.cloned.1.call-update
  126.7 0.1 collective-permute-start.19
  126.8 3.3 %collective-permute-start.20 = (bf16[2,160,128]{2,1,0:T(8,128)(2,1)S(1)}, bf16[2,160,128]{2,1,0:T(8,128)(2,1)S(1)}, u32[]{:S(2)}, u32[]{:S(2)}) collective-permute-start(bf16[2,160,128]{2,1,0:T(8,128)(2,1)S(1)} %slice.95), channel_id=1, source_target_pairs={{0,224},{1,225},{2,226},{3,227},{4,228},{5,229},{6,230},{7,231},{8... | collective-permute-start | bytes 245768 | tf_op jit(solution)/shard_map/ppermute | solution.py:21
  130.1 0.1 pad_add_fusion.place
  130.1 2.2 %collective-permute-done.19 = bf16[2,160,128]{2,1,0:T(8,128)(2,1)S(1)} collective-permute-done((bf16[2,160,128]{2,1,0:T(8,128)(2,1)S(1)}, bf16[2,160,128]{2,1,0:T(8,128)(2,1)S(1)}, u32[]{:S(2)}, u32[]{:S(2)}) %collective-permute-start.19) | collective-permute-done | bytes 81952 | tf_op jit(solution)/shard_map/ppermute | solution.py:21
  132.4 1.0 pad_maximum_fusion.1.refs_2_
  133.5 10.5 %shard_map.59 = (f32[4,256,256]{2,1,0:T(8,128)S(1)}, f32[4,256,256]{2,1,0:T(8,128)S(1)}) custom-call(s32[3]{0:T(128)S(1)} %pad_add_fusion.place, bf16[4,2,320,128]{3,2,1,0:T(8,128)(2,1)S(1)} %pad_maximum_fusion.refs_0_, bf16[4,2,320,128]{3,2,1,0:T(8,128)(2,1)S(1)} %collective-permute-done.8.refs_1_, bf16[4,2,320,128]{3,2,1,0:T(8,128)(2,1)S(1)} %pad_maximum_fusion.1.refs_2_, ...), custom_call_target="tpu_custom_call" | custom-call | flops 1400000000 | bytes 6000000 | tf_op jit(solution)/shard_map/pallas_call | solution.py:85
  144.0 0.1 collective-permute-start.21
  144.1 2.6 %collective-permute-done.21 = f32[4,256,256]{2,1,0:T(8,128)S(1)} collective-permute-done((f32[4,256,256]{2,1,0:T(8,128)S(1)}, f32[4,256,256]{2,1,0:T(8,128)S(1)}, u32[]{:S(2)}, u32[]{:S(2)}) %collective-permute-start.21) | collective-permute-done | bytes 1048608 | tf_op jit(solution)/shard_map/ppermute | solution.py:21
  146.7 0.2 add_convert_fusion
  147.0 2.9 %collective-permute-start.24 = (bf16[256,256]{1,0:T(8,128)(2,1)S(1)}, bf16[256,256]{1,0:T(8,128)(2,1)S(1)}, u32[]{:S(2)}, u32[]{:S(2)}) collective-permute-start(bf16[256,256]{1,0:T(8,128)(2,1)S(1)} %get-tuple-element.7), channel_id=1, source_target_pairs={{0,24},{1,25},{2,26},{3,27},{4,28},{5,29},{6,30},{7,31},{8,0},{9,1... | collective-permute-start | bytes 393224 | tf_op jit(solution)/shard_map/ppermute | solution.py:21
  149.8 1.0 collective-permute-start.22
  150.8 4.9 %collective-permute-done.24 = bf16[256,256]{1,0:T(8,128)(2,1)S(1)} collective-permute-done((bf16[256,256]{1,0:T(8,128)(2,1)S(1)}, bf16[256,256]{1,0:T(8,128)(2,1)S(1)}, u32[]{:S(2)}, u32[]{:S(2)}) %collective-permute-start.24) | collective-permute-done | bytes 131104 | tf_op jit(solution)/shard_map/ppermute | solution.py:21
  155.7 2.0 %collective-permute-done.23 = bf16[256,256]{1,0:T(8,128)(2,1)S(1)} collective-permute-done((bf16[256,256]{1,0:T(8,128)(2,1)S(1)}, bf16[256,256]{1,0:T(8,128)(2,1)S(1)}, u32[]{:S(2)}, u32[]{:S(2)}) %collective-permute-start.23) | collective-permute-done | bytes 131104 | tf_op jit(solution)/shard_map/ppermute | solution.py:21
  157.7 1.4 collective-permute-done.22
  159.1 0.1 pad_maximum_fusion.2.cores
  159.2 0.0 all-gather.5.cloned.1.call-done.left
  159.2 1.3 copy-done
  160.5 6.9 %shard_map.60 = bf16[2,1,8,128,2560]{4,3,2,1,0:T(8,128)(2,1)} custom-call(s32[1]{0:T(128)} %bitcast.18.place, bf16[4,256,256]{2,1,0:T(8,128)(2,1)S(1)} %pad_maximum_fusion.2.cores, bf16[2,2560,128]{2,1,0:T(8,128)(2,1)S(1)} %copy-done), custom_call_target="tpu_custom_call" | custom-call | flops 1400000000 | bytes 12000000 | tf_op jit(solution)/shard_map/pallas_call | solution.py:121
  (37 shorter events, 0.4 us)
Async XLA Ops:
  7.2 53.5 %all-gather.3.cloned.1.call-start = ((), (), s32[]{:S(2)}) async-start(), calls=%async_computation.1 | async-start | bytes 1474560 | tf_op jit(solution)/shard_map/all_gather | solution.py:136
  9.6 149.6 %all-gather.5.cloned.1.call-start = ((), (), s32[]{:S(2)}) async-start(), calls=%async_computation.2 | async-start | bytes 1474560 | tf_op jit(solution)/shard_map/all_gather | solution.py:137
  37.9 14.5 %collective-permute-start.1 = (bf16[8,96,320]{2,1,0:T(8,128)(2,1)S(1)}, bf16[8,96,320]{2,1,0:T(8,128)(2,1)S(1)}, u32[]{:S(2)}, u32[]{:S(2)}) collective-permute-start(bf16[8,96,320]{2,1,0:T(8,128)(2,1)S(1)} %all_to_all.5), channel_id=1, source_target_pairs={{0,8},{1,9},{2,10},{3,11},{4,12},{5,13},{6,14},{7,15},{8,16},{9,17... | collective-permute-start | bytes 1474568 | tf_op jit(solution)/shard_map/ppermute | solution.py:21
  39.4 13.5 %collective-permute-start = (bf16[8,96,320]{2,1,0:T(8,128)(2,1)S(1)}, bf16[8,96,320]{2,1,0:T(8,128)(2,1)S(1)}, u32[]{:S(2)}, u32[]{:S(2)}) collective-permute-start(bf16[8,96,320]{2,1,0:T(8,128)(2,1)S(1)} %all_to_all.5), channel_id=1, source_target_pairs={{0,24},{1,25},{2,26},{3,27},{4,28},{5,29},{6,30},{7,31},{8,0},{9,1... | collective-permute-start | bytes 1474568 | tf_op jit(solution)/shard_map/ppermute | solution.py:21
  52.5 8.0 %collective-permute-start.2 = (bf16[4,96,320]{2,1,0:T(8,128)(2,1)S(1)}, bf16[4,96,320]{2,1,0:T(8,128)(2,1)S(1)}, u32[]{:S(2)}, u32[]{:S(2)}) collective-permute-start(bf16[4,96,320]{2,1,0:T(8,128)(2,1)S(1)} %slice.82), channel_id=1, source_target_pairs={{0,8},{1,9},{2,10},{3,11},{4,12},{5,13},{6,14},{7,15},{8,16},{9,17... | collective-permute-start | bytes 737288 | tf_op jit(solution)/shard_map/ppermute | solution.py:21
  53.0 7.6 %collective-permute-start.3 = (bf16[4,96,320]{2,1,0:T(8,128)(2,1)S(1)}, bf16[4,96,320]{2,1,0:T(8,128)(2,1)S(1)}, u32[]{:S(2)}, u32[]{:S(2)}) collective-permute-start(bf16[4,96,320]{2,1,0:T(8,128)(2,1)S(1)} %slice.83), channel_id=1, source_target_pairs={{0,24},{1,25},{2,26},{3,27},{4,28},{5,29},{6,30},{7,31},{8,0},{9,1... | collective-permute-start | bytes 737288 | tf_op jit(solution)/shard_map/ppermute | solution.py:21
  60.7 2.9 %copy-start.2 = (bf16[2,2560,128]{2,1,0:T(8,128)(2,1)S(1)}, bf16[2,2560,128]{2,1,0:T(8,128)(2,1)}, u32[]{:S(2)}) copy-start(bf16[2,2560,128]{2,1,0:T(8,128)(2,1)} %all-gather.3.cloned.1.call-done) | copy-start | bytes 3932164
  62.1 1.8 %copy-start.1 = (bf16[2,128,320]{1,2,0:T(8,128)(2,1)S(1)}, bf16[2,128,320]{1,2,0:T(8,128)(2,1)}, u32[]{:S(2)}) copy-start(bf16[2,128,320]{1,2,0:T(8,128)(2,1)} %param.5) | copy-start | bytes 491524
  65.1 5.5 %collective-permute-start.5 = (bf16[2,320,128]{2,1,0:T(8,128)(2,1)S(1)}, bf16[2,320,128]{2,1,0:T(8,128)(2,1)S(1)}, u32[]{:S(2)}, u32[]{:S(2)}) collective-permute-start(bf16[2,320,128]{2,1,0:T(8,128)(2,1)S(1)} %fusion.3), channel_id=1, source_target_pairs={{0,2},{1,3},{2,4},{3,5},{4,6},{5,7},{6,0},{7,1},{8,10},{9,11},{10,... | collective-permute-start | bytes 491528 | tf_op jit(solution)/shard_map/ppermute | solution.py:21
  66.7 5.4 %collective-permute-start.4 = (bf16[2,320,128]{2,1,0:T(8,128)(2,1)S(1)}, bf16[2,320,128]{2,1,0:T(8,128)(2,1)S(1)}, u32[]{:S(2)}, u32[]{:S(2)}) collective-permute-start(bf16[2,320,128]{2,1,0:T(8,128)(2,1)S(1)} %fusion.3), channel_id=1, source_target_pairs={{0,6},{1,7},{2,0},{3,1},{4,2},{5,3},{6,4},{7,5},{8,14},{9,15},{10,... | collective-permute-start | bytes 491528 | tf_op jit(solution)/shard_map/ppermute | solution.py:21
  70.6 4.8 %collective-permute-start.6 = (bf16[2,160,128]{2,1,0:T(8,128)(2,1)S(1)}, bf16[2,160,128]{2,1,0:T(8,128)(2,1)S(1)}, u32[]{:S(2)}, u32[]{:S(2)}) collective-permute-start(bf16[2,160,128]{2,1,0:T(8,128)(2,1)S(1)} %slice.90), channel_id=1, source_target_pairs={{0,2},{1,3},{2,4},{3,5},{4,6},{5,7},{6,0},{7,1},{8,10},{9,11},{10,... | collective-permute-start | bytes 245768 | tf_op jit(solution)/shard_map/ppermute | solution.py:21
  72.2 4.5 %collective-permute-start.7 = (bf16[2,160,128]{2,1,0:T(8,128)(2,1)S(1)}, bf16[2,160,128]{2,1,0:T(8,128)(2,1)S(1)}, u32[]{:S(2)}, u32[]{:S(2)}) collective-permute-start(bf16[2,160,128]{2,1,0:T(8,128)(2,1)S(1)} %slice.91), channel_id=1, source_target_pairs={{0,6},{1,7},{2,0},{3,1},{4,2},{5,3},{6,4},{7,5},{8,14},{9,15},{10,... | collective-permute-start | bytes 245768 | tf_op jit(solution)/shard_map/ppermute | solution.py:21
  76.8 45.1 %collective-permute-start.9 = (bf16[4,2,320,128]{3,2,1,0:T(8,128)(2,1)S(1)}, bf16[4,2,320,128]{3,2,1,0:T(8,128)(2,1)S(1)}, u32[]{:S(2)}, u32[]{:S(2)}) collective-permute-start(bf16[4,2,320,128]{3,2,1,0:T(8,128)(2,1)S(1)} %pad_maximum_fusion.refs_0_), channel_id=1, source_target_pairs={{0,8},{1,9},{2,10},{3,11},{4,12},{5,13},{6,14},{7,15},{8,16},{9,17... | collective-permute-start | bytes 1966088 | tf_op jit(solution)/shard_map/ppermute | solution.py:21
  77.6 45.1 %collective-permute-start.8 = (bf16[4,2,320,128]{3,2,1,0:T(8,128)(2,1)S(1)}, bf16[4,2,320,128]{3,2,1,0:T(8,128)(2,1)S(1)}, u32[]{:S(2)}, u32[]{:S(2)}) collective-permute-start(bf16[4,2,320,128]{3,2,1,0:T(8,128)(2,1)S(1)} %pad_maximum_fusion.refs_0_), channel_id=1, source_target_pairs={{0,24},{1,25},{2,26},{3,27},{4,28},{5,29},{6,30},{7,31},{8,0},{9,1... | collective-permute-start | bytes 1966088 | tf_op jit(solution)/shard_map/ppermute | solution.py:21
  80.2 25.3 %collective-permute-start.12 = (bf16[2,320,128]{2,1,0:T(8,128)(2,1)S(1)}, bf16[2,320,128]{2,1,0:T(8,128)(2,1)S(1)}, u32[]{:S(2)}, u32[]{:S(2)}) collective-permute-start(bf16[2,320,128]{2,1,0:T(8,128)(2,1)S(1)} %fusion.3), channel_id=1, source_target_pairs={{0,0},{1,1},{2,64},{3,65},{4,128},{5,129},{6,192},{7,193},{8,32},{... | collective-permute-start | bytes 491528 | tf_op jit(solution)/shard_map/ppermute | solution.py:21
  105.6 6.5 %collective-permute-start.16 = (bf16[2,320,128]{2,1,0:T(8,128)(2,1)S(1)}, bf16[2,320,128]{2,1,0:T(8,128)(2,1)S(1)}, u32[]{:S(2)}, u32[]{:S(2)}) collective-permute-start(bf16[2,320,128]{2,1,0:T(8,128)(2,1)S(1)} %collective-permute-done.12.refs_4_), channel_id=1, source_target_pairs={{0,32},{1,33},{2,34},{3,35},{4,36},{5,37},{6,38},{7,39},{8,40},{9,... | collective-permute-start | bytes 491528 | tf_op jit(solution)/shard_map/ppermute | solution.py:21
  105.6 6.5 %collective-permute-start.13 = (bf16[2,320,128]{2,1,0:T(8,128)(2,1)S(1)}, bf16[2,320,128]{2,1,0:T(8,128)(2,1)S(1)}, u32[]{:S(2)}, u32[]{:S(2)}) collective-permute-start(bf16[2,320,128]{2,1,0:T(8,128)(2,1)S(1)} %collective-permute-done.12.refs_4_), channel_id=1, source_target_pairs={{0,224},{1,225},{2,226},{3,227},{4,228},{5,229},{6,230},{7,231},{8... | collective-permute-start | bytes 491528 | tf_op jit(solution)/shard_map/ppermute | solution.py:21
  112.1 6.5 %collective-permute-start.17 = (bf16[2,320,128]{2,1,0:T(8,128)(2,1)S(1)}, bf16[2,320,128]{2,1,0:T(8,128)(2,1)S(1)}, u32[]{:S(2)}, u32[]{:S(2)}) collective-permute-start(bf16[2,320,128]{2,1,0:T(8,128)(2,1)S(1)} %collective-permute-done.16.refs_11_), channel_id=1, source_target_pairs={{0,32},{1,33},{2,34},{3,35},{4,36},{5,37},{6,38},{7,39},{8,40},{9,... | collective-permute-start | bytes 491528 | tf_op jit(solution)/shard_map/ppermute | solution.py:21
  112.1 6.5 %collective-permute-start.14 = (bf16[2,320,128]{2,1,0:T(8,128)(2,1)S(1)}, bf16[2,320,128]{2,1,0:T(8,128)(2,1)S(1)}, u32[]{:S(2)}, u32[]{:S(2)}) collective-permute-start(bf16[2,320,128]{2,1,0:T(8,128)(2,1)S(1)} %collective-permute-done.13.refs_5_), channel_id=1, source_target_pairs={{0,224},{1,225},{2,226},{3,227},{4,228},{5,229},{6,230},{7,231},{8... | collective-permute-start | bytes 491528 | tf_op jit(solution)/shard_map/ppermute | solution.py:21
  118.6 8.0 %collective-permute-start.18 = (bf16[2,320,128]{2,1,0:T(8,128)(2,1)S(1)}, bf16[2,320,128]{2,1,0:T(8,128)(2,1)S(1)}, u32[]{:S(2)}, u32[]{:S(2)}) collective-permute-start(bf16[2,320,128]{2,1,0:T(8,128)(2,1)S(1)} %collective-permute-done.17.refs_10_), channel_id=1, source_target_pairs={{0,32},{1,33},{2,34},{3,35},{4,36},{5,37},{6,38},{7,39},{8,40},{9,... | collective-permute-start | bytes 491528 | tf_op jit(solution)/shard_map/ppermute | solution.py:21
  118.6 8.1 %collective-permute-start.15 = (bf16[2,320,128]{2,1,0:T(8,128)(2,1)S(1)}, bf16[2,320,128]{2,1,0:T(8,128)(2,1)S(1)}, u32[]{:S(2)}, u32[]{:S(2)}) collective-permute-start(bf16[2,320,128]{2,1,0:T(8,128)(2,1)S(1)} %collective-permute-done.14.refs_6_), channel_id=1, source_target_pairs={{0,224},{1,225},{2,226},{3,227},{4,228},{5,229},{6,230},{7,231},{8... | collective-permute-start | bytes 491528 | tf_op jit(solution)/shard_map/ppermute | solution.py:21
  122.6 9.8 %collective-permute-start.10 = (bf16[2,2,320,128]{3,2,1,0:T(8,128)(2,1)}, bf16[2,2,320,128]{3,2,1,0:T(8,128)(2,1)S(1)}, u32[]{:S(2)}, u32[]{:S(2)}) collective-permute-start(bf16[2,2,320,128]{3,2,1,0:T(8,128)(2,1)} %slice.92), channel_id=1, source_target_pairs={{0,8},{1,9},{2,10},{3,11},{4,12},{5,13},{6,14},{7,15},{8,16},{9,17... | collective-permute-start | bytes 983048 | tf_op jit(solution)/shard_map/ppermute | solution.py:21
  123.4 9.0 %collective-permute-start.11 = (bf16[2,2,320,128]{3,2,1,0:T(8,128)(2,1)}, bf16[2,2,320,128]{3,2,1,0:T(8,128)(2,1)}, u32[]{:S(2)}, u32[]{:S(2)}) collective-permute-start(bf16[2,2,320,128]{3,2,1,0:T(8,128)(2,1)} %slice.93), channel_id=1, source_target_pairs={{0,24},{1,25},{2,26},{3,27},{4,28},{5,29},{6,30},{7,31},{8,0},{9,1... | collective-permute-start | bytes 983048 | tf_op jit(solution)/shard_map/ppermute | solution.py:21
  126.7 5.7 %collective-permute-start.19 = (bf16[2,160,128]{2,1,0:T(8,128)(2,1)S(1)}, bf16[2,160,128]{2,1,0:T(8,128)(2,1)S(1)}, u32[]{:S(2)}, u32[]{:S(2)}) collective-permute-start(bf16[2,160,128]{2,1,0:T(8,128)(2,1)S(1)} %slice.94), channel_id=1, source_target_pairs={{0,32},{1,33},{2,34},{3,35},{4,36},{5,37},{6,38},{7,39},{8,40},{9,... | collective-permute-start | bytes 245768 | tf_op jit(solution)/shard_map/ppermute | solution.py:21
  126.8 5.6 %collective-permute-start.20 = (bf16[2,160,128]{2,1,0:T(8,128)(2,1)S(1)}, bf16[2,160,128]{2,1,0:T(8,128)(2,1)S(1)}, u32[]{:S(2)}, u32[]{:S(2)}) collective-permute-start(bf16[2,160,128]{2,1,0:T(8,128)(2,1)S(1)} %slice.95), channel_id=1, source_target_pairs={{0,224},{1,225},{2,226},{3,227},{4,228},{5,229},{6,230},{7,231},{8... | collective-permute-start | bytes 245768 | tf_op jit(solution)/shard_map/ppermute | solution.py:21
  144.0 2.7 %collective-permute-start.21 = (f32[4,256,256]{2,1,0:T(8,128)S(1)}, f32[4,256,256]{2,1,0:T(8,128)S(1)}, u32[]{:S(2)}, u32[]{:S(2)}) collective-permute-start(f32[4,256,256]{2,1,0:T(8,128)S(1)} %get-tuple-element.5), channel_id=1, source_target_pairs={{0,1},{1,0},{2,3},{3,2},{4,5},{5,4},{6,7},{7,6},{8,9},{9,8},{10,11... | collective-permute-start | bytes 3145736 | tf_op jit(solution)/shard_map/ppermute | solution.py:21
  147.0 8.8 %collective-permute-start.24 = (bf16[256,256]{1,0:T(8,128)(2,1)S(1)}, bf16[256,256]{1,0:T(8,128)(2,1)S(1)}, u32[]{:S(2)}, u32[]{:S(2)}) collective-permute-start(bf16[256,256]{1,0:T(8,128)(2,1)S(1)} %get-tuple-element.7), channel_id=1, source_target_pairs={{0,24},{1,25},{2,26},{3,27},{4,28},{5,29},{6,30},{7,31},{8,0},{9,1... | collective-permute-start | bytes 393224 | tf_op jit(solution)/shard_map/ppermute | solution.py:21
  149.8 7.9 %collective-permute-start.23 = (bf16[256,256]{1,0:T(8,128)(2,1)S(1)}, bf16[256,256]{1,0:T(8,128)(2,1)S(1)}, u32[]{:S(2)}, u32[]{:S(2)}) collective-permute-start(bf16[256,256]{1,0:T(8,128)(2,1)S(1)} %get-tuple-element.8), channel_id=1, source_target_pairs={{0,16},{1,17},{2,18},{3,19},{4,20},{5,21},{6,22},{7,23},{8,24},{9,... | collective-permute-start | bytes 393224 | tf_op jit(solution)/shard_map/ppermute | solution.py:21
  149.8 9.3 %collective-permute-start.22 = (bf16[256,256]{1,0:T(8,128)(2,1)S(1)}, bf16[256,256]{1,0:T(8,128)(2,1)S(1)}, u32[]{:S(2)}, u32[]{:S(2)}) collective-permute-start(bf16[256,256]{1,0:T(8,128)(2,1)S(1)} %get-tuple-element.9), channel_id=1, source_target_pairs={{0,8},{1,9},{2,10},{3,11},{4,12},{5,13},{6,14},{7,15},{8,16},{9,17... | collective-permute-start | bytes 393224 | tf_op jit(solution)/shard_map/ppermute | solution.py:21
  159.2 1.3 copy-start
Sparse Core Ops, SparseCore 0:
  10.4 27.8 all-gather.2
  126.8 19.9 all-gather.4

commit v2 on v1

v2 whole, which is shorter than its diff:
```python
import jax
import jax.numpy as jnp
from jax import lax
from jax.experimental import pallas as pl
from jax.experimental.pallas import tpu as pltpu
from jax.sharding import Mesh, PartitionSpec as P

AXES = ("z", "x", "y", "core")
SIZES = (8, 4, 4, 2)


def permute(value, target):
    pairs = []
    for z in range(8):
        for x in range(4):
            for y in range(4):
                for core in range(2):
                    goal = [p % s for p, s in zip(target(z, x, y, core), SIZES)]
                    source = ((z * 4 + x) * 4 + y) * 2 + core
                    pairs.append((source, ((goal[0] * 4 + goal[1]) * 4 + goal[2]) * 2 + goal[3]))
    return lax.ppermute(value, AXES, pairs)


def along_x(value, step):
    return permute(value, lambda z, x, y, core: (z, x + step, y, core))


def ring_of_four(value, shift, dim, after=None):
    below, above = shift(value, 1), shift(value, -1)
    if after is not None:
        below, above, after = lax.optimization_barrier((below, above, after))
    half = value.shape[dim] // 2
    first = lax.slice_in_dim(below, 0, half, axis=dim)
    second = lax.slice_in_dim(above, half, value.shape[dim], axis=dim)
    across = jnp.concatenate([shift(first, 1), shift(second, -1)], axis=dim)
    gathered = [value, above, across, below]
    return gathered if after is None else (gathered, after)


def along_y(value, step):
    return permute(value, lambda z, x, y, core: (z, x, y + step, core))


def along_z(value, step):
    return permute(value, lambda z, x, y, core: (z + step, x, y, core))


def ring_of_eight(value, shift, after):
    below, above = [value], [value]
    for step in range(3):
        near, far = shift(below[-1], 1), shift(above[-1], -1)
        if step == 0:
            near, far, after = lax.optimization_barrier((near, far, after))
        below.append(near)
        above.append(far)
    half = value.shape[1] // 2
    first = shift(below[3][:, :half], 1)
    second = shift(above[3][:, half:], -1)
    across = jnp.concatenate([first, second], axis=1)
    return above + [across] + below[:0:-1], after


def partial_kernel(place, *refs):
    rows, lines, kept, given, columns = refs[:4], refs[4:12], refs[12], refs[13], refs[14]
    first, core, mid = place[0], place[1], place[2]
    for far, line in enumerate(lines):
        at = lax.rem(first + far, 8)
        start = pl.multiple_of(320 * lax.rem(at, 4), 64)
        side = lax.rem(lax.div(at, 4) + core, 2)
        columns[side, pl.ds(start, 320), :] = jnp.concatenate([line[0], line[1]], axis=1)
    mine, others = columns[0].T, columns[1].T
    for step, row in enumerate(rows):
        near = [lax.rem(y + 4 - mid, 4) for y in range(4)]
        block = jnp.concatenate([jnp.concatenate([row[at, 0], row[at, 1]], axis=1) for at in near], axis=0)
        kept[step] = jnp.dot(mine, block, preferred_element_type=jnp.float32)
        given[step] = jnp.dot(others, block, preferred_element_type=jnp.float32)


def partial_cores(rows, lines):
    z, x, y, core = (lax.axis_index(name).astype(jnp.int32) for name in AXES)
    first = z - 2 * ((x - 2 * (y % 2) - 1) % 4) - y // 2 - 2
    place = jnp.stack([first % 8, core, y])
    wide = 2 * rows[0].shape[-1]
    vmem = pl.BlockSpec(memory_space=pltpu.VMEM)
    out = jax.ShapeDtypeStruct((4, wide, wide), jnp.float32)
    return pl.pallas_call(
        partial_kernel,
        out_shape=(out, out),
        in_specs=[pl.BlockSpec(memory_space=pltpu.SMEM)] + [vmem] * 12,
        out_specs=(vmem, vmem),
        scratch_shapes=[pltpu.VMEM((2, 1280, wide), rows[0].dtype)],
        compiler_params=pltpu.CompilerParams(vmem_limit_bytes=32 * 2**20),
        cost_estimate=pl.CostEstimate(flops=1400000000, bytes_accessed=6000000, transcendentals=0),
    )(place, *rows, *lines)


def apply_kernel(place, cores, left, *refs):
    out = refs[-1]
    for tile in range(2):
        product = jnp.dot(
            cores[:, tile * 128:(tile + 1) * 128], left[tile], preferred_element_type=jnp.float32
        ).astype(out.dtype)
        for column in range(2):
            out[tile, 0, column] = product[128 * column:128 * column + 128]


def apply_cores(step, cores, left, so_far=None):
    tiles, slots, order = left.shape
    _, x, y, core = (lax.axis_index(name).astype(jnp.int32) for name in AXES)
    place = ((x - 2 * (y % 2) - core - step) % 4).reshape(1)
    span = 1280
    earlier = [] if so_far is None else [so_far]
    grid_spec = pltpu.PrefetchScalarGridSpec(
        num_scalar_prefetch=1,
        grid=(order // span,),
        in_specs=[
            pl.BlockSpec(cores.shape, lambda n, place: (0, 0)),
            pl.BlockSpec((tiles, slots, span), lambda n, place: (0, 0, n)),
        ] + [pl.BlockSpec(memory_space=pl.ANY)] * len(earlier),
        out_specs=pl.BlockSpec((tiles, 1, 2, slots, span), lambda n, place: (0, 0, place[0], 0, n)),
    )
    return pl.pallas_call(
        apply_kernel,
        out_shape=jax.ShapeDtypeStruct((tiles, 1, 8, slots, order), jnp.bfloat16),
        grid_spec=grid_spec,
        input_output_aliases={3: 0} if earlier else {},
        compiler_params=pltpu.CompilerParams(vmem_limit_bytes=32 * 2**20),
        cost_estimate=pl.CostEstimate(flops=350000000, bytes_accessed=4000000, transcendentals=0),
    )(place, cores, left, *earlier)


VMEM = pl.BlockSpec(memory_space=pltpu.VMEM)
SMEM = pl.BlockSpec(memory_space=pltpu.SMEM)


def local_call(kernel, shapes, *operands, flops=0, bytes_accessed=4000000):
    outs = [jax.ShapeDtypeStruct(shape, dtype) for shape, dtype in shapes]
    return pl.pallas_call(
        kernel,
        out_shape=outs,
        in_specs=[SMEM] + [VMEM] * (len(operands) - 1),
        out_specs=[VMEM] * len(outs),
        compiler_params=pltpu.CompilerParams(vmem_limit_bytes=32 * 2**20),
        cost_estimate=pl.CostEstimate(flops=flops, bytes_accessed=bytes_accessed, transcendentals=0),
    )(*operands)


def pack_kernel(place, inverse, out):
    exact = inverse[...]
    rounded = exact.astype(jnp.bfloat16).astype(jnp.float32)
    rows = lax.broadcasted_iota(jnp.int32, exact.shape, 0) + place[0]
    cols = lax.broadcasted_iota(jnp.int32, exact.shape, 1) + place[1]
    rest = jnp.sum(jnp.where(rows == cols, exact - rounded, 0.0), axis=0, keepdims=True)
    tail = jnp.concatenate([rounded[48:, 256:], jnp.zeros((16, 64), jnp.float32)], axis=0)
    ends = jnp.concatenate([rounded[:48, 256:], tail], axis=1)
    last = jnp.concatenate([rest[:, 256:], jnp.zeros((1, 64), jnp.float32)], axis=1)
    rest = jnp.concatenate([rest[:, :128], rest[:, 128:256], last, jnp.zeros((13, 128), jnp.float32)], axis=0)
    packed = jnp.concatenate([rounded[:, :128], rounded[:, 128:256], ends, rest], axis=0).astype(jnp.bfloat16)
    for copy in range(8):
        out[copy] = packed


def arrange_kernel(place, own, other, full, mine):
    x, mid = place[0], place[1]
    for step in range(4):
        start = pl.multiple_of(80 * lax.rem(x + step, 4), 16)
        low, high = [], []
        for side in (own, other):
            for y in range(4):
                near = lax.rem(y + 4 - mid, 4)
                part = jnp.concatenate([side[near, 2 + tile, pl.ds(start, 80), :] for tile in range(2)], axis=1)
                low.append(part[:48])
                high.append(part[48:])
        full[step] = jnp.concatenate(low + high, axis=0).T
    here = jnp.concatenate([own[0, 2], own[0, 3]], axis=1)
    mine[...] = jnp.concatenate([here, jnp.zeros((64, 256), here.dtype)], axis=0).T


def left_kernel(place, own, other, left, rows):
    mid, core = place[1], place[2]
    for tile in range(2):
        for side, at in ((own, core), (other, 1 - core)):
            for near in range(4):
                y = lax.rem(mid + near, 4)
                rows[pl.ds(pl.multiple_of(640 * y + 320 * at, 64), 320), :] = side[near, tile]
        left[tile] = rows[...].T


def solve_kernel(place, full, mine, *refs):
    blocks, out = refs[:4], refs[4]
    core = place[2]
    order = [2 * y + core for y in range(4)] + [2 * y + 1 - core for y in range(4)]
    wide = jnp.zeros((256, 256), jnp.float32)
    first = jnp.zeros((256, 128), jnp.float32)
    second = jnp.zeros((256, 128), jnp.float32)
    rest = jnp.zeros((16, 128), jnp.float32)
    for step, block in enumerate(blocks):
        parts = [
            jnp.concatenate(
                [block[at, low:low + 48, :] for at in order] + [block[at, low + 48:low + 80, :] for at in order], axis=0
            )
            for low in (0, 80)
        ]
        ends = jnp.concatenate([block[at, 160:208, :] for at in order], axis=0)
        tails = jnp.concatenate([block[at, 160:192, :] for at in order], axis=0)
        rows = full[step]
        wide += jnp.dot(rows, jnp.concatenate(parts, axis=1), preferred_element_type=jnp.float32)
        first += jnp.dot(rows[:, :384], ends, preferred_element_type=jnp.float32)
        second += jnp.dot(rows[:, 384:], tails, preferred_element_type=jnp.float32)
        for at in range(8):
            rest += block[at, 208:224, :].astype(jnp.float32)
    own = mine[...].astype(jnp.float32)
    wide += own[:, :256] * jnp.concatenate([rest[0:1], rest[1:2]], axis=1)
    first += own[:, 256:] * rest[2:3]
    ends = first.T[:64] + second.T[64:]
    total = jnp.concatenate([wide.T, ends], axis=0)
    slot = lax.broadcasted_iota(jnp.int32, (320, 128), 1)
    for tile in range(2):
        part = total[:, tile * 128:(tile + 1) * 128]
        out[tile] = jnp.where(slot < place[3 + tile], part, 0.0).astype(out.dtype)


def local(u_panel, v_panel, ranks, inverse_t):
    tiles, slots, width = v_panel.shape
    depth = inverse_t.shape[0]
    z, x, y, core = (lax.axis_index(name).astype(jnp.int32) for name in AXES)
    place = jnp.stack([x, y, core, ranks[0], ranks[1], z])
    corner = jnp.stack([depth * (z * 4 + x), width * (y * 2 + core)])
    half = jnp.bfloat16

    (sent,) = local_call(pack_kernel, [((8, 224, 128), half)], corner, inverse_t)
    both = jnp.concatenate([jnp.swapaxes(u_panel, 1, 2), jnp.swapaxes(v_panel, 1, 2)], axis=0)
    both, sent = lax.optimization_barrier((both, sent))
    planes = lax.all_to_all(sent, "z", split_axis=0, concat_axis=0, tiled=True)
    own, planes = ring_of_four(both, along_y, 1, after=planes)
    own = jnp.stack(own)
    blocks, own = ring_of_four(planes, along_x, 0, after=own)
    other = permute(own, lambda z, x, y, core: (z, x, y, core + 1))
    full, mine = local_call(arrange_kernel, [((4, 256, 640), half), ((256, 384), half)], place, own, other)
    left = pl.pallas_call(
        left_kernel,
        out_shape=jax.ShapeDtypeStruct((tiles, slots, 8 * width), half),
        in_specs=[SMEM, VMEM, VMEM],
        out_specs=VMEM,
        scratch_shapes=[pltpu.VMEM((8 * width, slots), half)],
        compiler_params=pltpu.CompilerParams(vmem_limit_bytes=32 * 2**20),
        cost_estimate=pl.CostEstimate(flops=0, bytes_accessed=4000000, transcendentals=0),
    )(place, own, other)
    (solved,) = local_call(
        solve_kernel, [((tiles, width, slots), half)], place, full, mine, *blocks, flops=500000000
    )

    moved = permute(
        solved,
        lambda z, x, y, core: (
            z + y - 2 * (x % 2),
            x + z // 2,
            2 * (z % 2) + x // 2,
            core,
        ),
    )
    rows, moved = ring_of_four(solved, along_y, 1, after=moved)
    rows = jnp.stack(rows)
    lines, rows = ring_of_eight(moved, along_z, rows)
    rows = ring_of_four(rows, along_x, 0)
    kept, given = partial_cores(rows, lines)
    given = permute(given, lambda z, x, y, core: (z, x, y, core + 1))
    cores = (kept + given).astype(half)
    pieces = [cores[0]] + [along_x(cores[step], step) for step in range(1, 4)]
    update = apply_cores(0, pieces[0], left)
    for step in (1, 3, 2):
        update = apply_cores(step, pieces[step], left, update)
    return jnp.swapaxes(solved, 1, 2), update


def solution(mesh):
    fine = Mesh(mesh.devices.reshape(SIZES), AXES)
    row, col = ("z", "x"), ("y", "core")
    placed = (P(row, None, col), P(row, None, col), P(row), P(row, col))
    return jax.shard_map(
        local,
        mesh=fine,
        in_specs=placed,
        out_specs=(P(row, None, col), P(row, col, None, None, None)),
        check_vma=False,
    )
```

time: 175 us -> 134 us (0.77)
  the two profiles are of different devices: /device:TPU:8 before, /device:TPU:1 now
where the time goes in v2:
time: 134 us
  starting transfers between devices  62.7 us (47%)
  waiting for transfers between devices  41.5 us (31%)
  Pallas kernels  17.2 us (13%)
  local copies, waits for them, and re-layouts  6.74 us (5%)
  other arithmetic  4.81 us (4%)
    ppermute x30, starting transfers between devices, permute(): return lax.ppermute(value, AXES, pairs)  53.7 us
    ppermute x30, waiting for transfers between devices, permute(): return lax.ppermute(value, AXES, pairs)  34.6 us
    all_to_all x1, starting transfers between devices, local(): planes = lax.all_to_all(sent, 'z', split_axis=0, concat_axis=0, tiled=True)  9.03 us
    pallas_call x4, Pallas kernels, apply_cores(): pl.pallas_call(apply_kernel, out_shape=jax.ShapeDtypeStruct((tiles, 1, 8,...  8.69 us
    all_to_all x1, waiting for transfers between devices, local(): planes = lax.all_to_all(sent, 'z', split_axis=0, concat_axis=0, tiled=True)  6.86 us
    pallas_call x3, Pallas kernels, local_call(): pl.pallas_call(kernel, out_shape=outs, in_specs=[SMEM] + [VMEM] * (len(op...  4.65 us
    pallas_call x1, Pallas kernels, partial_cores(): pl.pallas_call(partial_kernel, out_shape=(out, out), in_specs=[pl.BlockSp...  2.86 us
  transfers between devices with their start and end apart: 31, of which 14 were waited for; matrix products, arithmetic and copies ran while one was open for 5% of the time, Pallas kernels for 6%

profile of v2, /device:TPU:1, one launch (start us, length us, event | category | flops | bytes accessed | tf_op | source)
XLA Modules:
  0.0 133.9 jit_solution(1845908218592969379)
XLA Ops:
  0.7 0.9 copy-done.6
  1.6 1.4 %shard_map.59 = bf16[8,224,128]{2,1,0:T(8,128)(2,1)} custom-call(s32[2]{0:T(128)S(1)} %pad_add_fusion.place, f32[80,320]{1,0:T(8,128)S(1)} %copy-done.6), custom_call_target="tpu_custom_call" | custom-call | bytes 4000000 | tf_op jit(solution)/shard_map/pallas_call | solution.py:138
  3.0 1.0 pad_maximum_fusion.4
  4.1 9.0 %all-to-all-start = ((bf16[8,224,128]{2,1,0:T(8,128)(2,1)}), bf16[8,224,128]{2,1,0:T(8,128)(2,1)S(1)}, u32[]{:S(2)}, u32[]{:S(2)}) async-start(bf16[8,224,128]{2,1,0:T(8,128)(2,1)} %shard_map.59), calls=%async_computation | async-start | bytes 917504 | tf_op jit(solution)/shard_map/all_to_all | solution.py:234
  13.1 1.3 collective-permute-start
  14.4 1.5 %collective-permute-start.1 = (bf16[4,320,128]{2,1,0:T(8,128)(2,1)S(1)}, bf16[4,320,128]{2,1,0:T(8,128)(2,1)S(1)}, u32[]{:S(2)}, u32[]{:S(2)}) collective-permute-start(bf16[4,320,128]{2,1,0:T(8,128)(2,1)S(1)} %pad_maximum_fusion.4), channel_id=1, source_target_pairs={{0,6},{1,7},{2,0},{3,1},{4,2},{5,3},{6,4},{7,5},{8,14},{9,15},{10,... | collective-permute-start | bytes 983048 | tf_op jit(solution)/shard_map/ppermute | solution.py:21
  15.9 6.8 %collective-permute-done = bf16[4,320,128]{2,1,0:T(8,128)(2,1)S(1)} collective-permute-done((bf16[4,320,128]{2,1,0:T(8,128)(2,1)S(1)}, bf16[4,320,128]{2,1,0:T(8,128)(2,1)S(1)}, u32[]{:S(2)}, u32[]{:S(2)}) %collective-permute-start) | collective-permute-done | bytes 327712 | tf_op jit(solution)/shard_map/ppermute | solution.py:21
  22.7 6.9 %all-to-all-done.refs_0_ = bf16[8,224,128]{2,1,0:T(8,128)(2,1)S(1)} async-done(((bf16[8,224,128]{2,1,0:T(8,128)(2,1)}), bf16[8,224,128]{2,1,0:T(8,128)(2,1)S(1)}, u32[]{:S(2)}, u32[]{:S(2)}) %all-to-all-start) | async-done | bytes 458784 | tf_op jit(solution)/shard_map/all_to_all | solution.py:234
  29.5 1.2 collective-permute-start.2
  30.8 1.5 %collective-permute-start.3 = (bf16[8,224,128]{2,1,0:T(8,128)(2,1)S(1)}, bf16[8,224,128]{2,1,0:T(8,128)(2,1)S(1)}, u32[]{:S(2)}, u32[]{:S(2)}) collective-permute-start(bf16[8,224,128]{2,1,0:T(8,128)(2,1)S(1)} %all-to-all-done.refs_0_), channel_id=1, source_target_pairs={{0,24},{1,25},{2,26},{3,27},{4,28},{5,29},{6,30},{7,31},{8,0},{9,1... | collective-permute-start | bytes 1376264 | tf_op jit(solution)/shard_map/ppermute | solution.py:21
  32.2 1.4 %collective-permute-start.4 = (bf16[4,160,128]{2,1,0:T(8,128)(2,1)S(1)}, bf16[4,160,128]{2,1,0:T(8,128)(2,1)S(1)}, u32[]{:S(2)}, u32[]{:S(2)}) collective-permute-start(bf16[4,160,128]{2,1,0:T(8,128)(2,1)S(1)} %slice.45), channel_id=1, source_target_pairs={{0,2},{1,3},{2,4},{3,5},{4,6},{5,7},{6,0},{7,1},{8,10},{9,11},{10,... | collective-permute-start | bytes 491528 | tf_op jit(solution)/shard_map/ppermute | solution.py:21
  33.6 1.5 %collective-permute-start.5 = (bf16[4,160,128]{2,1,0:T(8,128)(2,1)S(1)}, bf16[4,160,128]{2,1,0:T(8,128)(2,1)S(1)}, u32[]{:S(2)}, u32[]{:S(2)}) collective-permute-start(bf16[4,160,128]{2,1,0:T(8,128)(2,1)S(1)} %slice.46), channel_id=1, source_target_pairs={{0,6},{1,7},{2,0},{3,1},{4,2},{5,3},{6,4},{7,5},{8,14},{9,15},{10,... | collective-permute-start | bytes 491528 | tf_op jit(solution)/shard_map/ppermute | solution.py:21
  35.2 3.0 %collective-permute-done.4 = bf16[4,160,128]{2,1,0:T(8,128)(2,1)S(1)} collective-permute-done((bf16[4,160,128]{2,1,0:T(8,128)(2,1)S(1)}, bf16[4,160,128]{2,1,0:T(8,128)(2,1)S(1)}, u32[]{:S(2)}, u32[]{:S(2)}) %collective-permute-start.4) | collective-permute-done | bytes 163872 | tf_op jit(solution)/shard_map/ppermute | solution.py:21
  38.2 0.2 pad_maximum_fusion.own
  38.4 3.8 %collective-permute-done.2.refs_3_ = bf16[8,224,128]{2,1,0:T(8,128)(2,1)S(1)} collective-permute-done((bf16[8,224,128]{2,1,0:T(8,128)(2,1)S(1)}, bf16[8,224,128]{2,1,0:T(8,128)(2,1)S(1)}, u32[]{:S(2)}, u32[]{:S(2)}) %collective-permute-start.2) | collective-permute-done | bytes 458784 | tf_op jit(solution)/shard_map/ppermute | solution.py:21
  42.2 1.4 %collective-permute-start.6 = (bf16[4,4,320,128]{3,2,1,0:T(8,128)(2,1)S(1)}, bf16[4,4,320,128]{3,2,1,0:T(8,128)(2,1)S(1)}, u32[]{:S(2)}, u32[]{:S(2)}) collective-permute-start(bf16[4,4,320,128]{3,2,1,0:T(8,128)(2,1)S(1)} %pad_maximum_fusion.own), channel_id=1, source_target_pairs={{0,1},{1,0},{2,3},{3,2},{4,5},{5,4},{6,7},{7,6},{8,9},{9,8},{10,11... | collective-permute-start | bytes 3932168 | tf_op jit(solution)/shard_map/ppermute | solution.py:21
  43.7 0.7 slice.47
  44.4 1.2 collective-permute-start.7
  45.6 0.7 slice.48
  46.3 1.5 %collective-permute-start.8 = (bf16[4,224,128]{2,1,0:T(8,128)(2,1)}, bf16[4,224,128]{2,1,0:T(8,128)(2,1)}, u32[]{:S(2)}, u32[]{:S(2)}) collective-permute-start(bf16[4,224,128]{2,1,0:T(8,128)(2,1)} %slice.48), channel_id=1, source_target_pairs={{0,24},{1,25},{2,26},{3,27},{4,28},{5,29},{6,30},{7,31},{8,0},{9,1... | collective-permute-start | bytes 688136 | tf_op jit(solution)/shard_map/ppermute | solution.py:21
  47.9 5.2 %collective-permute-done.7 = bf16[4,224,128]{2,1,0:T(8,128)(2,1)} collective-permute-done((bf16[4,224,128]{2,1,0:T(8,128)(2,1)}, bf16[4,224,128]{2,1,0:T(8,128)(2,1)}, u32[]{:S(2)}, u32[]{:S(2)}) %collective-permute-start.7) | collective-permute-done | bytes 229408 | tf_op jit(solution)/shard_map/ppermute | solution.py:21
  53.1 0.4 collective-permute-done.8
  53.5 1.1 pad_maximum_fusion.3.refs_2_
  54.6 1.0 shard_map.60
  55.6 2.3 %shard_map.61 = bf16[2,320,128]{2,1,0:T(8,128)(2,1)} custom-call(s32[6]{0:T(128)S(1)} %stack.66.place, bf16[4,256,640]{2,1,0:T(8,128)(2,1)S(1)} %get-tuple-element.26.full, bf16[256,384]{1,0:T(8,128)(2,1)S(1)} %get-tuple-element.27.mine, bf16[8,224,128]{2,1,0:T(8,128)(2,1)S(1)} %all-to-all-done.refs_0_, bf16[8,224,128]{2,1,0:T(8,128)(2,1)S(1)} %copy-done.1, ...), custom_call_target="tpu_custom_call" | custom-call | flops 500000000 | bytes 4000000 | tf_op jit(solution)/shard_map/pallas_call | solution.py:138
  57.9 2.7 %collective-permute-start.10 = (bf16[2,320,128]{2,1,0:T(8,128)(2,1)}, bf16[2,320,128]{2,1,0:T(8,128)(2,1)S(1)}, u32[]{:S(2)}, u32[]{:S(2)}) collective-permute-start(bf16[2,320,128]{2,1,0:T(8,128)(2,1)} %shard_map.61), channel_id=1, source_target_pairs={{0,6},{1,7},{2,0},{3,1},{4,2},{5,3},{6,4},{7,5},{8,14},{9,15},{10,... | collective-permute-start | bytes 491528 | tf_op jit(solution)/shard_map/ppermute | solution.py:21
  60.6 1.6 %collective-permute-start.11 = (bf16[2,320,128]{2,1,0:T(8,128)(2,1)}, bf16[2,320,128]{2,1,0:T(8,128)(2,1)S(1)}, u32[]{:S(2)}, u32[]{:S(2)}) collective-permute-start(bf16[2,320,128]{2,1,0:T(8,128)(2,1)} %shard_map.61), channel_id=1, source_target_pairs={{0,0},{1,1},{2,32},{3,33},{4,64},{5,65},{6,96},{7,97},{8,200},{9,2... | collective-permute-start | bytes 491528 | tf_op jit(solution)/shard_map/ppermute | solution.py:21
  62.2 1.0 collective-permute-done.10
  63.2 4.6 %collective-permute-done.9 = bf16[2,320,128]{2,1,0:T(8,128)(2,1)S(1)} collective-permute-done((bf16[2,320,128]{2,1,0:T(8,128)(2,1)}, bf16[2,320,128]{2,1,0:T(8,128)(2,1)S(1)}, u32[]{:S(2)}, u32[]{:S(2)}) %collective-permute-start.9) | collective-permute-done | bytes 163872 | tf_op jit(solution)/shard_map/ppermute | solution.py:21
  67.8 4.0 %collective-permute-start.14 = (bf16[2,160,128]{2,1,0:T(8,128)(2,1)S(1)}, bf16[2,160,128]{2,1,0:T(8,128)(2,1)S(1)}, u32[]{:S(2)}, u32[]{:S(2)}) collective-permute-start(bf16[2,160,128]{2,1,0:T(8,128)(2,1)S(1)} %slice.49), channel_id=1, source_target_pairs={{0,2},{1,3},{2,4},{3,5},{4,6},{5,7},{6,0},{7,1},{8,10},{9,11},{10,... | collective-permute-start | bytes 245768 | tf_op jit(solution)/shard_map/ppermute | solution.py:21
  71.8 1.3 %collective-permute-start.15 = (bf16[2,160,128]{2,1,0:T(8,128)(2,1)S(1)}, bf16[2,160,128]{2,1,0:T(8,128)(2,1)S(1)}, u32[]{:S(2)}, u32[]{:S(2)}) collective-permute-start(bf16[2,160,128]{2,1,0:T(8,128)(2,1)S(1)} %slice.50), channel_id=1, source_target_pairs={{0,6},{1,7},{2,0},{3,1},{4,2},{5,3},{6,4},{7,5},{8,14},{9,15},{10,... | collective-permute-start | bytes 245768 | tf_op jit(solution)/shard_map/ppermute | solution.py:21
  73.1 2.7 %collective-permute-start.13 = (bf16[2,320,128]{2,1,0:T(8,128)(2,1)S(1)}, bf16[2,320,128]{2,1,0:T(8,128)(2,1)S(1)}, u32[]{:S(2)}, u32[]{:S(2)}) collective-permute-start(bf16[2,320,128]{2,1,0:T(8,128)(2,1)S(1)} %collective-permute-done.11.refs_4_), channel_id=1, source_target_pairs={{0,224},{1,225},{2,226},{3,227},{4,228},{5,229},{6,230},{7,231},{8... | collective-permute-start | bytes 491528 | tf_op jit(solution)/shard_map/ppermute | solution.py:21
  75.8 1.0 pad_maximum_fusion.1.refs_0_
  76.8 1.7 %collective-permute-done.12.refs_11_ = bf16[2,320,128]{2,1,0:T(8,128)(2,1)S(1)} collective-permute-done((bf16[2,320,128]{2,1,0:T(8,128)(2,1)S(1)}, bf16[2,320,128]{2,1,0:T(8,128)(2,1)S(1)}, u32[]{:S(2)}, u32[]{:S(2)}) %collective-permute-start.12) | collective-permute-done | bytes 163872 | tf_op jit(solution)/shard_map/ppermute | solution.py:21
  78.5 4.0 %collective-permute-start.17 = (bf16[4,2,320,128]{3,2,1,0:T(8,128)(2,1)S(1)}, bf16[4,2,320,128]{3,2,1,0:T(8,128)(2,1)S(1)}, u32[]{:S(2)}, u32[]{:S(2)}) collective-permute-start(bf16[4,2,320,128]{3,2,1,0:T(8,128)(2,1)S(1)} %pad_maximum_fusion.1.refs_0_), channel_id=1, source_target_pairs={{0,8},{1,9},{2,10},{3,11},{4,12},{5,13},{6,14},{7,15},{8,16},{9,17... | collective-permute-start | bytes 1966088 | tf_op jit(solution)/shard_map/ppermute | solution.py:21
  82.5 4.8 %collective-permute-start.16 = (bf16[4,2,320,128]{3,2,1,0:T(8,128)(2,1)S(1)}, bf16[4,2,320,128]{3,2,1,0:T(8,128)(2,1)S(1)}, u32[]{:S(2)}, u32[]{:S(2)}) collective-permute-start(bf16[4,2,320,128]{3,2,1,0:T(8,128)(2,1)S(1)} %pad_maximum_fusion.1.refs_0_), channel_id=1, source_target_pairs={{0,24},{1,25},{2,26},{3,27},{4,28},{5,29},{6,30},{7,31},{8,0},{9,1... | collective-permute-start | bytes 1966088 | tf_op jit(solution)/shard_map/ppermute | solution.py:21
  87.2 0.7 copy-done.9
  87.9 2.7 %collective-permute-start.20 = (bf16[2,320,128]{2,1,0:T(8,128)(2,1)S(1)}, bf16[2,320,128]{2,1,0:T(8,128)(2,1)}, u32[]{:S(2)}, u32[]{:S(2)}) collective-permute-start(bf16[2,320,128]{2,1,0:T(8,128)(2,1)S(1)} %collective-permute-done.13.refs_5_), channel_id=1, source_target_pairs={{0,224},{1,225},{2,226},{3,227},{4,228},{5,229},{6,230},{7,231},{8... | collective-permute-start | bytes 491528 | tf_op jit(solution)/shard_map/ppermute | solution.py:21
  90.6 0.7 copy-done.11
  91.2 1.7 %collective-permute-done.22.refs_10_ = bf16[2,320,128]{2,1,0:T(8,128)(2,1)} collective-permute-done((bf16[2,320,128]{2,1,0:T(8,128)(2,1)S(1)}, bf16[2,320,128]{2,1,0:T(8,128)(2,1)}, u32[]{:S(2)}, u32[]{:S(2)}) %collective-permute-start.22) | collective-permute-done | bytes 163872 | tf_op jit(solution)/shard_map/ppermute | solution.py:21
  92.9 3.3 %collective-permute-start.21 = (bf16[2,320,128]{2,1,0:T(8,128)(2,1)}, bf16[2,320,128]{2,1,0:T(8,128)(2,1)}, u32[]{:S(2)}, u32[]{:S(2)}) collective-permute-start(bf16[2,320,128]{2,1,0:T(8,128)(2,1)} %collective-permute-done.20.refs_6_), channel_id=1, source_target_pairs={{0,224},{1,225},{2,226},{3,227},{4,228},{5,229},{6,230},{7,231},{8... | collective-permute-start | bytes 491528 | tf_op jit(solution)/shard_map/ppermute | solution.py:21
  96.2 2.7 %collective-permute-done.17.refs_3_ = bf16[4,2,320,128]{3,2,1,0:T(8,128)(2,1)S(1)} collective-permute-done((bf16[4,2,320,128]{3,2,1,0:T(8,128)(2,1)S(1)}, bf16[4,2,320,128]{3,2,1,0:T(8,128)(2,1)S(1)}, u32[]{:S(2)}, u32[]{:S(2)}) %collective-permute-start.17) | collective-permute-done | bytes 655392 | tf_op jit(solution)/shard_map/ppermute | solution.py:21
  99.0 0.8 slice.59
  99.8 0.1 copy-done.2
  99.9 0.8 slice.60
  100.7 0.1 copy-done.4
  100.9 2.5 %collective-permute-start.19 = (bf16[2,2,320,128]{3,2,1,0:T(8,128)(2,1)}, bf16[2,2,320,128]{3,2,1,0:T(8,128)(2,1)}, u32[]{:S(2)}, u32[]{:S(2)}) collective-permute-start(bf16[2,2,320,128]{3,2,1,0:T(8,128)(2,1)} %slice.60), channel_id=1, source_target_pairs={{0,24},{1,25},{2,26},{3,27},{4,28},{5,29},{6,30},{7,31},{8,0},{9,1... | collective-permute-start | bytes 983048 | tf_op jit(solution)/shard_map/ppermute | solution.py:21
  103.5 0.1 collective-permute-start.24
  103.6 1.0 slice.62
  104.6 2.5 %collective-permute-start.25 = (bf16[2,160,128]{2,1,0:T(8,128)(2,1)S(1)}, bf16[2,160,128]{2,1,0:T(8,128)(2,1)S(1)}, u32[]{:S(2)}, u32[]{:S(2)}) collective-permute-start(bf16[2,160,128]{2,1,0:T(8,128)(2,1)S(1)} %slice.62), channel_id=1, source_target_pairs={{0,224},{1,225},{2,226},{3,227},{4,228},{5,229},{6,230},{7,231},{8... | collective-permute-start | bytes 245768 | tf_op jit(solution)/shard_map/ppermute | solution.py:21
  107.2 1.3 collective-permute-done.24
  108.4 0.2 collective-permute-done.25
  108.6 1.1 pad_maximum_fusion.2.refs_2_
  109.8 2.9 %shard_map.62 = (f32[4,256,256]{2,1,0:T(8,128)S(1)}, f32[4,256,256]{2,1,0:T(8,128)S(1)}) custom-call(s32[3]{0:T(128)S(1)} %pad_add_fusion.1.place, bf16[4,2,320,128]{3,2,1,0:T(8,128)(2,1)S(1)} %pad_maximum_fusion.1.refs_0_, bf16[4,2,320,128]{3,2,1,0:T(8,128)(2,1)S(1)} %copy-done.5, bf16[4,2,320,128]{3,2,1,0:T(8,128)(2,1)S(1)} %pad_maximum_fusion.2.refs_2_, ...), custom_call_target="tpu_custom_call" | custom-call | flops 1400000000 | bytes 6000000 | tf_op jit(solution)/shard_map/pallas_call | solution.py:86
  112.7 5.7 %collective-permute-start.26 = (f32[4,256,256]{2,1,0:T(8,128)S(1)}, f32[4,256,256]{2,1,0:T(8,128)S(1)}, u32[]{:S(2)}, u32[]{:S(2)}) collective-permute-start(f32[4,256,256]{2,1,0:T(8,128)S(1)} %get-tuple-element.37), channel_id=1, source_target_pairs={{0,1},{1,0},{2,3},{3,2},{4,5},{5,4},{6,7},{7,6},{8,9},{9,8},{10,11... | collective-permute-start | bytes 3145736 | tf_op jit(solution)/shard_map/ppermute | solution.py:21
  118.4 2.3 %collective-permute-done.26 = f32[4,256,256]{2,1,0:T(8,128)S(1)} collective-permute-done((f32[4,256,256]{2,1,0:T(8,128)S(1)}, f32[4,256,256]{2,1,0:T(8,128)S(1)}, u32[]{:S(2)}, u32[]{:S(2)}) %collective-permute-start.26) | collective-permute-done | bytes 1048608 | tf_op jit(solution)/shard_map/ppermute | solution.py:21
  120.7 0.2 add_convert_fusion
  121.0 2.7 %collective-permute-start.28 = (bf16[256,256]{1,0:T(8,128)(2,1)S(1)}, bf16[256,256]{1,0:T(8,128)(2,1)S(1)}, u32[]{:S(2)}, u32[]{:S(2)}) collective-permute-start(bf16[256,256]{1,0:T(8,128)(2,1)S(1)} %get-tuple-element.40), channel_id=1, source_target_pairs={{0,24},{1,25},{2,26},{3,27},{4,28},{5,29},{6,30},{7,31},{8,0},{9,1... | collective-permute-start | bytes 393224 | tf_op jit(solution)/shard_map/ppermute | solution.py:21
  123.7 0.5 collective-permute-start.27
  124.2 1.0 shard_map.63.left
  125.2 2.2 %shard_map.64.refs_0_ = bf16[2,1,8,128,2560]{4,3,2,1,0:T(8,128)(2,1)} custom-call(s32[1]{0:T(128)} %bitcast.24.place, bf16[256,256]{1,0:T(8,128)(2,1)S(1)} %get-tuple-element.38.cores, bf16[2,128,2560]{2,1,0:T(8,128)(2,1)S(1)} %shard_map.63.left), custom_call_target="tpu_custom_call" | custom-call | flops 350000000 | bytes 4000000 | tf_op jit(solution)/shard_map/pallas_call | solution.py:122
  127.3 2.2 %shard_map.65.refs_0_ = bf16[2,1,8,128,2560]{4,3,2,1,0:T(8,128)(2,1)} custom-call(s32[1]{0:T(128)} %bitcast.22.place, bf16[256,256]{1,0:T(8,128)(2,1)S(1)} %collective-permute-done.29.cores, bf16[2,128,2560]{2,1,0:T(8,128)(2,1)S(1)} %shard_map.63.left, bf16[2,1,8,128,2560]{4,3,2,1,0:T(8,128)(2,1)} %shard_map.64.refs_0_), custom_call_target="tpu_custom_call", output_to_operand_aliasing={{}: (3, {})} | custom-call | flops 350000000 | bytes 4000000 | tf_op jit(solution)/shard_map/pallas_call | solution.py:122
  129.5 2.2 %shard_map.66.refs_0_ = bf16[2,1,8,128,2560]{4,3,2,1,0:T(8,128)(2,1)} custom-call(s32[1]{0:T(128)} %bitcast.20.place, bf16[256,256]{1,0:T(8,128)(2,1)S(1)} %collective-permute-done.28.cores, bf16[2,128,2560]{2,1,0:T(8,128)(2,1)S(1)} %shard_map.63.left, bf16[2,1,8,128,2560]{4,3,2,1,0:T(8,128)(2,1)} %shard_map.65.refs_0_), custom_call_target="tpu_custom_call", output_to_operand_aliasing={{}: (3, {})} | custom-call | flops 350000000 | bytes 4000000 | tf_op jit(solution)/shard_map/pallas_call | solution.py:122
  131.7 2.2 %shard_map.67 = bf16[2,1,8,128,2560]{4,3,2,1,0:T(8,128)(2,1)} custom-call(s32[1]{0:T(128)} %bitcast.13.place, bf16[256,256]{1,0:T(8,128)(2,1)S(1)} %collective-permute-done.27.cores, bf16[2,128,2560]{2,1,0:T(8,128)(2,1)S(1)} %shard_map.63.left, bf16[2,1,8,128,2560]{4,3,2,1,0:T(8,128)(2,1)} %shard_map.66.refs_0_), custom_call_target="tpu_custom_call", output_to_operand_aliasing={{}: (3, {})} | custom-call | flops 350000000 | bytes 4000000 | tf_op jit(solution)/shard_map/pallas_call | solution.py:122
  (58 shorter events, 0.5 us)
Async XLA Ops:
  0.7 0.9 copy-start.6
  4.1 25.5 %all-to-all-start = ((bf16[8,224,128]{2,1,0:T(8,128)(2,1)}), bf16[8,224,128]{2,1,0:T(8,128)(2,1)S(1)}, u32[]{:S(2)}, u32[]{:S(2)}) async-start(bf16[8,224,128]{2,1,0:T(8,128)(2,1)} %shard_map.59), calls=%async_computation | async-start | bytes 917504 | tf_op jit(solution)/shard_map/all_to_all | solution.py:234
  13.1 9.6 %collective-permute-start = (bf16[4,320,128]{2,1,0:T(8,128)(2,1)S(1)}, bf16[4,320,128]{2,1,0:T(8,128)(2,1)S(1)}, u32[]{:S(2)}, u32[]{:S(2)}) collective-permute-start(bf16[4,320,128]{2,1,0:T(8,128)(2,1)S(1)} %pad_maximum_fusion.4), channel_id=1, source_target_pairs={{0,2},{1,3},{2,4},{3,5},{4,6},{5,7},{6,0},{7,1},{8,10},{9,11},{10,... | collective-permute-start | bytes 983048 | tf_op jit(solution)/shard_map/ppermute | solution.py:21
  14.4 8.3 %collective-permute-start.1 = (bf16[4,320,128]{2,1,0:T(8,128)(2,1)S(1)}, bf16[4,320,128]{2,1,0:T(8,128)(2,1)S(1)}, u32[]{:S(2)}, u32[]{:S(2)}) collective-permute-start(bf16[4,320,128]{2,1,0:T(8,128)(2,1)S(1)} %pad_maximum_fusion.4), channel_id=1, source_target_pairs={{0,6},{1,7},{2,0},{3,1},{4,2},{5,3},{6,4},{7,5},{8,14},{9,15},{10,... | collective-permute-start | bytes 983048 | tf_op jit(solution)/shard_map/ppermute | solution.py:21
  29.5 12.7 %collective-permute-start.2 = (bf16[8,224,128]{2,1,0:T(8,128)(2,1)S(1)}, bf16[8,224,128]{2,1,0:T(8,128)(2,1)S(1)}, u32[]{:S(2)}, u32[]{:S(2)}) collective-permute-start(bf16[8,224,128]{2,1,0:T(8,128)(2,1)S(1)} %all-to-all-done.refs_0_), channel_id=1, source_target_pairs={{0,8},{1,9},{2,10},{3,11},{4,12},{5,13},{6,14},{7,15},{8,16},{9,17... | collective-permute-start | bytes 1376264 | tf_op jit(solution)/shard_map/ppermute | solution.py:21
  30.8 11.5 %collective-permute-start.3 = (bf16[8,224,128]{2,1,0:T(8,128)(2,1)S(1)}, bf16[8,224,128]{2,1,0:T(8,128)(2,1)S(1)}, u32[]{:S(2)}, u32[]{:S(2)}) collective-permute-start(bf16[8,224,128]{2,1,0:T(8,128)(2,1)S(1)} %all-to-all-done.refs_0_), channel_id=1, source_target_pairs={{0,24},{1,25},{2,26},{3,27},{4,28},{5,29},{6,30},{7,31},{8,0},{9,1... | collective-permute-start | bytes 1376264 | tf_op jit(solution)/shard_map/ppermute | solution.py:21
  32.2 6.0 %collective-permute-start.4 = (bf16[4,160,128]{2,1,0:T(8,128)(2,1)S(1)}, bf16[4,160,128]{2,1,0:T(8,128)(2,1)S(1)}, u32[]{:S(2)}, u32[]{:S(2)}) collective-permute-start(bf16[4,160,128]{2,1,0:T(8,128)(2,1)S(1)} %slice.45), channel_id=1, source_target_pairs={{0,2},{1,3},{2,4},{3,5},{4,6},{5,7},{6,0},{7,1},{8,10},{9,11},{10,... | collective-permute-start | bytes 491528 | tf_op jit(solution)/shard_map/ppermute | solution.py:21
  33.6 4.6 %collective-permute-start.5 = (bf16[4,160,128]{2,1,0:T(8,128)(2,1)S(1)}, bf16[4,160,128]{2,1,0:T(8,128)(2,1)S(1)}, u32[]{:S(2)}, u32[]{:S(2)}) collective-permute-start(bf16[4,160,128]{2,1,0:T(8,128)(2,1)S(1)} %slice.46), channel_id=1, source_target_pairs={{0,6},{1,7},{2,0},{3,1},{4,2},{5,3},{6,4},{7,5},{8,14},{9,15},{10,... | collective-permute-start | bytes 491528 | tf_op jit(solution)/shard_map/ppermute | solution.py:21
  38.2 9.6 %copy-start.13 = (s32[2]{0:T(128)S(1)}, s32[2]{0:T(128)}, u32[]{:S(2)}) copy-start(s32[2]{0:T(128)} %param.6) | copy-start | bytes 28
  42.2 3.4 %copy-start = (bf16[8,224,128]{2,1,0:T(8,128)(2,1)}, bf16[8,224,128]{2,1,0:T(8,128)(2,1)S(1)}, u32[]{:S(2)}) copy-start(bf16[8,224,128]{2,1,0:T(8,128)(2,1)S(1)} %collective-permute-done.3.refs_1_) | copy-start | bytes 1376260
  42.2 12.4 %collective-permute-start.6 = (bf16[4,4,320,128]{3,2,1,0:T(8,128)(2,1)S(1)}, bf16[4,4,320,128]{3,2,1,0:T(8,128)(2,1)S(1)}, u32[]{:S(2)}, u32[]{:S(2)}) collective-permute-start(bf16[4,4,320,128]{3,2,1,0:T(8,128)(2,1)S(1)} %pad_maximum_fusion.own), channel_id=1, source_target_pairs={{0,1},{1,0},{2,3},{3,2},{4,5},{5,4},{6,7},{7,6},{8,9},{9,8},{10,11... | collective-permute-start | bytes 3932168 | tf_op jit(solution)/shard_map/ppermute | solution.py:21
  44.4 8.7 %collective-permute-start.7 = (bf16[4,224,128]{2,1,0:T(8,128)(2,1)}, bf16[4,224,128]{2,1,0:T(8,128)(2,1)}, u32[]{:S(2)}, u32[]{:S(2)}) collective-permute-start(bf16[4,224,128]{2,1,0:T(8,128)(2,1)} %slice.47), channel_id=1, source_target_pairs={{0,8},{1,9},{2,10},{3,11},{4,12},{5,13},{6,14},{7,15},{8,16},{9,17... | collective-permute-start | bytes 688136 | tf_op jit(solution)/shard_map/ppermute | solution.py:21
  46.3 7.2 %collective-permute-start.8 = (bf16[4,224,128]{2,1,0:T(8,128)(2,1)}, bf16[4,224,128]{2,1,0:T(8,128)(2,1)}, u32[]{:S(2)}, u32[]{:S(2)}) collective-permute-start(bf16[4,224,128]{2,1,0:T(8,128)(2,1)} %slice.48), channel_id=1, source_target_pairs={{0,24},{1,25},{2,26},{3,27},{4,28},{5,29},{6,30},{7,31},{8,0},{9,1... | collective-permute-start | bytes 688136 | tf_op jit(solution)/shard_map/ppermute | solution.py:21
  54.6 1.0 copy-start.1
  57.9 5.3 %collective-permute-start.10 = (bf16[2,320,128]{2,1,0:T(8,128)(2,1)}, bf16[2,320,128]{2,1,0:T(8,128)(2,1)S(1)}, u32[]{:S(2)}, u32[]{:S(2)}) collective-permute-start(bf16[2,320,128]{2,1,0:T(8,128)(2,1)} %shard_map.61), channel_id=1, source_target_pairs={{0,6},{1,7},{2,0},{3,1},{4,2},{5,3},{6,4},{7,5},{8,14},{9,15},{10,... | collective-permute-start | bytes 491528 | tf_op jit(solution)/shard_map/ppermute | solution.py:21
  60.6 2.6 %collective-permute-start.11 = (bf16[2,320,128]{2,1,0:T(8,128)(2,1)}, bf16[2,320,128]{2,1,0:T(8,128)(2,1)S(1)}, u32[]{:S(2)}, u32[]{:S(2)}) collective-permute-start(bf16[2,320,128]{2,1,0:T(8,128)(2,1)} %shard_map.61), channel_id=1, source_target_pairs={{0,0},{1,1},{2,32},{3,33},{4,64},{5,65},{6,96},{7,97},{8,200},{9,2... | collective-permute-start | bytes 491528 | tf_op jit(solution)/shard_map/ppermute | solution.py:21
  62.2 5.6 %collective-permute-start.9 = (bf16[2,320,128]{2,1,0:T(8,128)(2,1)}, bf16[2,320,128]{2,1,0:T(8,128)(2,1)S(1)}, u32[]{:S(2)}, u32[]{:S(2)}) collective-permute-start(bf16[2,320,128]{2,1,0:T(8,128)(2,1)} %shard_map.61), channel_id=1, source_target_pairs={{0,2},{1,3},{2,4},{3,5},{4,6},{5,7},{6,0},{7,1},{8,10},{9,11},{10,... | collective-permute-start | bytes 491528 | tf_op jit(solution)/shard_map/ppermute | solution.py:21
  63.2 27.4 %copy-start.7 = (bf16[2,320,128]{2,1,0:T(8,128)(2,1)}, bf16[2,320,128]{2,1,0:T(8,128)(2,1)S(1)}, u32[]{:S(2)}) copy-start(bf16[2,320,128]{2,1,0:T(8,128)(2,1)S(1)} %collective-permute-done.11.refs_4_) | copy-start | bytes 491524
  67.8 8.0 %collective-permute-start.14 = (bf16[2,160,128]{2,1,0:T(8,128)(2,1)S(1)}, bf16[2,160,128]{2,1,0:T(8,128)(2,1)S(1)}, u32[]{:S(2)}, u32[]{:S(2)}) collective-permute-start(bf16[2,160,128]{2,1,0:T(8,128)(2,1)S(1)} %slice.49), channel_id=1, source_target_pairs={{0,2},{1,3},{2,4},{3,5},{4,6},{5,7},{6,0},{7,1},{8,10},{9,11},{10,... | collective-permute-start | bytes 245768 | tf_op jit(solution)/shard_map/ppermute | solution.py:21
  71.8 4.0 %collective-permute-start.15 = (bf16[2,160,128]{2,1,0:T(8,128)(2,1)S(1)}, bf16[2,160,128]{2,1,0:T(8,128)(2,1)S(1)}, u32[]{:S(2)}, u32[]{:S(2)}) collective-permute-start(bf16[2,160,128]{2,1,0:T(8,128)(2,1)S(1)} %slice.50), channel_id=1, source_target_pairs={{0,6},{1,7},{2,0},{3,1},{4,2},{5,3},{6,4},{7,5},{8,14},{9,15},{10,... | collective-permute-start | bytes 245768 | tf_op jit(solution)/shard_map/ppermute | solution.py:21
  73.1 5.4 %collective-permute-start.12 = (bf16[2,320,128]{2,1,0:T(8,128)(2,1)S(1)}, bf16[2,320,128]{2,1,0:T(8,128)(2,1)S(1)}, u32[]{:S(2)}, u32[]{:S(2)}) collective-permute-start(bf16[2,320,128]{2,1,0:T(8,128)(2,1)S(1)} %collective-permute-done.11.refs_4_), channel_id=1, source_target_pairs={{0,32},{1,33},{2,34},{3,35},{4,36},{5,37},{6,38},{7,39},{8,40},{9,... | collective-permute-start | bytes 491528 | tf_op jit(solution)/shard_map/ppermute | solution.py:21
  73.1 5.4 %collective-permute-start.13 = (bf16[2,320,128]{2,1,0:T(8,128)(2,1)S(1)}, bf16[2,320,128]{2,1,0:T(8,128)(2,1)S(1)}, u32[]{:S(2)}, u32[]{:S(2)}) collective-permute-start(bf16[2,320,128]{2,1,0:T(8,128)(2,1)S(1)} %collective-permute-done.11.refs_4_), channel_id=1, source_target_pairs={{0,224},{1,225},{2,226},{3,227},{4,228},{5,229},{6,230},{7,231},{8... | collective-permute-start | bytes 491528 | tf_op jit(solution)/shard_map/ppermute | solution.py:21
  78.5 20.5 %collective-permute-start.17 = (bf16[4,2,320,128]{3,2,1,0:T(8,128)(2,1)S(1)}, bf16[4,2,320,128]{3,2,1,0:T(8,128)(2,1)S(1)}, u32[]{:S(2)}, u32[]{:S(2)}) collective-permute-start(bf16[4,2,320,128]{3,2,1,0:T(8,128)(2,1)S(1)} %pad_maximum_fusion.1.refs_0_), channel_id=1, source_target_pairs={{0,8},{1,9},{2,10},{3,11},{4,12},{5,13},{6,14},{7,15},{8,16},{9,17... | collective-permute-start | bytes 1966088 | tf_op jit(solution)/shard_map/ppermute | solution.py:21
  82.5 17.3 %collective-permute-start.16 = (bf16[4,2,320,128]{3,2,1,0:T(8,128)(2,1)S(1)}, bf16[4,2,320,128]{3,2,1,0:T(8,128)(2,1)S(1)}, u32[]{:S(2)}, u32[]{:S(2)}) collective-permute-start(bf16[4,2,320,128]{3,2,1,0:T(8,128)(2,1)S(1)} %pad_maximum_fusion.1.refs_0_), channel_id=1, source_target_pairs={{0,24},{1,25},{2,26},{3,27},{4,28},{5,29},{6,30},{7,31},{8,0},{9,1... | collective-permute-start | bytes 1966088 | tf_op jit(solution)/shard_map/ppermute | solution.py:21
  87.2 5.7 %collective-permute-start.22 = (bf16[2,320,128]{2,1,0:T(8,128)(2,1)S(1)}, bf16[2,320,128]{2,1,0:T(8,128)(2,1)}, u32[]{:S(2)}, u32[]{:S(2)}) collective-permute-start(bf16[2,320,128]{2,1,0:T(8,128)(2,1)S(1)} %collective-permute-done.12.refs_11_), channel_id=1, source_target_pairs={{0,32},{1,33},{2,34},{3,35},{4,36},{5,37},{6,38},{7,39},{8,40},{9,... | collective-permute-start | bytes 491528 | tf_op jit(solution)/shard_map/ppermute | solution.py:21
  87.2 0.7 copy-start.9
  87.9 5.0 %collective-permute-start.20 = (bf16[2,320,128]{2,1,0:T(8,128)(2,1)S(1)}, bf16[2,320,128]{2,1,0:T(8,128)(2,1)}, u32[]{:S(2)}, u32[]{:S(2)}) collective-permute-start(bf16[2,320,128]{2,1,0:T(8,128)(2,1)S(1)} %collective-permute-done.13.refs_5_), channel_id=1, source_target_pairs={{0,224},{1,225},{2,226},{3,227},{4,228},{5,229},{6,230},{7,231},{8... | collective-permute-start | bytes 491528 | tf_op jit(solution)/shard_map/ppermute | solution.py:21
  90.6 0.7 copy-start.11
  92.9 10.5 %collective-permute-start.23 = (bf16[2,320,128]{2,1,0:T(8,128)(2,1)}, bf16[2,320,128]{2,1,0:T(8,128)(2,1)S(1)}, u32[]{:S(2)}, u32[]{:S(2)}) collective-permute-start(bf16[2,320,128]{2,1,0:T(8,128)(2,1)} %collective-permute-done.22.refs_10_), channel_id=1, source_target_pairs={{0,32},{1,33},{2,34},{3,35},{4,36},{5,37},{6,38},{7,39},{8,40},{9,... | collective-permute-start | bytes 491528 | tf_op jit(solution)/shard_map/ppermute | solution.py:21
  92.9 10.6 %collective-permute-start.21 = (bf16[2,320,128]{2,1,0:T(8,128)(2,1)}, bf16[2,320,128]{2,1,0:T(8,128)(2,1)}, u32[]{:S(2)}, u32[]{:S(2)}) collective-permute-start(bf16[2,320,128]{2,1,0:T(8,128)(2,1)} %collective-permute-done.20.refs_6_), channel_id=1, source_target_pairs={{0,224},{1,225},{2,226},{3,227},{4,228},{5,229},{6,230},{7,231},{8... | collective-permute-start | bytes 491528 | tf_op jit(solution)/shard_map/ppermute | solution.py:21
  99.0 1.0 copy-start.2
  99.8 8.8 %collective-permute-start.18 = (bf16[2,2,320,128]{3,2,1,0:T(8,128)(2,1)}, bf16[2,2,320,128]{3,2,1,0:T(8,128)(2,1)}, u32[]{:S(2)}, u32[]{:S(2)}) collective-permute-start(bf16[2,2,320,128]{3,2,1,0:T(8,128)(2,1)} %slice.59), channel_id=1, source_target_pairs={{0,8},{1,9},{2,10},{3,11},{4,12},{5,13},{6,14},{7,15},{8,16},{9,17... | collective-permute-start | bytes 983048 | tf_op jit(solution)/shard_map/ppermute | solution.py:21
  99.9 0.9 copy-start.4
  100.9 7.8 %collective-permute-start.19 = (bf16[2,2,320,128]{3,2,1,0:T(8,128)(2,1)}, bf16[2,2,320,128]{3,2,1,0:T(8,128)(2,1)}, u32[]{:S(2)}, u32[]{:S(2)}) collective-permute-start(bf16[2,2,320,128]{3,2,1,0:T(8,128)(2,1)} %slice.60), channel_id=1, source_target_pairs={{0,24},{1,25},{2,26},{3,27},{4,28},{5,29},{6,30},{7,31},{8,0},{9,1... | collective-permute-start | bytes 983048 | tf_op jit(solution)/shard_map/ppermute | solution.py:21
  103.4 6.4 %copy-start.3 = (bf16[4,2,320,128]{3,2,1,0:T(8,128)(2,1)S(1)}, bf16[4,2,320,128]{3,2,1,0:T(8,128)(2,1)}, u32[]{:S(2)}) copy-start(bf16[4,2,320,128]{3,2,1,0:T(8,128)(2,1)} %copy-done.2) | copy-start | bytes 1966084
  103.4 6.4 %copy-start.5 = (bf16[4,2,320,128]{3,2,1,0:T(8,128)(2,1)S(1)}, bf16[4,2,320,128]{3,2,1,0:T(8,128)(2,1)}, u32[]{:S(2)}) copy-start(bf16[4,2,320,128]{3,2,1,0:T(8,128)(2,1)} %copy-done.4) | copy-start | bytes 1966084
  103.4 6.4 %copy-start.8 = (bf16[2,320,128]{2,1,0:T(8,128)(2,1)S(1)}, bf16[2,320,128]{2,1,0:T(8,128)(2,1)}, u32[]{:S(2)}) copy-start(bf16[2,320,128]{2,1,0:T(8,128)(2,1)} %copy-done.7) | copy-start | bytes 491524
  103.4 6.4 %copy-start.10 = (bf16[2,320,128]{2,1,0:T(8,128)(2,1)S(1)}, bf16[2,320,128]{2,1,0:T(8,128)(2,1)}, u32[]{:S(2)}) copy-start(bf16[2,320,128]{2,1,0:T(8,128)(2,1)} %copy-done.9) | copy-start | bytes 491524
  103.4 6.4 %copy-start.12 = (bf16[2,320,128]{2,1,0:T(8,128)(2,1)S(1)}, bf16[2,320,128]{2,1,0:T(8,128)(2,1)}, u32[]{:S(2)}) copy-start(bf16[2,320,128]{2,1,0:T(8,128)(2,1)} %copy-done.11) | copy-start | bytes 491524
  103.5 5.0 %collective-permute-start.24 = (bf16[2,160,128]{2,1,0:T(8,128)(2,1)S(1)}, bf16[2,160,128]{2,1,0:T(8,128)(2,1)S(1)}, u32[]{:S(2)}, u32[]{:S(2)}) collective-permute-start(bf16[2,160,128]{2,1,0:T(8,128)(2,1)S(1)} %slice.61), channel_id=1, source_target_pairs={{0,32},{1,33},{2,34},{3,35},{4,36},{5,37},{6,38},{7,39},{8,40},{9,... | collective-permute-start | bytes 245768 | tf_op jit(solution)/shard_map/ppermute | solution.py:21
  104.6 4.0 %collective-permute-start.25 = (bf16[2,160,128]{2,1,0:T(8,128)(2,1)S(1)}, bf16[2,160,128]{2,1,0:T(8,128)(2,1)S(1)}, u32[]{:S(2)}, u32[]{:S(2)}) collective-permute-start(bf16[2,160,128]{2,1,0:T(8,128)(2,1)S(1)} %slice.62), channel_id=1, source_target_pairs={{0,224},{1,225},{2,226},{3,227},{4,228},{5,229},{6,230},{7,231},{8... | collective-permute-start | bytes 245768 | tf_op jit(solution)/shard_map/ppermute | solution.py:21
  112.7 8.0 %collective-permute-start.26 = (f32[4,256,256]{2,1,0:T(8,128)S(1)}, f32[4,256,256]{2,1,0:T(8,128)S(1)}, u32[]{:S(2)}, u32[]{:S(2)}) collective-permute-start(f32[4,256,256]{2,1,0:T(8,128)S(1)} %get-tuple-element.37), channel_id=1, source_target_pairs={{0,1},{1,0},{2,3},{3,2},{4,5},{5,4},{6,7},{7,6},{8,9},{9,8},{10,11... | collective-permute-start | bytes 3145736 | tf_op jit(solution)/shard_map/ppermute | solution.py:21
  120.9 6.4 %collective-permute-start.29 = (bf16[256,256]{1,0:T(8,128)(2,1)S(1)}, bf16[256,256]{1,0:T(8,128)(2,1)S(1)}, u32[]{:S(2)}, u32[]{:S(2)}) collective-permute-start(bf16[256,256]{1,0:T(8,128)(2,1)S(1)} %get-tuple-element.39), channel_id=1, source_target_pairs={{0,8},{1,9},{2,10},{3,11},{4,12},{5,13},{6,14},{7,15},{8,16},{9,17... | collective-permute-start | bytes 393224 | tf_op jit(solution)/shard_map/ppermute | solution.py:21
  121.0 8.5 %collective-permute-start.28 = (bf16[256,256]{1,0:T(8,128)(2,1)S(1)}, bf16[256,256]{1,0:T(8,128)(2,1)S(1)}, u32[]{:S(2)}, u32[]{:S(2)}) collective-permute-start(bf16[256,256]{1,0:T(8,128)(2,1)S(1)} %get-tuple-element.40), channel_id=1, source_target_pairs={{0,24},{1,25},{2,26},{3,27},{4,28},{5,29},{6,30},{7,31},{8,0},{9,1... | collective-permute-start | bytes 393224 | tf_op jit(solution)/shard_map/ppermute | solution.py:21
  123.7 8.0 %collective-permute-start.27 = (bf16[256,256]{1,0:T(8,128)(2,1)S(1)}, bf16[256,256]{1,0:T(8,128)(2,1)S(1)}, u32[]{:S(2)}, u32[]{:S(2)}) collective-permute-start(bf16[256,256]{1,0:T(8,128)(2,1)S(1)} %get-tuple-element.41), channel_id=1, source_target_pairs={{0,16},{1,17},{2,18},{3,19},{4,20},{5,21},{6,22},{7,23},{8,24},{9,... | collective-permute-start | bytes 393224 | tf_op jit(solution)/shard_map/ppermute | solution.py:21

commit v3 on v2

--- a/solution.py
+++ b/solution.py
@@ -1,3 +1,5 @@
+import functools
+
 import jax
 import jax.numpy as jnp
 from jax import lax
@@ -32,13 +34,25 @@
     half = value.shape[dim] // 2
     first = lax.slice_in_dim(below, 0, half, axis=dim)
     second = lax.slice_in_dim(above, half, value.shape[dim], axis=dim)
-    across = jnp.concatenate([shift(first, 1), shift(second, -1)], axis=dim)
-    gathered = [value, above, across, below]
+    gathered = [value, above, (shift(first, 1), shift(second, -1)), below]
     return gathered if after is None else (gathered, after)
+
+
+def flat(blocks):
+    return jax.tree.leaves(blocks)
+
+
+def stacked(blocks, dim):
+    return jnp.stack([jnp.concatenate(b, axis=dim) if isinstance(b, tuple) else b for b in blocks])
 
 
 def along_y(value, step):
     return permute(value, lambda z, x, y, core: (z, x, y + step, core))
+
+
+def gather_y(value):
+    far, above, below = along_y(value, 2), along_y(value, -1), along_y(value, 1)
+    return jnp.stack([value, above, far, below])
 
 
 def along_z(value, step):
@@ -49,8 +63,6 @@
     below, above = [value], [value]
     for step in range(3):
         near, far = shift(below[-1], 1), shift(above[-1], -1)
-        if step == 0:
-            near, far, after = lax.optimization_barrier((near, far, after))
         below.append(near)
         above.append(far)
     half = value.shape[1] // 2
@@ -61,7 +73,7 @@
 
 
 def partial_kernel(place, *refs):
-    rows, lines, kept, given, columns = refs[:4], refs[4:12], refs[12], refs[13], refs[14]
+    rows, lines, (kept, given, columns) = refs[:4], refs[4:12], refs[12:]
     first, core, mid = place[0], place[1], place[2]
     for far, line in enumerate(lines):
         at = lax.rem(first + far, 8)
@@ -73,19 +85,19 @@
         near = [lax.rem(y + 4 - mid, 4) for y in range(4)]
         block = jnp.concatenate([jnp.concatenate([row[at, 0], row[at, 1]], axis=1) for at in near], axis=0)
         kept[step] = jnp.dot(mine, block, preferred_element_type=jnp.float32)
-        given[step] = jnp.dot(others, block, preferred_element_type=jnp.float32)
+        given[step] = jnp.dot(others, block, preferred_element_type=jnp.float32).astype(given.dtype)
 
 
 def partial_cores(rows, lines):
+    rows = [jnp.concatenate(row, axis=0) if isinstance(row, tuple) else row for row in rows]
     z, x, y, core = (lax.axis_index(name).astype(jnp.int32) for name in AXES)
-    first = z - 2 * ((x - 2 * (y % 2) - 1) % 4) - y // 2 - 2
+    first = z - 2 * ((x - 2 * (y % 2) - 2) % 4) - y // 2 - 2
     place = jnp.stack([first % 8, core, y])
     wide = 2 * rows[0].shape[-1]
     vmem = pl.BlockSpec(memory_space=pltpu.VMEM)
-    out = jax.ShapeDtypeStruct((4, wide, wide), jnp.float32)
     return pl.pallas_call(
         partial_kernel,
-        out_shape=(out, out),
+        out_shape=[jax.ShapeDtypeStruct((4, wide, wide), dtype) for dtype in (jnp.float32, jnp.float32)],
         in_specs=[pl.BlockSpec(memory_space=pltpu.SMEM)] + [vmem] * 12,
         out_specs=(vmem, vmem),
         scratch_shapes=[pltpu.VMEM((2, 1280, wide), rows[0].dtype)],
@@ -94,39 +106,47 @@
     )(place, *rows, *lines)
 
 
-def apply_kernel(place, cores, left, *refs):
-    out = refs[-1]
-    for tile in range(2):
-        product = jnp.dot(
-            cores[:, tile * 128:(tile + 1) * 128], left[tile], preferred_element_type=jnp.float32
-        ).astype(out.dtype)
-        for column in range(2):
-            out[tile, 0, column] = product[128 * column:128 * column + 128]
-
-
-def apply_cores(step, cores, left, so_far=None):
+def apply_kernel(count, place, left, *refs):
+    pieces = refs[:count]
+    out, product, sems = refs[-3:]
+    copies = []
+    for number, cores in enumerate(pieces):
+        for part in range(5):
+            span = pl.ds(512 * part, 512)
+            for tile in range(2):
+                block = jnp.dot(
+                    cores[:, tile * 128:(tile + 1) * 128], left[tile, :, span], preferred_element_type=jnp.float32
+                ).astype(out.dtype)
+                for column in range(2):
+                    product[number, tile, column, :, span] = block[128 * column:128 * column + 128]
+                copies.append(
+                    pltpu.make_async_copy(
+                        product.at[number, tile, :, :, span],
+                        out.at[tile, 0, pl.ds(2 * place[number], 2), :, span],
+                        sems.at[number, part, tile],
+                    )
+                )
+                copies[-1].start()
+    for copy in copies:
+        copy.wait()
+
+
+def apply_cores(steps, pieces, left, so_far=None):
     tiles, slots, order = left.shape
     _, x, y, core = (lax.axis_index(name).astype(jnp.int32) for name in AXES)
-    place = ((x - 2 * (y % 2) - core - step) % 4).reshape(1)
-    span = 1280
+    place = jnp.stack([(x - 2 * (y % 2) - 2 * core - step) % 4 for step in steps])
+    count = len(steps)
     earlier = [] if so_far is None else [so_far]
-    grid_spec = pltpu.PrefetchScalarGridSpec(
-        num_scalar_prefetch=1,
-        grid=(order // span,),
-        in_specs=[
-            pl.BlockSpec(cores.shape, lambda n, place: (0, 0)),
-            pl.BlockSpec((tiles, slots, span), lambda n, place: (0, 0, n)),
-        ] + [pl.BlockSpec(memory_space=pl.ANY)] * len(earlier),
-        out_specs=pl.BlockSpec((tiles, 1, 2, slots, span), lambda n, place: (0, 0, place[0], 0, n)),
-    )
     return pl.pallas_call(
-        apply_kernel,
+        functools.partial(apply_kernel, count),
         out_shape=jax.ShapeDtypeStruct((tiles, 1, 8, slots, order), jnp.bfloat16),
-        grid_spec=grid_spec,
-        input_output_aliases={3: 0} if earlier else {},
+        in_specs=[SMEM] + [VMEM] * (1 + count) + [pl.BlockSpec(memory_space=pl.ANY)] * len(earlier),
+        out_specs=pl.BlockSpec(memory_space=pl.ANY),
+        input_output_aliases={2 + count: 0} if earlier else {},
+        scratch_shapes=[pltpu.VMEM((count, tiles, 2, slots, order), jnp.bfloat16), pltpu.SemaphoreType.DMA((count, 5, 2))],
         compiler_params=pltpu.CompilerParams(vmem_limit_bytes=32 * 2**20),
-        cost_estimate=pl.CostEstimate(flops=350000000, bytes_accessed=4000000, transcendentals=0),
-    )(place, cores, left, *earlier)
+        cost_estimate=pl.CostEstimate(flops=350000000 * count, bytes_accessed=4000000 * count, transcendentals=0),
+    )(place, left, *pieces, *earlier)
 
 
 VMEM = pl.BlockSpec(memory_space=pltpu.VMEM)
@@ -151,11 +171,10 @@
     rows = lax.broadcasted_iota(jnp.int32, exact.shape, 0) + place[0]
     cols = lax.broadcasted_iota(jnp.int32, exact.shape, 1) + place[1]
     rest = jnp.sum(jnp.where(rows == cols, exact - rounded, 0.0), axis=0, keepdims=True)
-    tail = jnp.concatenate([rounded[48:, 256:], jnp.zeros((16, 64), jnp.float32)], axis=0)
+    rests = [rest[:, at:at + 64] for at in range(0, 320, 64)]
+    tail = jnp.concatenate([rounded[48:, 256:]] + rests + [jnp.zeros((11, 64), jnp.float32)], axis=0)
     ends = jnp.concatenate([rounded[:48, 256:], tail], axis=1)
-    last = jnp.concatenate([rest[:, 256:], jnp.zeros((1, 64), jnp.float32)], axis=1)
-    rest = jnp.concatenate([rest[:, :128], rest[:, 128:256], last, jnp.zeros((13, 128), jnp.float32)], axis=0)
-    packed = jnp.concatenate([rounded[:, :128], rounded[:, 128:256], ends, rest], axis=0).astype(jnp.bfloat16)
+    packed = jnp.concatenate([rounded[:, :128], rounded[:, 128:256], ends], axis=0).astype(jnp.bfloat16)
     for copy in range(8):
         out[copy] = packed
 
@@ -186,33 +205,38 @@
         left[tile] = rows[...].T
 
 
-def solve_kernel(place, full, mine, *refs):
-    blocks, out = refs[:4], refs[4]
+def solve_kernel(place, full, mine, here, above, first, second, below, out):
     core = place[2]
     order = [2 * y + core for y in range(4)] + [2 * y + 1 - core for y in range(4)]
     wide = jnp.zeros((256, 256), jnp.float32)
-    first = jnp.zeros((256, 128), jnp.float32)
-    second = jnp.zeros((256, 128), jnp.float32)
+    lows = jnp.zeros((256, 128), jnp.float32)
+    highs = jnp.zeros((256, 128), jnp.float32)
     rest = jnp.zeros((16, 128), jnp.float32)
-    for step, block in enumerate(blocks):
+    for step in range(4):
+        if step == 2:
+            blocks = [(first if at % 4 < 2 else second, order[at] - at % 4 // 2 * 4) for at in range(8)]
+        else:
+            blocks = [((here, above, None, below)[step], at) for at in order]
         parts = [
             jnp.concatenate(
-                [block[at, low:low + 48, :] for at in order] + [block[at, low + 48:low + 80, :] for at in order], axis=0
+                [ref[at, low:low + 48, :] for ref, at in blocks] + [ref[at, low + 48:low + 80, :] for ref, at in blocks],
+                axis=0,
             )
             for low in (0, 80)
         ]
-        ends = jnp.concatenate([block[at, 160:208, :] for at in order], axis=0)
-        tails = jnp.concatenate([block[at, 160:192, :] for at in order], axis=0)
+        ends = jnp.concatenate([ref[at, 160:208, :] for ref, at in blocks], axis=0)
+        tails = jnp.concatenate([ref[at, 160:192, :] for ref, at in blocks], axis=0)
         rows = full[step]
         wide += jnp.dot(rows, jnp.concatenate(parts, axis=1), preferred_element_type=jnp.float32)
-        first += jnp.dot(rows[:, :384], ends, preferred_element_type=jnp.float32)
-        second += jnp.dot(rows[:, 384:], tails, preferred_element_type=jnp.float32)
-        for at in range(8):
-            rest += block[at, 208:224, :].astype(jnp.float32)
+        lows += jnp.dot(rows[:, :384], ends, preferred_element_type=jnp.float32)
+        highs += jnp.dot(rows[:, 384:], tails, preferred_element_type=jnp.float32)
+        for ref, at in blocks:
+            rest += ref[at, 192:208, :].astype(jnp.float32)
     own = mine[...].astype(jnp.float32)
-    wide += own[:, :256] * jnp.concatenate([rest[0:1], rest[1:2]], axis=1)
-    first += own[:, 256:] * rest[2:3]
-    ends = first.T[:64] + second.T[64:]
+    rest = rest[:, 64:]
+    wide += own[:, :256] * jnp.concatenate([rest[at:at + 1] for at in range(4)], axis=1)
+    lows += own[:, 256:] * jnp.concatenate([rest[4:5], jnp.zeros((1, 64), jnp.float32)], axis=1)
+    ends = lows.T[:64] + highs.T[64:]
     total = jnp.concatenate([wide.T, ends], axis=0)
     slot = lax.broadcasted_iota(jnp.int32, (320, 128), 1)
     for tile in range(2):
@@ -228,12 +252,11 @@
     corner = jnp.stack([depth * (z * 4 + x), width * (y * 2 + core)])
     half = jnp.bfloat16
 
-    (sent,) = local_call(pack_kernel, [((8, 224, 128), half)], corner, inverse_t)
+    (sent,) = local_call(pack_kernel, [((8, 208, 128), half)], corner, inverse_t)
     both = jnp.concatenate([jnp.swapaxes(u_panel, 1, 2), jnp.swapaxes(v_panel, 1, 2)], axis=0)
     both, sent = lax.optimization_barrier((both, sent))
     planes = lax.all_to_all(sent, "z", split_axis=0, concat_axis=0, tiled=True)
-    own, planes = ring_of_four(both, along_y, 1, after=planes)
-    own = jnp.stack(own)
+    own = gather_y(both)
     blocks, own = ring_of_four(planes, along_x, 0, after=own)
     other = permute(own, lambda z, x, y, core: (z, x, y, core + 1))
     full, mine = local_call(arrange_kernel, [((4, 256, 640), half), ((256, 384), half)], place, own, other)
@@ -247,29 +270,28 @@
         cost_estimate=pl.CostEstimate(flops=0, bytes_accessed=4000000, transcendentals=0),
     )(place, own, other)
     (solved,) = local_call(
-        solve_kernel, [((tiles, width, slots), half)], place, full, mine, *blocks, flops=500000000
+        solve_kernel, [((tiles, width, slots), half)], place, full, mine, *flat(blocks), flops=500000000
     )
 
     moved = permute(
         solved,
         lambda z, x, y, core: (
-            z + y - 2 * (x % 2),
-            x + z // 2,
+            z + y - 2,
+            x + z // 2 + x % 2,
             2 * (z % 2) + x // 2,
             core,
         ),
     )
-    rows, moved = ring_of_four(solved, along_y, 1, after=moved)
-    rows = jnp.stack(rows)
+    rows, moved = lax.optimization_barrier((gather_y(solved), moved))
     lines, rows = ring_of_eight(moved, along_z, rows)
     rows = ring_of_four(rows, along_x, 0)
     kept, given = partial_cores(rows, lines)
     given = permute(given, lambda z, x, y, core: (z, x, y, core + 1))
-    cores = (kept + given).astype(half)
-    pieces = [cores[0]] + [along_x(cores[step], step) for step in range(1, 4)]
-    update = apply_cores(0, pieces[0], left)
+    cores = (kept + given.astype(jnp.float32)).astype(half)
+    pieces = [cores[0]] + [along_x(cores[step], step) for step in (1, 2, 3)]
+    update = apply_cores([0], [pieces[0]], left)
     for step in (1, 3, 2):
-        update = apply_cores(step, pieces[step], left, update)
+        update = apply_cores([step], [pieces[step]], left, update)
     return jnp.swapaxes(solved, 1, 2), update
 
 

time: 134 us -> 124 us (0.925); the launches traced: 134 us -> 122 us
  starting transfers between devices: 62.7 us -> 54.5 us
  waiting for transfers between devices: 41.5 us -> 39.6 us
    ppermute x30 -> x28, starting transfers between devices: 53.7 us -> 45.5 us  [permute(): return lax.ppermute(value, AXES, pairs)]
    ppermute x30 -> x28, waiting for transfers between devices: 34.6 us -> 30.1 us  [permute(): return lax.ppermute(value, AXES, pairs)]
    all_to_all x1, waiting for transfers between devices: 6.86 us -> 9.51 us  [local(): planes = lax.all_to_all(sent, 'z', split_axis=0, concat_axis=0, tiled=True)]
    pallas_call x5, Pallas kernels: 11.6 us -> 9.99 us  [the longest x4 7.13 us: apply_cores(): pl.pallas_call(functools.partial(apply_kernel, count), out_shape=jax.Shap...]
  transfers between devices with their start and end apart: 31 -> 29, of which waited for: 14 -> 13; matrix products, arithmetic and copies ran while one was open for 5% -> 4% of each run, Pallas kernels for 6% -> 6%
where the time goes in v3:
time: 124 us; the launch traced here: 122 us
  starting transfers between devices  54.5 us (44%)
  waiting for transfers between devices  39.6 us (32%)
  Pallas kernels  16.2 us (13%)
  local copies, waits for them, and re-layouts  7.22 us (6%)
  other arithmetic  3.68 us (3%)
    ppermute x28, starting transfers between devices, permute(): return lax.ppermute(value, AXES, pairs)  45.5 us
    ppermute x28, waiting for transfers between devices, permute(): return lax.ppermute(value, AXES, pairs)  30.1 us
    all_to_all x1, waiting for transfers between devices, local(): planes = lax.all_to_all(sent, 'z', split_axis=0, concat_axis=0, tiled=True)  9.51 us
    all_to_all x1, starting transfers between devices, local(): planes = lax.all_to_all(sent, 'z', split_axis=0, concat_axis=0, tiled=True)  9.03 us
    pallas_call x4, Pallas kernels, apply_cores(): pl.pallas_call(functools.partial(apply_kernel, count), out_shape=jax.Shap...  7.13 us
    pallas_call x3, Pallas kernels, local_call(): pl.pallas_call(kernel, out_shape=outs, in_specs=[SMEM] + [VMEM] * (len(op...  5.23 us
    unnamed x28, local copies, waits for them, and re-layouts  3.1 us
    pallas_call x1, Pallas kernels, partial_cores(): pl.pallas_call(partial_kernel, out_shape=[jax.ShapeDtypeStruct((4, wide,...  2.86 us
  transfers between devices with their start and end apart: 29, of which 13 were waited for; matrix products, arithmetic and copies ran while one was open for 4% of the time, Pallas kernels for 6%

profile of v3, /device:TPU:1, one launch (start us, length us, event | category | flops | bytes accessed | tf_op | source)
XLA Modules:
  0.0 122.3 jit_solution(1223533598028750776)
XLA Ops:
  0.6 0.1 pad_add_fusion.place
  0.7 0.9 copy-done.6
  1.6 1.5 %shard_map.59 = bf16[8,208,128]{2,1,0:T(8,128)(2,1)} custom-call(s32[2]{0:T(128)S(1)} %pad_add_fusion.place, f32[80,320]{1,0:T(8,128)S(1)} %copy-done.6), custom_call_target="tpu_custom_call" | custom-call | bytes 4000000 | tf_op jit(solution)/shard_map/pallas_call | solution.py:158
  3.1 1.0 pad_maximum_fusion.3
  4.1 9.0 %all-to-all-start = ((bf16[8,208,128]{2,1,0:T(8,128)(2,1)}), bf16[8,208,128]{2,1,0:T(8,128)(2,1)S(1)}, u32[]{:S(2)}, u32[]{:S(2)}) async-start(bf16[8,208,128]{2,1,0:T(8,128)(2,1)} %shard_map.59), calls=%async_computation | async-start | bytes 851968 | tf_op jit(solution)/shard_map/all_to_all | solution.py:258
  13.2 2.9 %collective-permute-start.3 = (bf16[4,320,128]{2,1,0:T(8,128)(2,1)S(1)}, bf16[4,320,128]{2,1,0:T(8,128)(2,1)S(1)}, u32[]{:S(2)}, u32[]{:S(2)}) collective-permute-start(bf16[4,320,128]{2,1,0:T(8,128)(2,1)S(1)} %pad_maximum_fusion.3), channel_id=1, source_target_pairs={{0,4},{1,5},{2,6},{3,7},{4,0},{5,1},{6,2},{7,3},{8,12},{9,13},{10,... | collective-permute-start | bytes 983048 | tf_op jit(solution)/shard_map/ppermute | solution.py:23
  16.1 0.4 collective-permute-start.4
  16.5 2.3 %collective-permute-start.2 = (bf16[4,320,128]{2,1,0:T(8,128)(2,1)S(1)}, bf16[4,320,128]{2,1,0:T(8,128)(2,1)S(1)}, u32[]{:S(2)}, u32[]{:S(2)}) collective-permute-start(bf16[4,320,128]{2,1,0:T(8,128)(2,1)S(1)} %pad_maximum_fusion.3), channel_id=1, source_target_pairs={{0,6},{1,7},{2,0},{3,1},{4,2},{5,3},{6,4},{7,5},{8,14},{9,15},{10,... | collective-permute-start | bytes 983048 | tf_op jit(solution)/shard_map/ppermute | solution.py:23
  18.7 9.5 %all-to-all-done.here = bf16[8,208,128]{2,1,0:T(8,128)(2,1)S(1)} async-done(((bf16[8,208,128]{2,1,0:T(8,128)(2,1)}), bf16[8,208,128]{2,1,0:T(8,128)(2,1)S(1)}, u32[]{:S(2)}, u32[]{:S(2)}) %all-to-all-start) | async-done | bytes 426016 | tf_op jit(solution)/shard_map/all_to_all | solution.py:258
  28.3 1.2 collective-permute-start
  29.5 1.5 %collective-permute-start.1 = (bf16[8,208,128]{2,1,0:T(8,128)(2,1)S(1)}, bf16[8,208,128]{2,1,0:T(8,128)(2,1)S(1)}, u32[]{:S(2)}, u32[]{:S(2)}) collective-permute-start(bf16[8,208,128]{2,1,0:T(8,128)(2,1)S(1)} %all-to-all-done.here), channel_id=1, source_target_pairs={{0,24},{1,25},{2,26},{3,27},{4,28},{5,29},{6,30},{7,31},{8,0},{9,1... | collective-permute-start | bytes 1277960 | tf_op jit(solution)/shard_map/ppermute | solution.py:23
  30.9 0.4 collective-permute-done.4
  31.3 0.2 pad_maximum_fusion.own
  31.5 8.0 %collective-permute-done.below = bf16[8,208,128]{2,1,0:T(8,128)(2,1)S(1)} collective-permute-done((bf16[8,208,128]{2,1,0:T(8,128)(2,1)S(1)}, bf16[8,208,128]{2,1,0:T(8,128)(2,1)S(1)}, u32[]{:S(2)}, u32[]{:S(2)}) %collective-permute-start) | collective-permute-done | bytes 426016 | tf_op jit(solution)/shard_map/ppermute | solution.py:23
  39.5 2.2 %collective-permute-start.5 = (bf16[4,4,320,128]{3,2,1,0:T(8,128)(2,1)S(1)}, bf16[4,4,320,128]{3,2,1,0:T(8,128)(2,1)S(1)}, u32[]{:S(2)}, u32[]{:S(2)}) collective-permute-start(bf16[4,4,320,128]{3,2,1,0:T(8,128)(2,1)S(1)} %pad_maximum_fusion.own), channel_id=1, source_target_pairs={{0,1},{1,0},{2,3},{3,2},{4,5},{5,4},{6,7},{7,6},{8,9},{9,8},{10,11... | collective-permute-start | bytes 3932168 | tf_op jit(solution)/shard_map/ppermute | solution.py:23
  41.7 0.7 slice.33
  42.4 1.2 collective-permute-start.6
  43.6 0.7 slice.34
  44.3 1.5 %collective-permute-start.7 = (bf16[4,208,128]{2,1,0:T(8,128)(2,1)}, bf16[4,208,128]{2,1,0:T(8,128)(2,1)}, u32[]{:S(2)}, u32[]{:S(2)}) collective-permute-start(bf16[4,208,128]{2,1,0:T(8,128)(2,1)} %slice.34), channel_id=1, source_target_pairs={{0,24},{1,25},{2,26},{3,27},{4,28},{5,29},{6,30},{7,31},{8,0},{9,1... | collective-permute-start | bytes 638984 | tf_op jit(solution)/shard_map/ppermute | solution.py:23
  45.9 1.0 shard_map.60
  46.9 3.9 %collective-permute-done.6.first = bf16[4,208,128]{2,1,0:T(8,128)(2,1)} collective-permute-done((bf16[4,208,128]{2,1,0:T(8,128)(2,1)}, bf16[4,208,128]{2,1,0:T(8,128)(2,1)}, u32[]{:S(2)}, u32[]{:S(2)}) %collective-permute-start.6) | collective-permute-done | bytes 213024 | tf_op jit(solution)/shard_map/ppermute | solution.py:23
  50.8 0.4 collective-permute-done.7.second
  51.1 2.8 %shard_map.61 = bf16[2,320,128]{2,1,0:T(8,128)(2,1)} custom-call(s32[6]{0:T(128)S(1)} %stack.78.place, bf16[4,256,640]{2,1,0:T(8,128)(2,1)S(1)} %get-tuple-element.16.full, bf16[256,384]{1,0:T(8,128)(2,1)S(1)} %get-tuple-element.17.mine, bf16[8,208,128]{2,1,0:T(8,128)(2,1)S(1)} %all-to-all-done.here, bf16[8,208,128]{2,1,0:T(8,128)(2,1)S(1)} %copy-done.1, ...), custom_call_target="tpu_custom_call" | custom-call | flops 500000000 | bytes 4000000 | tf_op jit(solution)/shard_map/pallas_call | solution.py:158
  53.9 2.7 %collective-permute-start.8 = (bf16[2,320,128]{2,1,0:T(8,128)(2,1)}, bf16[2,320,128]{2,1,0:T(8,128)(2,1)S(1)}, u32[]{:S(2)}, u32[]{:S(2)}) collective-permute-start(bf16[2,320,128]{2,1,0:T(8,128)(2,1)} %shard_map.61), channel_id=1, source_target_pairs={{0,6},{1,7},{2,0},{3,1},{4,2},{5,3},{6,4},{7,5},{8,14},{9,15},{10,... | collective-permute-start | bytes 491528 | tf_op jit(solution)/shard_map/ppermute | solution.py:23
  56.6 0.3 collective-permute-start.9
  57.0 0.7 collective-permute-start.10
  57.7 1.9 %collective-permute-start.11 = (bf16[2,320,128]{2,1,0:T(8,128)(2,1)}, bf16[2,320,128]{2,1,0:T(8,128)(2,1)S(1)}, u32[]{:S(2)}, u32[]{:S(2)}) collective-permute-start(bf16[2,320,128]{2,1,0:T(8,128)(2,1)} %shard_map.61), channel_id=1, source_target_pairs={{0,192},{1,193},{2,224},{3,225},{4,0},{5,1},{6,32},{7,33},{8,208},... | collective-permute-start | bytes 491528 | tf_op jit(solution)/shard_map/ppermute | solution.py:23
  59.6 1.2 collective-permute-done.8
  60.8 1.8 %collective-permute-done.9 = bf16[2,320,128]{2,1,0:T(8,128)(2,1)S(1)} collective-permute-done((bf16[2,320,128]{2,1,0:T(8,128)(2,1)}, bf16[2,320,128]{2,1,0:T(8,128)(2,1)S(1)}, u32[]{:S(2)}, u32[]{:S(2)}) %collective-permute-start.9) | collective-permute-done | bytes 163872 | tf_op jit(solution)/shard_map/ppermute | solution.py:23
  62.6 6.7 %collective-permute-done.10 = bf16[2,320,128]{2,1,0:T(8,128)(2,1)S(1)} collective-permute-done((bf16[2,320,128]{2,1,0:T(8,128)(2,1)}, bf16[2,320,128]{2,1,0:T(8,128)(2,1)S(1)}, u32[]{:S(2)}, u32[]{:S(2)}) %collective-permute-start.10) | collective-permute-done | bytes 163872 | tf_op jit(solution)/shard_map/ppermute | solution.py:23
  69.3 1.0 pad_maximum_fusion.1.refs_0_
  70.3 0.1 collective-permute-start.13
  70.4 3.6 %collective-permute-start.12 = (bf16[4,2,320,128]{3,2,1,0:T(8,128)(2,1)S(1)}, bf16[4,2,320,128]{3,2,1,0:T(8,128)(2,1)S(1)}, u32[]{:S(2)}, u32[]{:S(2)}) collective-permute-start(bf16[4,2,320,128]{3,2,1,0:T(8,128)(2,1)S(1)} %pad_maximum_fusion.1.refs_0_), channel_id=1, source_target_pairs={{0,24},{1,25},{2,26},{3,27},{4,28},{5,29},{6,30},{7,31},{8,0},{9,1... | collective-permute-start | bytes 1966088 | tf_op jit(solution)/shard_map/ppermute | solution.py:23
  74.0 2.7 %collective-permute-start.16 = (bf16[2,320,128]{2,1,0:T(8,128)(2,1)S(1)}, bf16[2,320,128]{2,1,0:T(8,128)(2,1)S(1)}, u32[]{:S(2)}, u32[]{:S(2)}) collective-permute-start(bf16[2,320,128]{2,1,0:T(8,128)(2,1)S(1)} %collective-permute-done.11.refs_4_), channel_id=1, source_target_pairs={{0,224},{1,225},{2,226},{3,227},{4,228},{5,229},{6,230},{7,231},{8... | collective-permute-start | bytes 491528 | tf_op jit(solution)/shard_map/ppermute | solution.py:23
  76.7 0.7 copy-done.7
  77.3 2.3 %collective-permute-done.19.refs_11_ = bf16[2,320,128]{2,1,0:T(8,128)(2,1)S(1)} collective-permute-done((bf16[2,320,128]{2,1,0:T(8,128)(2,1)S(1)}, bf16[2,320,128]{2,1,0:T(8,128)(2,1)S(1)}, u32[]{:S(2)}, u32[]{:S(2)}) %collective-permute-start.19) | collective-permute-done | bytes 163872 | tf_op jit(solution)/shard_map/ppermute | solution.py:23
  79.7 0.7 copy-done.9
  80.4 2.7 %collective-permute-start.17 = (bf16[2,320,128]{2,1,0:T(8,128)(2,1)S(1)}, bf16[2,320,128]{2,1,0:T(8,128)(2,1)}, u32[]{:S(2)}, u32[]{:S(2)}) collective-permute-start(bf16[2,320,128]{2,1,0:T(8,128)(2,1)S(1)} %collective-permute-done.16.refs_5_), channel_id=1, source_target_pairs={{0,224},{1,225},{2,226},{3,227},{4,228},{5,229},{6,230},{7,231},{8... | collective-permute-start | bytes 491528 | tf_op jit(solution)/shard_map/ppermute | solution.py:23
  83.0 0.7 copy-done.11
  83.7 1.7 %collective-permute-done.20.refs_10_ = bf16[2,320,128]{2,1,0:T(8,128)(2,1)} collective-permute-done((bf16[2,320,128]{2,1,0:T(8,128)(2,1)S(1)}, bf16[2,320,128]{2,1,0:T(8,128)(2,1)}, u32[]{:S(2)}, u32[]{:S(2)}) %collective-permute-start.20) | collective-permute-done | bytes 163872 | tf_op jit(solution)/shard_map/ppermute | solution.py:23
  85.4 3.2 %collective-permute-start.18 = (bf16[2,320,128]{2,1,0:T(8,128)(2,1)}, bf16[2,320,128]{2,1,0:T(8,128)(2,1)}, u32[]{:S(2)}, u32[]{:S(2)}) collective-permute-start(bf16[2,320,128]{2,1,0:T(8,128)(2,1)} %collective-permute-done.17.refs_6_), channel_id=1, source_target_pairs={{0,224},{1,225},{2,226},{3,227},{4,228},{5,229},{6,230},{7,231},{8... | collective-permute-start | bytes 491528 | tf_op jit(solution)/shard_map/ppermute | solution.py:23
  88.5 0.8 slice.43
  89.3 0.9 collective-permute-start.14
  90.2 0.8 slice.44
  91.0 0.2 copy-done.4
  91.2 1.8 %collective-permute-start.15 = (bf16[2,2,320,128]{3,2,1,0:T(8,128)(2,1)}, bf16[2,2,320,128]{3,2,1,0:T(8,128)(2,1)}, u32[]{:S(2)}, u32[]{:S(2)}) collective-permute-start(bf16[2,2,320,128]{3,2,1,0:T(8,128)(2,1)} %slice.44), channel_id=1, source_target_pairs={{0,24},{1,25},{2,26},{3,27},{4,28},{5,29},{6,30},{7,31},{8,0},{9,1... | collective-permute-start | bytes 983048 | tf_op jit(solution)/shard_map/ppermute | solution.py:23
  93.0 0.1 collective-permute-start.22
  93.1 1.0 slice.46
  94.1 2.5 %collective-permute-start.23 = (bf16[2,160,128]{2,1,0:T(8,128)(2,1)S(1)}, bf16[2,160,128]{2,1,0:T(8,128)(2,1)S(1)}, u32[]{:S(2)}, u32[]{:S(2)}) collective-permute-start(bf16[2,160,128]{2,1,0:T(8,128)(2,1)S(1)} %slice.46), channel_id=1, source_target_pairs={{0,224},{1,225},{2,226},{3,227},{4,228},{5,229},{6,230},{7,231},{8... | collective-permute-start | bytes 245768 | tf_op jit(solution)/shard_map/ppermute | solution.py:23
  96.7 0.9 collective-permute-done.22
  97.6 0.6 collective-permute-done.23
  98.2 1.1 pad_maximum_fusion.2.refs_2_
  99.4 2.9 %shard_map.63 = (f32[4,256,256]{2,1,0:T(8,128)S(1)}, f32[4,256,256]{2,1,0:T(8,128)S(1)}) custom-call(s32[3]{0:T(128)S(1)} %pad_add_fusion.1.place, bf16[4,2,320,128]{3,2,1,0:T(8,128)(2,1)S(1)} %pad_maximum_fusion.1.refs_0_, bf16[4,2,320,128]{3,2,1,0:T(8,128)(2,1)S(1)} %copy-done.5, bf16[4,2,320,128]{3,2,1,0:T(8,128)(2,1)S(1)} %pad_maximum_fusion.2.refs_2_, ...), custom_call_target="tpu_custom_call" | custom-call | flops 1400000000 | bytes 6000000 | tf_op jit(solution)/shard_map/pallas_call | solution.py:98
  102.2 6.0 %collective-permute-start.24 = (f32[4,256,256]{2,1,0:T(8,128)S(1)}, f32[4,256,256]{2,1,0:T(8,128)S(1)}, u32[]{:S(2)}, u32[]{:S(2)}) collective-permute-start(f32[4,256,256]{2,1,0:T(8,128)S(1)} %get-tuple-element.23), channel_id=1, source_target_pairs={{0,1},{1,0},{2,3},{3,2},{4,5},{5,4},{6,7},{7,6},{8,9},{9,8},{10,11... | collective-permute-start | bytes 3145736 | tf_op jit(solution)/shard_map/ppermute | solution.py:23
  108.2 2.3 %collective-permute-done.24 = f32[4,256,256]{2,1,0:T(8,128)S(1)} collective-permute-done((f32[4,256,256]{2,1,0:T(8,128)S(1)}, f32[4,256,256]{2,1,0:T(8,128)S(1)}, u32[]{:S(2)}, u32[]{:S(2)}) %collective-permute-start.24) | collective-permute-done | bytes 1048608 | tf_op jit(solution)/shard_map/ppermute | solution.py:23
  110.5 0.2 add_convert_fusion
  110.7 0.1 collective-permute-start.27
  110.8 2.7 %collective-permute-start.26 = (bf16[256,256]{1,0:T(8,128)(2,1)S(1)}, bf16[256,256]{1,0:T(8,128)(2,1)S(1)}, u32[]{:S(2)}, u32[]{:S(2)}) collective-permute-start(bf16[256,256]{1,0:T(8,128)(2,1)S(1)} %get-tuple-element.26), channel_id=1, source_target_pairs={{0,24},{1,25},{2,26},{3,27},{4,28},{5,29},{6,30},{7,31},{8,0},{9,1... | collective-permute-start | bytes 393224 | tf_op jit(solution)/shard_map/ppermute | solution.py:23
  113.5 0.5 collective-permute-start.25
  114.0 1.0 shard_map.62.left
  115.0 1.8 %shard_map.64.refs_1_ = bf16[2,1,8,128,2560]{4,3,2,1,0:T(8,128)(2,1)} custom-call(s32[1]{0:T(128)} %bitcast.24.place, bf16[2,128,2560]{2,1,0:T(8,128)(2,1)S(1)} %shard_map.62.left, bf16[256,256]{1,0:T(8,128)(2,1)S(1)} %get-tuple-element.24.refs_0_), custom_call_target="tpu_custom_call" | custom-call | flops 350000000 | bytes 4000000 | tf_op jit(solution)/shard_map/pallas_call | solution.py:140
  116.8 1.8 %shard_map.65.refs_1_ = bf16[2,1,8,128,2560]{4,3,2,1,0:T(8,128)(2,1)} custom-call(s32[1]{0:T(128)} %bitcast.22.place, bf16[2,128,2560]{2,1,0:T(8,128)(2,1)S(1)} %shard_map.62.left, bf16[256,256]{1,0:T(8,128)(2,1)S(1)} %collective-permute-done.27.refs_0_, bf16[2,1,8,128,2560]{4,3,2,1,0:T(8,128)(2,1)} %shard_map.64.refs_1_), custom_call_target="tpu_custom_call", output_to_operand_aliasing={{}: (3, {})} | custom-call | flops 350000000 | bytes 4000000 | tf_op jit(solution)/shard_map/pallas_call | solution.py:140
  118.6 1.8 %shard_map.66.refs_1_ = bf16[2,1,8,128,2560]{4,3,2,1,0:T(8,128)(2,1)} custom-call(s32[1]{0:T(128)} %bitcast.20.place, bf16[2,128,2560]{2,1,0:T(8,128)(2,1)S(1)} %shard_map.62.left, bf16[256,256]{1,0:T(8,128)(2,1)S(1)} %collective-permute-done.26.refs_0_, bf16[2,1,8,128,2560]{4,3,2,1,0:T(8,128)(2,1)} %shard_map.65.refs_1_), custom_call_target="tpu_custom_call", output_to_operand_aliasing={{}: (3, {})} | custom-call | flops 350000000 | bytes 4000000 | tf_op jit(solution)/shard_map/pallas_call | solution.py:140
  120.4 1.8 %shard_map.67 = bf16[2,1,8,128,2560]{4,3,2,1,0:T(8,128)(2,1)} custom-call(s32[1]{0:T(128)} %bitcast.13.place, bf16[2,128,2560]{2,1,0:T(8,128)(2,1)S(1)} %shard_map.62.left, bf16[256,256]{1,0:T(8,128)(2,1)S(1)} %collective-permute-done.25.refs_0_, bf16[2,1,8,128,2560]{4,3,2,1,0:T(8,128)(2,1)} %shard_map.66.refs_1_), custom_call_target="tpu_custom_call", output_to_operand_aliasing={{}: (3, {})} | custom-call | flops 350000000 | bytes 4000000 | tf_op jit(solution)/shard_map/pallas_call | solution.py:140
  (47 shorter events, 0.3 us)
Async XLA Ops:
  0.7 0.9 copy-start.6
  4.1 24.1 %all-to-all-start = ((bf16[8,208,128]{2,1,0:T(8,128)(2,1)}), bf16[8,208,128]{2,1,0:T(8,128)(2,1)S(1)}, u32[]{:S(2)}, u32[]{:S(2)}) async-start(bf16[8,208,128]{2,1,0:T(8,128)(2,1)} %shard_map.59), calls=%async_computation | async-start | bytes 851968 | tf_op jit(solution)/shard_map/all_to_all | solution.py:258
  13.2 17.8 %collective-permute-start.3 = (bf16[4,320,128]{2,1,0:T(8,128)(2,1)S(1)}, bf16[4,320,128]{2,1,0:T(8,128)(2,1)S(1)}, u32[]{:S(2)}, u32[]{:S(2)}) collective-permute-start(bf16[4,320,128]{2,1,0:T(8,128)(2,1)S(1)} %pad_maximum_fusion.3), channel_id=1, source_target_pairs={{0,4},{1,5},{2,6},{3,7},{4,0},{5,1},{6,2},{7,3},{8,12},{9,13},{10,... | collective-permute-start | bytes 983048 | tf_op jit(solution)/shard_map/ppermute | solution.py:23
  16.1 15.2 %collective-permute-start.4 = (bf16[4,320,128]{2,1,0:T(8,128)(2,1)S(1)}, bf16[4,320,128]{2,1,0:T(8,128)(2,1)S(1)}, u32[]{:S(2)}, u32[]{:S(2)}) collective-permute-start(bf16[4,320,128]{2,1,0:T(8,128)(2,1)S(1)} %pad_maximum_fusion.3), channel_id=1, source_target_pairs={{0,2},{1,3},{2,4},{3,5},{4,6},{5,7},{6,0},{7,1},{8,10},{9,11},{10,... | collective-permute-start | bytes 983048 | tf_op jit(solution)/shard_map/ppermute | solution.py:23
  16.5 14.8 %collective-permute-start.2 = (bf16[4,320,128]{2,1,0:T(8,128)(2,1)S(1)}, bf16[4,320,128]{2,1,0:T(8,128)(2,1)S(1)}, u32[]{:S(2)}, u32[]{:S(2)}) collective-permute-start(bf16[4,320,128]{2,1,0:T(8,128)(2,1)S(1)} %pad_maximum_fusion.3), channel_id=1, source_target_pairs={{0,6},{1,7},{2,0},{3,1},{4,2},{5,3},{6,4},{7,5},{8,14},{9,15},{10,... | collective-permute-start | bytes 983048 | tf_op jit(solution)/shard_map/ppermute | solution.py:23
  28.3 11.3 %collective-permute-start = (bf16[8,208,128]{2,1,0:T(8,128)(2,1)S(1)}, bf16[8,208,128]{2,1,0:T(8,128)(2,1)S(1)}, u32[]{:S(2)}, u32[]{:S(2)}) collective-permute-start(bf16[8,208,128]{2,1,0:T(8,128)(2,1)S(1)} %all-to-all-done.here), channel_id=1, source_target_pairs={{0,8},{1,9},{2,10},{3,11},{4,12},{5,13},{6,14},{7,15},{8,16},{9,17... | collective-permute-start | bytes 1277960 | tf_op jit(solution)/shard_map/ppermute | solution.py:23
  29.5 10.1 %collective-permute-start.1 = (bf16[8,208,128]{2,1,0:T(8,128)(2,1)S(1)}, bf16[8,208,128]{2,1,0:T(8,128)(2,1)S(1)}, u32[]{:S(2)}, u32[]{:S(2)}) collective-permute-start(bf16[8,208,128]{2,1,0:T(8,128)(2,1)S(1)} %all-to-all-done.here), channel_id=1, source_target_pairs={{0,24},{1,25},{2,26},{3,27},{4,28},{5,29},{6,30},{7,31},{8,0},{9,1... | collective-permute-start | bytes 1277960 | tf_op jit(solution)/shard_map/ppermute | solution.py:23
  31.3 14.5 %copy-start.13 = (s32[2]{0:T(128)S(1)}, s32[2]{0:T(128)}, u32[]{:S(2)}) copy-start(s32[2]{0:T(128)} %param.6) | copy-start | bytes 28
  39.5 4.1 %copy-start = (bf16[8,208,128]{2,1,0:T(8,128)(2,1)}, bf16[8,208,128]{2,1,0:T(8,128)(2,1)S(1)}, u32[]{:S(2)}) copy-start(bf16[8,208,128]{2,1,0:T(8,128)(2,1)S(1)} %collective-permute-done.1.above) | copy-start | bytes 1277956
  39.5 6.3 %collective-permute-start.5 = (bf16[4,4,320,128]{3,2,1,0:T(8,128)(2,1)S(1)}, bf16[4,4,320,128]{3,2,1,0:T(8,128)(2,1)S(1)}, u32[]{:S(2)}, u32[]{:S(2)}) collective-permute-start(bf16[4,4,320,128]{3,2,1,0:T(8,128)(2,1)S(1)} %pad_maximum_fusion.own), channel_id=1, source_target_pairs={{0,1},{1,0},{2,3},{3,2},{4,5},{5,4},{6,7},{7,6},{8,9},{9,8},{10,11... | collective-permute-start | bytes 3932168 | tf_op jit(solution)/shard_map/ppermute | solution.py:23
  42.4 8.4 %collective-permute-start.6 = (bf16[4,208,128]{2,1,0:T(8,128)(2,1)}, bf16[4,208,128]{2,1,0:T(8,128)(2,1)}, u32[]{:S(2)}, u32[]{:S(2)}) collective-permute-start(bf16[4,208,128]{2,1,0:T(8,128)(2,1)} %slice.33), channel_id=1, source_target_pairs={{0,8},{1,9},{2,10},{3,11},{4,12},{5,13},{6,14},{7,15},{8,16},{9,17... | collective-permute-start | bytes 638984 | tf_op jit(solution)/shard_map/ppermute | solution.py:23
  44.3 6.8 %collective-permute-start.7 = (bf16[4,208,128]{2,1,0:T(8,128)(2,1)}, bf16[4,208,128]{2,1,0:T(8,128)(2,1)}, u32[]{:S(2)}, u32[]{:S(2)}) collective-permute-start(bf16[4,208,128]{2,1,0:T(8,128)(2,1)} %slice.34), channel_id=1, source_target_pairs={{0,24},{1,25},{2,26},{3,27},{4,28},{5,29},{6,30},{7,31},{8,0},{9,1... | collective-permute-start | bytes 638984 | tf_op jit(solution)/shard_map/ppermute | solution.py:23
  45.9 5.3 %copy-start.1 = (bf16[8,208,128]{2,1,0:T(8,128)(2,1)S(1)}, bf16[8,208,128]{2,1,0:T(8,128)(2,1)}, u32[]{:S(2)}) copy-start(bf16[8,208,128]{2,1,0:T(8,128)(2,1)} %copy-done) | copy-start | bytes 1277956
  53.9 6.9 %collective-permute-start.8 = (bf16[2,320,128]{2,1,0:T(8,128)(2,1)}, bf16[2,320,128]{2,1,0:T(8,128)(2,1)S(1)}, u32[]{:S(2)}, u32[]{:S(2)}) collective-permute-start(bf16[2,320,128]{2,1,0:T(8,128)(2,1)} %shard_map.61), channel_id=1, source_target_pairs={{0,6},{1,7},{2,0},{3,1},{4,2},{5,3},{6,4},{7,5},{8,14},{9,15},{10,... | collective-permute-start | bytes 491528 | tf_op jit(solution)/shard_map/ppermute | solution.py:23
  56.6 6.0 %collective-permute-start.9 = (bf16[2,320,128]{2,1,0:T(8,128)(2,1)}, bf16[2,320,128]{2,1,0:T(8,128)(2,1)S(1)}, u32[]{:S(2)}, u32[]{:S(2)}) collective-permute-start(bf16[2,320,128]{2,1,0:T(8,128)(2,1)} %shard_map.61), channel_id=1, source_target_pairs={{0,4},{1,5},{2,6},{3,7},{4,0},{5,1},{6,2},{7,3},{8,12},{9,13},{10,... | collective-permute-start | bytes 491528 | tf_op jit(solution)/shard_map/ppermute | solution.py:23
  57.0 12.3 %collective-permute-start.10 = (bf16[2,320,128]{2,1,0:T(8,128)(2,1)}, bf16[2,320,128]{2,1,0:T(8,128)(2,1)S(1)}, u32[]{:S(2)}, u32[]{:S(2)}) collective-permute-start(bf16[2,320,128]{2,1,0:T(8,128)(2,1)} %shard_map.61), channel_id=1, source_target_pairs={{0,2},{1,3},{2,4},{3,5},{4,6},{5,7},{6,0},{7,1},{8,10},{9,11},{10,... | collective-permute-start | bytes 491528 | tf_op jit(solution)/shard_map/ppermute | solution.py:23
  57.7 12.6 %collective-permute-start.11 = (bf16[2,320,128]{2,1,0:T(8,128)(2,1)}, bf16[2,320,128]{2,1,0:T(8,128)(2,1)S(1)}, u32[]{:S(2)}, u32[]{:S(2)}) collective-permute-start(bf16[2,320,128]{2,1,0:T(8,128)(2,1)} %shard_map.61), channel_id=1, source_target_pairs={{0,192},{1,193},{2,224},{3,225},{4,0},{5,1},{6,32},{7,33},{8,208},... | collective-permute-start | bytes 491528 | tf_op jit(solution)/shard_map/ppermute | solution.py:23
  70.3 18.2 %collective-permute-start.13 = (bf16[4,2,320,128]{3,2,1,0:T(8,128)(2,1)S(1)}, bf16[4,2,320,128]{3,2,1,0:T(8,128)(2,1)S(1)}, u32[]{:S(2)}, u32[]{:S(2)}) collective-permute-start(bf16[4,2,320,128]{3,2,1,0:T(8,128)(2,1)S(1)} %pad_maximum_fusion.1.refs_0_), channel_id=1, source_target_pairs={{0,8},{1,9},{2,10},{3,11},{4,12},{5,13},{6,14},{7,15},{8,16},{9,17... | collective-permute-start | bytes 1966088 | tf_op jit(solution)/shard_map/ppermute | solution.py:23
  70.4 19.8 %collective-permute-start.12 = (bf16[4,2,320,128]{3,2,1,0:T(8,128)(2,1)S(1)}, bf16[4,2,320,128]{3,2,1,0:T(8,128)(2,1)S(1)}, u32[]{:S(2)}, u32[]{:S(2)}) collective-permute-start(bf16[4,2,320,128]{3,2,1,0:T(8,128)(2,1)S(1)} %pad_maximum_fusion.1.refs_0_), channel_id=1, source_target_pairs={{0,24},{1,25},{2,26},{3,27},{4,28},{5,29},{6,30},{7,31},{8,0},{9,1... | collective-permute-start | bytes 1966088 | tf_op jit(solution)/shard_map/ppermute | solution.py:23
  74.0 5.7 %collective-permute-start.19 = (bf16[2,320,128]{2,1,0:T(8,128)(2,1)S(1)}, bf16[2,320,128]{2,1,0:T(8,128)(2,1)S(1)}, u32[]{:S(2)}, u32[]{:S(2)}) collective-permute-start(bf16[2,320,128]{2,1,0:T(8,128)(2,1)S(1)} %collective-permute-done.11.refs_4_), channel_id=1, source_target_pairs={{0,32},{1,33},{2,34},{3,35},{4,36},{5,37},{6,38},{7,39},{8,40},{9,... | collective-permute-start | bytes 491528 | tf_op jit(solution)/shard_map/ppermute | solution.py:23
  74.0 6.4 %collective-permute-start.16 = (bf16[2,320,128]{2,1,0:T(8,128)(2,1)S(1)}, bf16[2,320,128]{2,1,0:T(8,128)(2,1)S(1)}, u32[]{:S(2)}, u32[]{:S(2)}) collective-permute-start(bf16[2,320,128]{2,1,0:T(8,128)(2,1)S(1)} %collective-permute-done.11.refs_4_), channel_id=1, source_target_pairs={{0,224},{1,225},{2,226},{3,227},{4,228},{5,229},{6,230},{7,231},{8... | collective-permute-start | bytes 491528 | tf_op jit(solution)/shard_map/ppermute | solution.py:23
  76.7 0.7 copy-start.7
  79.7 5.7 %collective-permute-start.20 = (bf16[2,320,128]{2,1,0:T(8,128)(2,1)S(1)}, bf16[2,320,128]{2,1,0:T(8,128)(2,1)}, u32[]{:S(2)}, u32[]{:S(2)}) collective-permute-start(bf16[2,320,128]{2,1,0:T(8,128)(2,1)S(1)} %collective-permute-done.19.refs_11_), channel_id=1, source_target_pairs={{0,32},{1,33},{2,34},{3,35},{4,36},{5,37},{6,38},{7,39},{8,40},{9,... | collective-permute-start | bytes 491528 | tf_op jit(solution)/shard_map/ppermute | solution.py:23
  79.7 0.7 copy-start.9
  80.4 5.0 %collective-permute-start.17 = (bf16[2,320,128]{2,1,0:T(8,128)(2,1)S(1)}, bf16[2,320,128]{2,1,0:T(8,128)(2,1)}, u32[]{:S(2)}, u32[]{:S(2)}) collective-permute-start(bf16[2,320,128]{2,1,0:T(8,128)(2,1)S(1)} %collective-permute-done.16.refs_5_), channel_id=1, source_target_pairs={{0,224},{1,225},{2,226},{3,227},{4,228},{5,229},{6,230},{7,231},{8... | collective-permute-start | bytes 491528 | tf_op jit(solution)/shard_map/ppermute | solution.py:23
  83.0 0.7 copy-start.11
  85.3 7.6 %collective-permute-start.21 = (bf16[2,320,128]{2,1,0:T(8,128)(2,1)}, bf16[2,320,128]{2,1,0:T(8,128)(2,1)S(1)}, u32[]{:S(2)}, u32[]{:S(2)}) collective-permute-start(bf16[2,320,128]{2,1,0:T(8,128)(2,1)} %collective-permute-done.20.refs_10_), channel_id=1, source_target_pairs={{0,32},{1,33},{2,34},{3,35},{4,36},{5,37},{6,38},{7,39},{8,40},{9,... | collective-permute-start | bytes 491528 | tf_op jit(solution)/shard_map/ppermute | solution.py:23
  85.4 7.8 %collective-permute-start.18 = (bf16[2,320,128]{2,1,0:T(8,128)(2,1)}, bf16[2,320,128]{2,1,0:T(8,128)(2,1)}, u32[]{:S(2)}, u32[]{:S(2)}) collective-permute-start(bf16[2,320,128]{2,1,0:T(8,128)(2,1)} %collective-permute-done.17.refs_6_), channel_id=1, source_target_pairs={{0,224},{1,225},{2,226},{3,227},{4,228},{5,229},{6,230},{7,231},{8... | collective-permute-start | bytes 491528 | tf_op jit(solution)/shard_map/ppermute | solution.py:23
  88.5 1.7 %copy-start.2 = (bf16[4,2,320,128]{3,2,1,0:T(8,128)(2,1)}, bf16[4,2,320,128]{3,2,1,0:T(8,128)(2,1)S(1)}, u32[]{:S(2)}) copy-start(bf16[4,2,320,128]{3,2,1,0:T(8,128)(2,1)S(1)} %collective-permute-done.13.refs_3_) | copy-start | bytes 1966084
  89.3 8.8 %collective-permute-start.14 = (bf16[2,2,320,128]{3,2,1,0:T(8,128)(2,1)}, bf16[2,2,320,128]{3,2,1,0:T(8,128)(2,1)}, u32[]{:S(2)}, u32[]{:S(2)}) collective-permute-start(bf16[2,2,320,128]{3,2,1,0:T(8,128)(2,1)} %slice.43), channel_id=1, source_target_pairs={{0,8},{1,9},{2,10},{3,11},{4,12},{5,13},{6,14},{7,15},{8,16},{9,17... | collective-permute-start | bytes 983048 | tf_op jit(solution)/shard_map/ppermute | solution.py:23
  90.2 0.9 copy-start.4
  91.2 7.0 %collective-permute-start.15 = (bf16[2,2,320,128]{3,2,1,0:T(8,128)(2,1)}, bf16[2,2,320,128]{3,2,1,0:T(8,128)(2,1)}, u32[]{:S(2)}, u32[]{:S(2)}) collective-permute-start(bf16[2,2,320,128]{3,2,1,0:T(8,128)(2,1)} %slice.44), channel_id=1, source_target_pairs={{0,24},{1,25},{2,26},{3,27},{4,28},{5,29},{6,30},{7,31},{8,0},{9,1... | collective-permute-start | bytes 983048 | tf_op jit(solution)/shard_map/ppermute | solution.py:23
  93.0 6.4 %copy-start.3 = (bf16[4,2,320,128]{3,2,1,0:T(8,128)(2,1)S(1)}, bf16[4,2,320,128]{3,2,1,0:T(8,128)(2,1)}, u32[]{:S(2)}) copy-start(bf16[4,2,320,128]{3,2,1,0:T(8,128)(2,1)} %copy-done.2) | copy-start | bytes 1966084
  93.0 6.4 %copy-start.5 = (bf16[4,2,320,128]{3,2,1,0:T(8,128)(2,1)S(1)}, bf16[4,2,320,128]{3,2,1,0:T(8,128)(2,1)}, u32[]{:S(2)}) copy-start(bf16[4,2,320,128]{3,2,1,0:T(8,128)(2,1)} %copy-done.4) | copy-start | bytes 1966084
  93.0 6.4 %copy-start.8 = (bf16[2,320,128]{2,1,0:T(8,128)(2,1)S(1)}, bf16[2,320,128]{2,1,0:T(8,128)(2,1)}, u32[]{:S(2)}) copy-start(bf16[2,320,128]{2,1,0:T(8,128)(2,1)} %copy-done.7) | copy-start | bytes 491524
  93.0 6.4 %copy-start.10 = (bf16[2,320,128]{2,1,0:T(8,128)(2,1)S(1)}, bf16[2,320,128]{2,1,0:T(8,128)(2,1)}, u32[]{:S(2)}) copy-start(bf16[2,320,128]{2,1,0:T(8,128)(2,1)} %copy-done.9) | copy-start | bytes 491524
  93.0 6.4 %copy-start.12 = (bf16[2,320,128]{2,1,0:T(8,128)(2,1)S(1)}, bf16[2,320,128]{2,1,0:T(8,128)(2,1)}, u32[]{:S(2)}) copy-start(bf16[2,320,128]{2,1,0:T(8,128)(2,1)} %copy-done.11) | copy-start | bytes 491524
  93.0 4.6 %collective-permute-start.22 = (bf16[2,160,128]{2,1,0:T(8,128)(2,1)S(1)}, bf16[2,160,128]{2,1,0:T(8,128)(2,1)S(1)}, u32[]{:S(2)}, u32[]{:S(2)}) collective-permute-start(bf16[2,160,128]{2,1,0:T(8,128)(2,1)S(1)} %slice.45), channel_id=1, source_target_pairs={{0,32},{1,33},{2,34},{3,35},{4,36},{5,37},{6,38},{7,39},{8,40},{9,... | collective-permute-start | bytes 245768 | tf_op jit(solution)/shard_map/ppermute | solution.py:23
  94.1 4.0 %collective-permute-start.23 = (bf16[2,160,128]{2,1,0:T(8,128)(2,1)S(1)}, bf16[2,160,128]{2,1,0:T(8,128)(2,1)S(1)}, u32[]{:S(2)}, u32[]{:S(2)}) collective-permute-start(bf16[2,160,128]{2,1,0:T(8,128)(2,1)S(1)} %slice.46), channel_id=1, source_target_pairs={{0,224},{1,225},{2,226},{3,227},{4,228},{5,229},{6,230},{7,231},{8... | collective-permute-start | bytes 245768 | tf_op jit(solution)/shard_map/ppermute | solution.py:23
  102.2 8.3 %collective-permute-start.24 = (f32[4,256,256]{2,1,0:T(8,128)S(1)}, f32[4,256,256]{2,1,0:T(8,128)S(1)}, u32[]{:S(2)}, u32[]{:S(2)}) collective-permute-start(f32[4,256,256]{2,1,0:T(8,128)S(1)} %get-tuple-element.23), channel_id=1, source_target_pairs={{0,1},{1,0},{2,3},{3,2},{4,5},{5,4},{6,7},{7,6},{8,9},{9,8},{10,11... | collective-permute-start | bytes 3145736 | tf_op jit(solution)/shard_map/ppermute | solution.py:23
  110.7 6.0 %collective-permute-start.27 = (bf16[256,256]{1,0:T(8,128)(2,1)S(1)}, bf16[256,256]{1,0:T(8,128)(2,1)S(1)}, u32[]{:S(2)}, u32[]{:S(2)}) collective-permute-start(bf16[256,256]{1,0:T(8,128)(2,1)S(1)} %get-tuple-element.25), channel_id=1, source_target_pairs={{0,8},{1,9},{2,10},{3,11},{4,12},{5,13},{6,14},{7,15},{8,16},{9,17... | collective-permute-start | bytes 393224 | tf_op jit(solution)/shard_map/ppermute | solution.py:23
  110.8 7.7 %collective-permute-start.26 = (bf16[256,256]{1,0:T(8,128)(2,1)S(1)}, bf16[256,256]{1,0:T(8,128)(2,1)S(1)}, u32[]{:S(2)}, u32[]{:S(2)}) collective-permute-start(bf16[256,256]{1,0:T(8,128)(2,1)S(1)} %get-tuple-element.26), channel_id=1, source_target_pairs={{0,24},{1,25},{2,26},{3,27},{4,28},{5,29},{6,30},{7,31},{8,0},{9,1... | collective-permute-start | bytes 393224 | tf_op jit(solution)/shard_map/ppermute | solution.py:23
  113.5 6.9 %collective-permute-start.25 = (bf16[256,256]{1,0:T(8,128)(2,1)S(1)}, bf16[256,256]{1,0:T(8,128)(2,1)S(1)}, u32[]{:S(2)}, u32[]{:S(2)}) collective-permute-start(bf16[256,256]{1,0:T(8,128)(2,1)S(1)} %get-tuple-element.27), channel_id=1, source_target_pairs={{0,16},{1,17},{2,18},{3,19},{4,20},{5,21},{6,22},{7,23},{8,24},{9,... | collective-permute-start | bytes 393224 | tf_op jit(solution)/shard_map/ppermute | solution.py:23

commit v4 on v3

--- a/solution.py
+++ b/solution.py
@@ -287,7 +287,8 @@
     rows = ring_of_four(rows, along_x, 0)
     kept, given = partial_cores(rows, lines)
     given = permute(given, lambda z, x, y, core: (z, x, y, core + 1))
-    cores = (kept + given.astype(jnp.float32)).astype(half)
+    given, left = lax.optimization_barrier((given, left))
+    cores = (kept + given).astype(half)
     pieces = [cores[0]] + [along_x(cores[step], step) for step in (1, 2, 3)]
     update = apply_cores([0], [pieces[0]], left)
     for step in (1, 3, 2):

time: 124 us -> 124 us (level)
    unnamed x28 -> x24, local copies, waits for them, and re-layouts: 3.1 us -> 2.98 us
  transfers between devices with their start and end apart: 29 -> 29, of which waited for: 13 -> 14; matrix products, arithmetic and copies ran while one was open for 4% -> 4% of each run, Pallas kernels for 6% -> 6%
where the time goes in v4:
time: 124 us; the launch traced here: 122 us
  starting transfers between devices  54.5 us (44%)
  waiting for transfers between devices  39.6 us (32%)
  Pallas kernels  16.3 us (13%)
  local copies, waits for them, and re-layouts  7.01 us (6%)
  other arithmetic  3.67 us (3%)
    ppermute x28, starting transfers between devices, permute(): return lax.ppermute(value, AXES, pairs)  45.5 us
    ppermute x28, waiting for transfers between devices, permute(): return lax.ppermute(value, AXES, pairs)  30.1 us
    all_to_all x1, waiting for transfers between devices, local(): planes = lax.all_to_all(sent, 'z', split_axis=0, concat_axis=0, tiled=True)  9.51 us
    all_to_all x1, starting transfers between devices, local(): planes = lax.all_to_all(sent, 'z', split_axis=0, concat_axis=0, tiled=True)  9.03 us
    pallas_call x4, Pallas kernels, apply_cores(): pl.pallas_call(functools.partial(apply_kernel, count), out_shape=jax.Shap...  7.12 us
    pallas_call x3, Pallas kernels, local_call(): pl.pallas_call(kernel, out_shape=outs, in_specs=[SMEM] + [VMEM] * (len(op...  5.23 us
    unnamed x24, local copies, waits for them, and re-layouts  2.98 us
    pallas_call x1, Pallas kernels, partial_cores(): pl.pallas_call(partial_kernel, out_shape=[jax.ShapeDtypeStruct((4, wide,...  2.95 us
  transfers between devices with their start and end apart: 29, of which 14 were waited for; matrix products, arithmetic and copies ran while one was open for 4% of the time, Pallas kernels for 6%

profile of v4, /device:TPU:1, one launch (start us, length us, event | category | flops | bytes accessed | tf_op | source)
XLA Modules:
  0.0 122.1 jit_solution(2537067239424337553)
XLA Ops:
  0.6 0.1 pad_add_fusion.place
  0.7 0.9 copy-done.4
  1.6 1.5 %shard_map.59 = bf16[8,208,128]{2,1,0:T(8,128)(2,1)} custom-call(s32[2]{0:T(128)S(1)} %pad_add_fusion.place, f32[80,320]{1,0:T(8,128)S(1)} %copy-done.4), custom_call_target="tpu_custom_call" | custom-call | bytes 4000000 | tf_op jit(solution)/shard_map/pallas_call | solution.py:158
  3.1 1.0 pad_maximum_fusion.3
  4.1 9.0 %all-to-all-start = ((bf16[8,208,128]{2,1,0:T(8,128)(2,1)}), bf16[8,208,128]{2,1,0:T(8,128)(2,1)S(1)}, u32[]{:S(2)}, u32[]{:S(2)}) async-start(bf16[8,208,128]{2,1,0:T(8,128)(2,1)} %shard_map.59), calls=%async_computation | async-start | bytes 851968 | tf_op jit(solution)/shard_map/all_to_all | solution.py:258
  13.2 2.9 %collective-permute-start.3 = (bf16[4,320,128]{2,1,0:T(8,128)(2,1)S(1)}, bf16[4,320,128]{2,1,0:T(8,128)(2,1)S(1)}, u32[]{:S(2)}, u32[]{:S(2)}) collective-permute-start(bf16[4,320,128]{2,1,0:T(8,128)(2,1)S(1)} %pad_maximum_fusion.3), channel_id=1, source_target_pairs={{0,4},{1,5},{2,6},{3,7},{4,0},{5,1},{6,2},{7,3},{8,12},{9,13},{10,... | collective-permute-start | bytes 983048 | tf_op jit(solution)/shard_map/ppermute | solution.py:23
  16.1 0.4 collective-permute-start.4
  16.5 2.3 %collective-permute-start.2 = (bf16[4,320,128]{2,1,0:T(8,128)(2,1)S(1)}, bf16[4,320,128]{2,1,0:T(8,128)(2,1)S(1)}, u32[]{:S(2)}, u32[]{:S(2)}) collective-permute-start(bf16[4,320,128]{2,1,0:T(8,128)(2,1)S(1)} %pad_maximum_fusion.3), channel_id=1, source_target_pairs={{0,6},{1,7},{2,0},{3,1},{4,2},{5,3},{6,4},{7,5},{8,14},{9,15},{10,... | collective-permute-start | bytes 983048 | tf_op jit(solution)/shard_map/ppermute | solution.py:23
  18.7 9.5 %all-to-all-done.here = bf16[8,208,128]{2,1,0:T(8,128)(2,1)S(1)} async-done(((bf16[8,208,128]{2,1,0:T(8,128)(2,1)}), bf16[8,208,128]{2,1,0:T(8,128)(2,1)S(1)}, u32[]{:S(2)}, u32[]{:S(2)}) %all-to-all-start) | async-done | bytes 426016 | tf_op jit(solution)/shard_map/all_to_all | solution.py:258
  28.3 1.2 collective-permute-start
  29.5 1.5 %collective-permute-start.1 = (bf16[8,208,128]{2,1,0:T(8,128)(2,1)S(1)}, bf16[8,208,128]{2,1,0:T(8,128)(2,1)S(1)}, u32[]{:S(2)}, u32[]{:S(2)}) collective-permute-start(bf16[8,208,128]{2,1,0:T(8,128)(2,1)S(1)} %all-to-all-done.here), channel_id=1, source_target_pairs={{0,24},{1,25},{2,26},{3,27},{4,28},{5,29},{6,30},{7,31},{8,0},{9,1... | collective-permute-start | bytes 1277960 | tf_op jit(solution)/shard_map/ppermute | solution.py:23
  30.9 0.4 collective-permute-done.4
  31.3 0.2 pad_maximum_fusion.own
  31.5 8.0 %collective-permute-done.below = bf16[8,208,128]{2,1,0:T(8,128)(2,1)S(1)} collective-permute-done((bf16[8,208,128]{2,1,0:T(8,128)(2,1)S(1)}, bf16[8,208,128]{2,1,0:T(8,128)(2,1)S(1)}, u32[]{:S(2)}, u32[]{:S(2)}) %collective-permute-start) | collective-permute-done | bytes 426016 | tf_op jit(solution)/shard_map/ppermute | solution.py:23
  39.5 2.2 %collective-permute-start.5 = (bf16[4,4,320,128]{3,2,1,0:T(8,128)(2,1)S(1)}, bf16[4,4,320,128]{3,2,1,0:T(8,128)(2,1)S(1)}, u32[]{:S(2)}, u32[]{:S(2)}) collective-permute-start(bf16[4,4,320,128]{3,2,1,0:T(8,128)(2,1)S(1)} %pad_maximum_fusion.own), channel_id=1, source_target_pairs={{0,1},{1,0},{2,3},{3,2},{4,5},{5,4},{6,7},{7,6},{8,9},{9,8},{10,11... | collective-permute-start | bytes 3932168 | tf_op jit(solution)/shard_map/ppermute | solution.py:23
  41.7 0.7 slice.33
  42.4 1.2 collective-permute-start.6
  43.6 0.7 slice.34
  44.3 1.5 %collective-permute-start.7 = (bf16[4,208,128]{2,1,0:T(8,128)(2,1)}, bf16[4,208,128]{2,1,0:T(8,128)(2,1)}, u32[]{:S(2)}, u32[]{:S(2)}) collective-permute-start(bf16[4,208,128]{2,1,0:T(8,128)(2,1)} %slice.34), channel_id=1, source_target_pairs={{0,24},{1,25},{2,26},{3,27},{4,28},{5,29},{6,30},{7,31},{8,0},{9,1... | collective-permute-start | bytes 638984 | tf_op jit(solution)/shard_map/ppermute | solution.py:23
  45.9 1.0 shard_map.60
  46.9 3.8 %collective-permute-done.6.first = bf16[4,208,128]{2,1,0:T(8,128)(2,1)} collective-permute-done((bf16[4,208,128]{2,1,0:T(8,128)(2,1)}, bf16[4,208,128]{2,1,0:T(8,128)(2,1)}, u32[]{:S(2)}, u32[]{:S(2)}) %collective-permute-start.6) | collective-permute-done | bytes 213024 | tf_op jit(solution)/shard_map/ppermute | solution.py:23
  50.8 0.4 collective-permute-done.7.second
  51.2 2.8 %shard_map.61 = bf16[2,320,128]{2,1,0:T(8,128)(2,1)} custom-call(s32[6]{0:T(128)S(1)} %stack.78.place, bf16[4,256,640]{2,1,0:T(8,128)(2,1)S(1)} %get-tuple-element.18.full, bf16[256,384]{1,0:T(8,128)(2,1)S(1)} %get-tuple-element.19.mine, bf16[8,208,128]{2,1,0:T(8,128)(2,1)S(1)} %all-to-all-done.here, bf16[8,208,128]{2,1,0:T(8,128)(2,1)S(1)} %copy-done.3, ...), custom_call_target="tpu_custom_call" | custom-call | flops 500000000 | bytes 4000000 | tf_op jit(solution)/shard_map/pallas_call | solution.py:158
  53.9 2.7 %collective-permute-start.8 = (bf16[2,320,128]{2,1,0:T(8,128)(2,1)}, bf16[2,320,128]{2,1,0:T(8,128)(2,1)S(1)}, u32[]{:S(2)}, u32[]{:S(2)}) collective-permute-start(bf16[2,320,128]{2,1,0:T(8,128)(2,1)} %shard_map.61), channel_id=1, source_target_pairs={{0,6},{1,7},{2,0},{3,1},{4,2},{5,3},{6,4},{7,5},{8,14},{9,15},{10,... | collective-permute-start | bytes 491528 | tf_op jit(solution)/shard_map/ppermute | solution.py:23
  56.7 0.3 collective-permute-start.9
  57.0 0.7 collective-permute-start.10
  57.7 1.9 %collective-permute-start.11 = (bf16[2,320,128]{2,1,0:T(8,128)(2,1)}, bf16[2,320,128]{2,1,0:T(8,128)(2,1)S(1)}, u32[]{:S(2)}, u32[]{:S(2)}) collective-permute-start(bf16[2,320,128]{2,1,0:T(8,128)(2,1)} %shard_map.61), channel_id=1, source_target_pairs={{0,192},{1,193},{2,224},{3,225},{4,0},{5,1},{6,32},{7,33},{8,208},... | collective-permute-start | bytes 491528 | tf_op jit(solution)/shard_map/ppermute | solution.py:23
  59.6 1.2 %collective-permute-done.8 = bf16[2,320,128]{2,1,0:T(8,128)(2,1)S(1)} collective-permute-done((bf16[2,320,128]{2,1,0:T(8,128)(2,1)}, bf16[2,320,128]{2,1,0:T(8,128)(2,1)S(1)}, u32[]{:S(2)}, u32[]{:S(2)}) %collective-permute-start.8) | collective-permute-done | bytes 163872 | tf_op jit(solution)/shard_map/ppermute | solution.py:23
  60.9 1.8 %collective-permute-done.9 = bf16[2,320,128]{2,1,0:T(8,128)(2,1)S(1)} collective-permute-done((bf16[2,320,128]{2,1,0:T(8,128)(2,1)}, bf16[2,320,128]{2,1,0:T(8,128)(2,1)S(1)}, u32[]{:S(2)}, u32[]{:S(2)}) %collective-permute-start.9) | collective-permute-done | bytes 163872 | tf_op jit(solution)/shard_map/ppermute | solution.py:23
  62.6 6.7 %collective-permute-done.10 = bf16[2,320,128]{2,1,0:T(8,128)(2,1)S(1)} collective-permute-done((bf16[2,320,128]{2,1,0:T(8,128)(2,1)}, bf16[2,320,128]{2,1,0:T(8,128)(2,1)S(1)}, u32[]{:S(2)}, u32[]{:S(2)}) %collective-permute-start.10) | collective-permute-done | bytes 163872 | tf_op jit(solution)/shard_map/ppermute | solution.py:23
  69.4 1.0 pad_maximum_fusion.1.refs_0_
  70.4 0.1 collective-permute-start.13
  70.5 3.6 %collective-permute-start.12 = (bf16[4,2,320,128]{3,2,1,0:T(8,128)(2,1)S(1)}, bf16[4,2,320,128]{3,2,1,0:T(8,128)(2,1)S(1)}, u32[]{:S(2)}, u32[]{:S(2)}) collective-permute-start(bf16[4,2,320,128]{3,2,1,0:T(8,128)(2,1)S(1)} %pad_maximum_fusion.1.refs_0_), channel_id=1, source_target_pairs={{0,24},{1,25},{2,26},{3,27},{4,28},{5,29},{6,30},{7,31},{8,0},{9,1... | collective-permute-start | bytes 1966088 | tf_op jit(solution)/shard_map/ppermute | solution.py:23
  74.0 2.7 %collective-permute-start.16 = (bf16[2,320,128]{2,1,0:T(8,128)(2,1)S(1)}, bf16[2,320,128]{2,1,0:T(8,128)(2,1)S(1)}, u32[]{:S(2)}, u32[]{:S(2)}) collective-permute-start(bf16[2,320,128]{2,1,0:T(8,128)(2,1)S(1)} %collective-permute-done.11.refs_4_), channel_id=1, source_target_pairs={{0,224},{1,225},{2,226},{3,227},{4,228},{5,229},{6,230},{7,231},{8... | collective-permute-start | bytes 491528 | tf_op jit(solution)/shard_map/ppermute | solution.py:23
  76.7 0.7 copy-done.5
  77.4 2.3 %collective-permute-done.19.refs_11_ = bf16[2,320,128]{2,1,0:T(8,128)(2,1)S(1)} collective-permute-done((bf16[2,320,128]{2,1,0:T(8,128)(2,1)S(1)}, bf16[2,320,128]{2,1,0:T(8,128)(2,1)S(1)}, u32[]{:S(2)}, u32[]{:S(2)}) %collective-permute-start.19) | collective-permute-done | bytes 163872 | tf_op jit(solution)/shard_map/ppermute | solution.py:23
  79.7 0.7 copy-done.7
  80.4 2.7 %collective-permute-start.17 = (bf16[2,320,128]{2,1,0:T(8,128)(2,1)S(1)}, bf16[2,320,128]{2,1,0:T(8,128)(2,1)}, u32[]{:S(2)}, u32[]{:S(2)}) collective-permute-start(bf16[2,320,128]{2,1,0:T(8,128)(2,1)S(1)} %collective-permute-done.16.refs_5_), channel_id=1, source_target_pairs={{0,224},{1,225},{2,226},{3,227},{4,228},{5,229},{6,230},{7,231},{8... | collective-permute-start | bytes 491528 | tf_op jit(solution)/shard_map/ppermute | solution.py:23
  83.1 0.7 copy-done.9
  83.7 1.7 %collective-permute-done.20.refs_10_ = bf16[2,320,128]{2,1,0:T(8,128)(2,1)} collective-permute-done((bf16[2,320,128]{2,1,0:T(8,128)(2,1)S(1)}, bf16[2,320,128]{2,1,0:T(8,128)(2,1)}, u32[]{:S(2)}, u32[]{:S(2)}) %collective-permute-start.20) | collective-permute-done | bytes 163872 | tf_op jit(solution)/shard_map/ppermute | solution.py:23
  85.4 3.2 %collective-permute-start.18 = (bf16[2,320,128]{2,1,0:T(8,128)(2,1)}, bf16[2,320,128]{2,1,0:T(8,128)(2,1)}, u32[]{:S(2)}, u32[]{:S(2)}) collective-permute-start(bf16[2,320,128]{2,1,0:T(8,128)(2,1)} %collective-permute-done.17.refs_6_), channel_id=1, source_target_pairs={{0,224},{1,225},{2,226},{3,227},{4,228},{5,229},{6,230},{7,231},{8... | collective-permute-start | bytes 491528 | tf_op jit(solution)/shard_map/ppermute | solution.py:23
  88.6 0.8 slice.43
  89.3 0.9 collective-permute-start.14
  90.3 0.8 slice.44
  91.0 1.7 %collective-permute-start.15 = (bf16[2,2,320,128]{3,2,1,0:T(8,128)(2,1)}, bf16[2,2,320,128]{3,2,1,0:T(8,128)(2,1)}, u32[]{:S(2)}, u32[]{:S(2)}) collective-permute-start(bf16[2,2,320,128]{3,2,1,0:T(8,128)(2,1)} %slice.44), channel_id=1, source_target_pairs={{0,24},{1,25},{2,26},{3,27},{4,28},{5,29},{6,30},{7,31},{8,0},{9,1... | collective-permute-start | bytes 983048 | tf_op jit(solution)/shard_map/ppermute | solution.py:23
  92.8 0.1 collective-permute-start.22
  92.9 1.0 slice.46
  93.9 2.6 %collective-permute-start.23 = (bf16[2,160,128]{2,1,0:T(8,128)(2,1)S(1)}, bf16[2,160,128]{2,1,0:T(8,128)(2,1)S(1)}, u32[]{:S(2)}, u32[]{:S(2)}) collective-permute-start(bf16[2,160,128]{2,1,0:T(8,128)(2,1)S(1)} %slice.46), channel_id=1, source_target_pairs={{0,224},{1,225},{2,226},{3,227},{4,228},{5,229},{6,230},{7,231},{8... | collective-permute-start | bytes 245768 | tf_op jit(solution)/shard_map/ppermute | solution.py:23
  96.5 0.9 collective-permute-done.22
  97.4 0.6 collective-permute-done.23
  97.9 1.1 pad_maximum_fusion.2.refs_2_
  99.1 3.0 %shard_map.62 = (f32[4,256,256]{2,1,0:T(8,128)S(1)}, f32[4,256,256]{2,1,0:T(8,128)S(1)}) custom-call(s32[3]{0:T(128)S(1)} %pad_add_fusion.1.place, bf16[4,2,320,128]{3,2,1,0:T(8,128)(2,1)S(1)} %pad_maximum_fusion.1.refs_0_, bf16[4,2,320,128]{3,2,1,0:T(8,128)(2,1)S(1)} %collective-permute-done.12.refs_1_, ...), custom_call_target="tpu_custom_call" | custom-call | flops 1400000000 | bytes 6000000 | tf_op jit(solution)/shard_map/pallas_call | solution.py:98
  102.1 6.0 %collective-permute-start.24 = (f32[4,256,256]{2,1,0:T(8,128)S(1)}, f32[4,256,256]{2,1,0:T(8,128)S(1)}, u32[]{:S(2)}, u32[]{:S(2)}) collective-permute-start(f32[4,256,256]{2,1,0:T(8,128)S(1)} %get-tuple-element.24), channel_id=1, source_target_pairs={{0,1},{1,0},{2,3},{3,2},{4,5},{5,4},{6,7},{7,6},{8,9},{9,8},{10,11... | collective-permute-start | bytes 3145736 | tf_op jit(solution)/shard_map/ppermute | solution.py:23
  108.0 1.0 shard_map.63.left
  109.0 1.3 %collective-permute-done.24 = f32[4,256,256]{2,1,0:T(8,128)S(1)} collective-permute-done((f32[4,256,256]{2,1,0:T(8,128)S(1)}, f32[4,256,256]{2,1,0:T(8,128)S(1)}, u32[]{:S(2)}, u32[]{:S(2)}) %collective-permute-start.24) | collective-permute-done | bytes 1048608 | tf_op jit(solution)/shard_map/ppermute | solution.py:23
  110.3 0.2 add_convert_fusion
  110.6 0.1 collective-permute-start.27
  110.7 2.7 %collective-permute-start.26 = (bf16[256,256]{1,0:T(8,128)(2,1)S(1)}, bf16[256,256]{1,0:T(8,128)(2,1)S(1)}, u32[]{:S(2)}, u32[]{:S(2)}) collective-permute-start(bf16[256,256]{1,0:T(8,128)(2,1)S(1)} %get-tuple-element.30), channel_id=1, source_target_pairs={{0,24},{1,25},{2,26},{3,27},{4,28},{5,29},{6,30},{7,31},{8,0},{9,1... | collective-permute-start | bytes 393224 | tf_op jit(solution)/shard_map/ppermute | solution.py:23
  113.3 0.5 collective-permute-start.25
  113.8 1.8 %shard_map.64.refs_1_ = bf16[2,1,8,128,2560]{4,3,2,1,0:T(8,128)(2,1)} custom-call(s32[1]{0:T(128)} %bitcast.24.place, bf16[2,128,2560]{2,1,0:T(8,128)(2,1)S(1)} %shard_map.63.left, bf16[256,256]{1,0:T(8,128)(2,1)S(1)} %get-tuple-element.28.refs_0_), custom_call_target="tpu_custom_call" | custom-call | flops 350000000 | bytes 4000000 | tf_op jit(solution)/shard_map/pallas_call | solution.py:140
  115.6 1.0 collective-permute-done.27.refs_0_
  116.6 1.8 %shard_map.65.refs_1_ = bf16[2,1,8,128,2560]{4,3,2,1,0:T(8,128)(2,1)} custom-call(s32[1]{0:T(128)} %bitcast.22.place, bf16[2,128,2560]{2,1,0:T(8,128)(2,1)S(1)} %shard_map.63.left, bf16[256,256]{1,0:T(8,128)(2,1)S(1)} %collective-permute-done.27.refs_0_, bf16[2,1,8,128,2560]{4,3,2,1,0:T(8,128)(2,1)} %shard_map.64.refs_1_), custom_call_target="tpu_custom_call", output_to_operand_aliasing={{}: (3, {})} | custom-call | flops 350000000 | bytes 4000000 | tf_op jit(solution)/shard_map/pallas_call | solution.py:140
  118.4 1.8 %shard_map.66.refs_1_ = bf16[2,1,8,128,2560]{4,3,2,1,0:T(8,128)(2,1)} custom-call(s32[1]{0:T(128)} %bitcast.20.place, bf16[2,128,2560]{2,1,0:T(8,128)(2,1)S(1)} %shard_map.63.left, bf16[256,256]{1,0:T(8,128)(2,1)S(1)} %collective-permute-done.26.refs_0_, bf16[2,1,8,128,2560]{4,3,2,1,0:T(8,128)(2,1)} %shard_map.65.refs_1_), custom_call_target="tpu_custom_call", output_to_operand_aliasing={{}: (3, {})} | custom-call | flops 350000000 | bytes 4000000 | tf_op jit(solution)/shard_map/pallas_call | solution.py:140
  120.2 1.8 %shard_map.67 = bf16[2,1,8,128,2560]{4,3,2,1,0:T(8,128)(2,1)} custom-call(s32[1]{0:T(128)} %bitcast.13.place, bf16[2,128,2560]{2,1,0:T(8,128)(2,1)S(1)} %shard_map.63.left, bf16[256,256]{1,0:T(8,128)(2,1)S(1)} %collective-permute-done.25.refs_0_, bf16[2,1,8,128,2560]{4,3,2,1,0:T(8,128)(2,1)} %shard_map.66.refs_1_), custom_call_target="tpu_custom_call", output_to_operand_aliasing={{}: (3, {})} | custom-call | flops 350000000 | bytes 4000000 | tf_op jit(solution)/shard_map/pallas_call | solution.py:140
  (43 shorter events, 0.3 us)
Async XLA Ops:
  0.7 0.9 copy-start.4
  4.1 24.1 %all-to-all-start = ((bf16[8,208,128]{2,1,0:T(8,128)(2,1)}), bf16[8,208,128]{2,1,0:T(8,128)(2,1)S(1)}, u32[]{:S(2)}, u32[]{:S(2)}) async-start(bf16[8,208,128]{2,1,0:T(8,128)(2,1)} %shard_map.59), calls=%async_computation | async-start | bytes 851968 | tf_op jit(solution)/shard_map/all_to_all | solution.py:258
  13.2 17.8 %collective-permute-start.3 = (bf16[4,320,128]{2,1,0:T(8,128)(2,1)S(1)}, bf16[4,320,128]{2,1,0:T(8,128)(2,1)S(1)}, u32[]{:S(2)}, u32[]{:S(2)}) collective-permute-start(bf16[4,320,128]{2,1,0:T(8,128)(2,1)S(1)} %pad_maximum_fusion.3), channel_id=1, source_target_pairs={{0,4},{1,5},{2,6},{3,7},{4,0},{5,1},{6,2},{7,3},{8,12},{9,13},{10,... | collective-permute-start | bytes 983048 | tf_op jit(solution)/shard_map/ppermute | solution.py:23
  16.1 15.2 %collective-permute-start.4 = (bf16[4,320,128]{2,1,0:T(8,128)(2,1)S(1)}, bf16[4,320,128]{2,1,0:T(8,128)(2,1)S(1)}, u32[]{:S(2)}, u32[]{:S(2)}) collective-permute-start(bf16[4,320,128]{2,1,0:T(8,128)(2,1)S(1)} %pad_maximum_fusion.3), channel_id=1, source_target_pairs={{0,2},{1,3},{2,4},{3,5},{4,6},{5,7},{6,0},{7,1},{8,10},{9,11},{10,... | collective-permute-start | bytes 983048 | tf_op jit(solution)/shard_map/ppermute | solution.py:23
  16.5 14.8 %collective-permute-start.2 = (bf16[4,320,128]{2,1,0:T(8,128)(2,1)S(1)}, bf16[4,320,128]{2,1,0:T(8,128)(2,1)S(1)}, u32[]{:S(2)}, u32[]{:S(2)}) collective-permute-start(bf16[4,320,128]{2,1,0:T(8,128)(2,1)S(1)} %pad_maximum_fusion.3), channel_id=1, source_target_pairs={{0,6},{1,7},{2,0},{3,1},{4,2},{5,3},{6,4},{7,5},{8,14},{9,15},{10,... | collective-permute-start | bytes 983048 | tf_op jit(solution)/shard_map/ppermute | solution.py:23
  28.3 11.3 %collective-permute-start = (bf16[8,208,128]{2,1,0:T(8,128)(2,1)S(1)}, bf16[8,208,128]{2,1,0:T(8,128)(2,1)S(1)}, u32[]{:S(2)}, u32[]{:S(2)}) collective-permute-start(bf16[8,208,128]{2,1,0:T(8,128)(2,1)S(1)} %all-to-all-done.here), channel_id=1, source_target_pairs={{0,8},{1,9},{2,10},{3,11},{4,12},{5,13},{6,14},{7,15},{8,16},{9,17... | collective-permute-start | bytes 1277960 | tf_op jit(solution)/shard_map/ppermute | solution.py:23
  29.5 10.1 %collective-permute-start.1 = (bf16[8,208,128]{2,1,0:T(8,128)(2,1)S(1)}, bf16[8,208,128]{2,1,0:T(8,128)(2,1)S(1)}, u32[]{:S(2)}, u32[]{:S(2)}) collective-permute-start(bf16[8,208,128]{2,1,0:T(8,128)(2,1)S(1)} %all-to-all-done.here), channel_id=1, source_target_pairs={{0,24},{1,25},{2,26},{3,27},{4,28},{5,29},{6,30},{7,31},{8,0},{9,1... | collective-permute-start | bytes 1277960 | tf_op jit(solution)/shard_map/ppermute | solution.py:23
  31.3 14.5 %copy-start.11 = (s32[2]{0:T(128)S(1)}, s32[2]{0:T(128)}, u32[]{:S(2)}) copy-start(s32[2]{0:T(128)} %param.6) | copy-start | bytes 28
  39.5 4.1 %copy-start.2 = (bf16[8,208,128]{2,1,0:T(8,128)(2,1)}, bf16[8,208,128]{2,1,0:T(8,128)(2,1)S(1)}, u32[]{:S(2)}) copy-start(bf16[8,208,128]{2,1,0:T(8,128)(2,1)S(1)} %collective-permute-done.1.above) | copy-start | bytes 1277956
  39.5 6.3 %collective-permute-start.5 = (bf16[4,4,320,128]{3,2,1,0:T(8,128)(2,1)S(1)}, bf16[4,4,320,128]{3,2,1,0:T(8,128)(2,1)S(1)}, u32[]{:S(2)}, u32[]{:S(2)}) collective-permute-start(bf16[4,4,320,128]{3,2,1,0:T(8,128)(2,1)S(1)} %pad_maximum_fusion.own), channel_id=1, source_target_pairs={{0,1},{1,0},{2,3},{3,2},{4,5},{5,4},{6,7},{7,6},{8,9},{9,8},{10,11... | collective-permute-start | bytes 3932168 | tf_op jit(solution)/shard_map/ppermute | solution.py:23
  42.4 8.4 %collective-permute-start.6 = (bf16[4,208,128]{2,1,0:T(8,128)(2,1)}, bf16[4,208,128]{2,1,0:T(8,128)(2,1)}, u32[]{:S(2)}, u32[]{:S(2)}) collective-permute-start(bf16[4,208,128]{2,1,0:T(8,128)(2,1)} %slice.33), channel_id=1, source_target_pairs={{0,8},{1,9},{2,10},{3,11},{4,12},{5,13},{6,14},{7,15},{8,16},{9,17... | collective-permute-start | bytes 638984 | tf_op jit(solution)/shard_map/ppermute | solution.py:23
  44.3 6.8 %collective-permute-start.7 = (bf16[4,208,128]{2,1,0:T(8,128)(2,1)}, bf16[4,208,128]{2,1,0:T(8,128)(2,1)}, u32[]{:S(2)}, u32[]{:S(2)}) collective-permute-start(bf16[4,208,128]{2,1,0:T(8,128)(2,1)} %slice.34), channel_id=1, source_target_pairs={{0,24},{1,25},{2,26},{3,27},{4,28},{5,29},{6,30},{7,31},{8,0},{9,1... | collective-permute-start | bytes 638984 | tf_op jit(solution)/shard_map/ppermute | solution.py:23
  45.9 5.3 %copy-start.3 = (bf16[8,208,128]{2,1,0:T(8,128)(2,1)S(1)}, bf16[8,208,128]{2,1,0:T(8,128)(2,1)}, u32[]{:S(2)}) copy-start(bf16[8,208,128]{2,1,0:T(8,128)(2,1)} %copy-done.2) | copy-start | bytes 1277956
  45.9 1.1 copy-start
  53.9 6.9 %collective-permute-start.8 = (bf16[2,320,128]{2,1,0:T(8,128)(2,1)}, bf16[2,320,128]{2,1,0:T(8,128)(2,1)S(1)}, u32[]{:S(2)}, u32[]{:S(2)}) collective-permute-start(bf16[2,320,128]{2,1,0:T(8,128)(2,1)} %shard_map.61), channel_id=1, source_target_pairs={{0,6},{1,7},{2,0},{3,1},{4,2},{5,3},{6,4},{7,5},{8,14},{9,15},{10,... | collective-permute-start | bytes 491528 | tf_op jit(solution)/shard_map/ppermute | solution.py:23
  56.7 6.0 %collective-permute-start.9 = (bf16[2,320,128]{2,1,0:T(8,128)(2,1)}, bf16[2,320,128]{2,1,0:T(8,128)(2,1)S(1)}, u32[]{:S(2)}, u32[]{:S(2)}) collective-permute-start(bf16[2,320,128]{2,1,0:T(8,128)(2,1)} %shard_map.61), channel_id=1, source_target_pairs={{0,4},{1,5},{2,6},{3,7},{4,0},{5,1},{6,2},{7,3},{8,12},{9,13},{10,... | collective-permute-start | bytes 491528 | tf_op jit(solution)/shard_map/ppermute | solution.py:23
  57.0 12.4 %collective-permute-start.10 = (bf16[2,320,128]{2,1,0:T(8,128)(2,1)}, bf16[2,320,128]{2,1,0:T(8,128)(2,1)S(1)}, u32[]{:S(2)}, u32[]{:S(2)}) collective-permute-start(bf16[2,320,128]{2,1,0:T(8,128)(2,1)} %shard_map.61), channel_id=1, source_target_pairs={{0,2},{1,3},{2,4},{3,5},{4,6},{5,7},{6,0},{7,1},{8,10},{9,11},{10,... | collective-permute-start | bytes 491528 | tf_op jit(solution)/shard_map/ppermute | solution.py:23
  57.7 12.7 %collective-permute-start.11 = (bf16[2,320,128]{2,1,0:T(8,128)(2,1)}, bf16[2,320,128]{2,1,0:T(8,128)(2,1)S(1)}, u32[]{:S(2)}, u32[]{:S(2)}) collective-permute-start(bf16[2,320,128]{2,1,0:T(8,128)(2,1)} %shard_map.61), channel_id=1, source_target_pairs={{0,192},{1,193},{2,224},{3,225},{4,0},{5,1},{6,32},{7,33},{8,208},... | collective-permute-start | bytes 491528 | tf_op jit(solution)/shard_map/ppermute | solution.py:23
  70.4 18.2 %collective-permute-start.13 = (bf16[4,2,320,128]{3,2,1,0:T(8,128)(2,1)S(1)}, bf16[4,2,320,128]{3,2,1,0:T(8,128)(2,1)S(1)}, u32[]{:S(2)}, u32[]{:S(2)}) collective-permute-start(bf16[4,2,320,128]{3,2,1,0:T(8,128)(2,1)S(1)} %pad_maximum_fusion.1.refs_0_), channel_id=1, source_target_pairs={{0,8},{1,9},{2,10},{3,11},{4,12},{5,13},{6,14},{7,15},{8,16},{9,17... | collective-permute-start | bytes 1966088 | tf_op jit(solution)/shard_map/ppermute | solution.py:23
  70.5 19.8 %collective-permute-start.12 = (bf16[4,2,320,128]{3,2,1,0:T(8,128)(2,1)S(1)}, bf16[4,2,320,128]{3,2,1,0:T(8,128)(2,1)S(1)}, u32[]{:S(2)}, u32[]{:S(2)}) collective-permute-start(bf16[4,2,320,128]{3,2,1,0:T(8,128)(2,1)S(1)} %pad_maximum_fusion.1.refs_0_), channel_id=1, source_target_pairs={{0,24},{1,25},{2,26},{3,27},{4,28},{5,29},{6,30},{7,31},{8,0},{9,1... | collective-permute-start | bytes 1966088 | tf_op jit(solution)/shard_map/ppermute | solution.py:23
  74.0 5.7 %collective-permute-start.19 = (bf16[2,320,128]{2,1,0:T(8,128)(2,1)S(1)}, bf16[2,320,128]{2,1,0:T(8,128)(2,1)S(1)}, u32[]{:S(2)}, u32[]{:S(2)}) collective-permute-start(bf16[2,320,128]{2,1,0:T(8,128)(2,1)S(1)} %collective-permute-done.11.refs_4_), channel_id=1, source_target_pairs={{0,32},{1,33},{2,34},{3,35},{4,36},{5,37},{6,38},{7,39},{8,40},{9,... | collective-permute-start | bytes 491528 | tf_op jit(solution)/shard_map/ppermute | solution.py:23
  74.0 6.4 %collective-permute-start.16 = (bf16[2,320,128]{2,1,0:T(8,128)(2,1)S(1)}, bf16[2,320,128]{2,1,0:T(8,128)(2,1)S(1)}, u32[]{:S(2)}, u32[]{:S(2)}) collective-permute-start(bf16[2,320,128]{2,1,0:T(8,128)(2,1)S(1)} %collective-permute-done.11.refs_4_), channel_id=1, source_target_pairs={{0,224},{1,225},{2,226},{3,227},{4,228},{5,229},{6,230},{7,231},{8... | collective-permute-start | bytes 491528 | tf_op jit(solution)/shard_map/ppermute | solution.py:23
  76.7 0.7 copy-start.5
  79.7 5.7 %collective-permute-start.20 = (bf16[2,320,128]{2,1,0:T(8,128)(2,1)S(1)}, bf16[2,320,128]{2,1,0:T(8,128)(2,1)}, u32[]{:S(2)}, u32[]{:S(2)}) collective-permute-start(bf16[2,320,128]{2,1,0:T(8,128)(2,1)S(1)} %collective-permute-done.19.refs_11_), channel_id=1, source_target_pairs={{0,32},{1,33},{2,34},{3,35},{4,36},{5,37},{6,38},{7,39},{8,40},{9,... | collective-permute-start | bytes 491528 | tf_op jit(solution)/shard_map/ppermute | solution.py:23
  79.7 0.7 copy-start.7
  80.4 5.0 %collective-permute-start.17 = (bf16[2,320,128]{2,1,0:T(8,128)(2,1)S(1)}, bf16[2,320,128]{2,1,0:T(8,128)(2,1)}, u32[]{:S(2)}, u32[]{:S(2)}) collective-permute-start(bf16[2,320,128]{2,1,0:T(8,128)(2,1)S(1)} %collective-permute-done.16.refs_5_), channel_id=1, source_target_pairs={{0,224},{1,225},{2,226},{3,227},{4,228},{5,229},{6,230},{7,231},{8... | collective-permute-start | bytes 491528 | tf_op jit(solution)/shard_map/ppermute | solution.py:23
  83.1 0.7 copy-start.9
  85.4 7.4 %collective-permute-start.21 = (bf16[2,320,128]{2,1,0:T(8,128)(2,1)}, bf16[2,320,128]{2,1,0:T(8,128)(2,1)S(1)}, u32[]{:S(2)}, u32[]{:S(2)}) collective-permute-start(bf16[2,320,128]{2,1,0:T(8,128)(2,1)} %collective-permute-done.20.refs_10_), channel_id=1, source_target_pairs={{0,32},{1,33},{2,34},{3,35},{4,36},{5,37},{6,38},{7,39},{8,40},{9,... | collective-permute-start | bytes 491528 | tf_op jit(solution)/shard_map/ppermute | solution.py:23
  85.4 7.5 %collective-permute-start.18 = (bf16[2,320,128]{2,1,0:T(8,128)(2,1)}, bf16[2,320,128]{2,1,0:T(8,128)(2,1)}, u32[]{:S(2)}, u32[]{:S(2)}) collective-permute-start(bf16[2,320,128]{2,1,0:T(8,128)(2,1)} %collective-permute-done.17.refs_6_), channel_id=1, source_target_pairs={{0,224},{1,225},{2,226},{3,227},{4,228},{5,229},{6,230},{7,231},{8... | collective-permute-start | bytes 491528 | tf_op jit(solution)/shard_map/ppermute | solution.py:23
  89.3 8.6 %collective-permute-start.14 = (bf16[2,2,320,128]{3,2,1,0:T(8,128)(2,1)}, bf16[2,2,320,128]{3,2,1,0:T(8,128)(2,1)}, u32[]{:S(2)}, u32[]{:S(2)}) collective-permute-start(bf16[2,2,320,128]{3,2,1,0:T(8,128)(2,1)} %slice.43), channel_id=1, source_target_pairs={{0,8},{1,9},{2,10},{3,11},{4,12},{5,13},{6,14},{7,15},{8,16},{9,17... | collective-permute-start | bytes 983048 | tf_op jit(solution)/shard_map/ppermute | solution.py:23
  91.0 6.9 %collective-permute-start.15 = (bf16[2,2,320,128]{3,2,1,0:T(8,128)(2,1)}, bf16[2,2,320,128]{3,2,1,0:T(8,128)(2,1)}, u32[]{:S(2)}, u32[]{:S(2)}) collective-permute-start(bf16[2,2,320,128]{3,2,1,0:T(8,128)(2,1)} %slice.44), channel_id=1, source_target_pairs={{0,24},{1,25},{2,26},{3,27},{4,28},{5,29},{6,30},{7,31},{8,0},{9,1... | collective-permute-start | bytes 983048 | tf_op jit(solution)/shard_map/ppermute | solution.py:23
  92.7 6.3 %copy-start.6 = (bf16[2,320,128]{2,1,0:T(8,128)(2,1)S(1)}, bf16[2,320,128]{2,1,0:T(8,128)(2,1)}, u32[]{:S(2)}) copy-start(bf16[2,320,128]{2,1,0:T(8,128)(2,1)} %copy-done.5) | copy-start | bytes 491524
  92.7 6.3 %copy-start.8 = (bf16[2,320,128]{2,1,0:T(8,128)(2,1)S(1)}, bf16[2,320,128]{2,1,0:T(8,128)(2,1)}, u32[]{:S(2)}) copy-start(bf16[2,320,128]{2,1,0:T(8,128)(2,1)} %copy-done.7) | copy-start | bytes 491524
  92.8 6.4 %copy-start.10 = (bf16[2,320,128]{2,1,0:T(8,128)(2,1)S(1)}, bf16[2,320,128]{2,1,0:T(8,128)(2,1)}, u32[]{:S(2)}) copy-start(bf16[2,320,128]{2,1,0:T(8,128)(2,1)} %copy-done.9) | copy-start | bytes 491524
  92.8 4.6 %collective-permute-start.22 = (bf16[2,160,128]{2,1,0:T(8,128)(2,1)S(1)}, bf16[2,160,128]{2,1,0:T(8,128)(2,1)S(1)}, u32[]{:S(2)}, u32[]{:S(2)}) collective-permute-start(bf16[2,160,128]{2,1,0:T(8,128)(2,1)S(1)} %slice.45), channel_id=1, source_target_pairs={{0,32},{1,33},{2,34},{3,35},{4,36},{5,37},{6,38},{7,39},{8,40},{9,... | collective-permute-start | bytes 245768 | tf_op jit(solution)/shard_map/ppermute | solution.py:23
  93.9 4.0 %collective-permute-start.23 = (bf16[2,160,128]{2,1,0:T(8,128)(2,1)S(1)}, bf16[2,160,128]{2,1,0:T(8,128)(2,1)S(1)}, u32[]{:S(2)}, u32[]{:S(2)}) collective-permute-start(bf16[2,160,128]{2,1,0:T(8,128)(2,1)S(1)} %slice.46), channel_id=1, source_target_pairs={{0,224},{1,225},{2,226},{3,227},{4,228},{5,229},{6,230},{7,231},{8... | collective-permute-start | bytes 245768 | tf_op jit(solution)/shard_map/ppermute | solution.py:23
  99.1 8.9 %copy-start.1 = (bf16[4,4,320,128]{3,2,1,0:T(8,128)(2,1)S(1)}, bf16[4,4,320,128]{3,2,1,0:T(8,128)(2,1)}, u32[]{:S(2)}) copy-start(bf16[4,4,320,128]{3,2,1,0:T(8,128)(2,1)} %copy-done) | copy-start | bytes 3932164
  102.1 8.2 %collective-permute-start.24 = (f32[4,256,256]{2,1,0:T(8,128)S(1)}, f32[4,256,256]{2,1,0:T(8,128)S(1)}, u32[]{:S(2)}, u32[]{:S(2)}) collective-permute-start(f32[4,256,256]{2,1,0:T(8,128)S(1)} %get-tuple-element.24), channel_id=1, source_target_pairs={{0,1},{1,0},{2,3},{3,2},{4,5},{5,4},{6,7},{7,6},{8,9},{9,8},{10,11... | collective-permute-start | bytes 3145736 | tf_op jit(solution)/shard_map/ppermute | solution.py:23
  110.6 6.0 %collective-permute-start.27 = (bf16[256,256]{1,0:T(8,128)(2,1)S(1)}, bf16[256,256]{1,0:T(8,128)(2,1)S(1)}, u32[]{:S(2)}, u32[]{:S(2)}) collective-permute-start(bf16[256,256]{1,0:T(8,128)(2,1)S(1)} %get-tuple-element.29), channel_id=1, source_target_pairs={{0,8},{1,9},{2,10},{3,11},{4,12},{5,13},{6,14},{7,15},{8,16},{9,17... | collective-permute-start | bytes 393224 | tf_op jit(solution)/shard_map/ppermute | solution.py:23
  110.7 7.7 %collective-permute-start.26 = (bf16[256,256]{1,0:T(8,128)(2,1)S(1)}, bf16[256,256]{1,0:T(8,128)(2,1)S(1)}, u32[]{:S(2)}, u32[]{:S(2)}) collective-permute-start(bf16[256,256]{1,0:T(8,128)(2,1)S(1)} %get-tuple-element.30), channel_id=1, source_target_pairs={{0,24},{1,25},{2,26},{3,27},{4,28},{5,29},{6,30},{7,31},{8,0},{9,1... | collective-permute-start | bytes 393224 | tf_op jit(solution)/shard_map/ppermute | solution.py:23
  113.3 6.8 %collective-permute-start.25 = (bf16[256,256]{1,0:T(8,128)(2,1)S(1)}, bf16[256,256]{1,0:T(8,128)(2,1)S(1)}, u32[]{:S(2)}, u32[]{:S(2)}) collective-permute-start(bf16[256,256]{1,0:T(8,128)(2,1)S(1)} %get-tuple-element.31), channel_id=1, source_target_pairs={{0,16},{1,17},{2,18},{3,19},{4,20},{5,21},{6,22},{7,23},{8,24},{9,... | collective-permute-start | bytes 393224 | tf_op jit(solution)/shard_map/ppermute | solution.py:23

commit v5 on v3

--- a/solution.py
+++ b/solution.py
@@ -290,7 +290,7 @@
     cores = (kept + given.astype(jnp.float32)).astype(half)
     pieces = [cores[0]] + [along_x(cores[step], step) for step in (1, 2, 3)]
     update = apply_cores([0], [pieces[0]], left)
-    for step in (1, 3, 2):
+    for step in (2, 1, 3):
         update = apply_cores([step], [pieces[step]], left, update)
     return jnp.swapaxes(solved, 1, 2), update
 

time: 124 us -> 125 us (level)
  waiting for transfers between devices: 39.6 us -> 41.1 us
    ppermute x28, waiting for transfers between devices: 30.1 us -> 31.6 us  [permute(): return lax.ppermute(value, AXES, pairs)]
  transfers between devices with their start and end apart: 29 -> 29, of which waited for: 13 -> 14; matrix products, arithmetic and copies ran while one was open for 4% -> 4% of each run, Pallas kernels for 6% -> 6%
where the time goes in v5:
time: 125 us; the launch traced here: 124 us
  starting transfers between devices  55 us (44%)
  waiting for transfers between devices  41.1 us (33%)
  Pallas kernels  16.2 us (13%)
  local copies, waits for them, and re-layouts  7.22 us (6%)
  other arithmetic  3.68 us (3%)
    ppermute x28, starting transfers between devices, permute(): return lax.ppermute(value, AXES, pairs)  46 us
    ppermute x28, waiting for transfers between devices, permute(): return lax.ppermute(value, AXES, pairs)  31.6 us
    all_to_all x1, waiting for transfers between devices, local(): planes = lax.all_to_all(sent, 'z', split_axis=0, concat_axis=0, tiled=True)  9.51 us
    all_to_all x1, starting transfers between devices, local(): planes = lax.all_to_all(sent, 'z', split_axis=0, concat_axis=0, tiled=True)  9.03 us
    pallas_call x4, Pallas kernels, apply_cores(): pl.pallas_call(functools.partial(apply_kernel, count), out_shape=jax.Shap...  7.12 us
    pallas_call x3, Pallas kernels, local_call(): pl.pallas_call(kernel, out_shape=outs, in_specs=[SMEM] + [VMEM] * (len(op...  5.23 us
    unnamed x28, local copies, waits for them, and re-layouts  3.1 us
    pallas_call x1, Pallas kernels, partial_cores(): pl.pallas_call(partial_kernel, out_shape=[jax.ShapeDtypeStruct((4, wide,...  2.86 us
  transfers between devices with their start and end apart: 29, of which 14 were waited for; matrix products, arithmetic and copies ran while one was open for 4% of the time, Pallas kernels for 6%

profile of v5, /device:TPU:1, one launch (start us, length us, event | category | flops | bytes accessed | tf_op | source)
XLA Modules:
  0.0 124.3 jit_solution(14803592327883026809)
XLA Ops:
  0.7 0.9 copy-done.6
  1.6 1.5 %shard_map.59 = bf16[8,208,128]{2,1,0:T(8,128)(2,1)} custom-call(s32[2]{0:T(128)S(1)} %pad_add_fusion.place, f32[80,320]{1,0:T(8,128)S(1)} %copy-done.6), custom_call_target="tpu_custom_call" | custom-call | bytes 4000000 | tf_op jit(solution)/shard_map/pallas_call | solution.py:158
  3.1 1.0 pad_maximum_fusion.3
  4.1 9.0 %all-to-all-start = ((bf16[8,208,128]{2,1,0:T(8,128)(2,1)}), bf16[8,208,128]{2,1,0:T(8,128)(2,1)S(1)}, u32[]{:S(2)}, u32[]{:S(2)}) async-start(bf16[8,208,128]{2,1,0:T(8,128)(2,1)} %shard_map.59), calls=%async_computation | async-start | bytes 851968 | tf_op jit(solution)/shard_map/all_to_all | solution.py:258
  13.2 2.9 %collective-permute-start.3 = (bf16[4,320,128]{2,1,0:T(8,128)(2,1)S(1)}, bf16[4,320,128]{2,1,0:T(8,128)(2,1)S(1)}, u32[]{:S(2)}, u32[]{:S(2)}) collective-permute-start(bf16[4,320,128]{2,1,0:T(8,128)(2,1)S(1)} %pad_maximum_fusion.3), channel_id=1, source_target_pairs={{0,4},{1,5},{2,6},{3,7},{4,0},{5,1},{6,2},{7,3},{8,12},{9,13},{10,... | collective-permute-start | bytes 983048 | tf_op jit(solution)/shard_map/ppermute | solution.py:23
  16.1 0.4 collective-permute-start.4
  16.5 2.3 %collective-permute-start.2 = (bf16[4,320,128]{2,1,0:T(8,128)(2,1)S(1)}, bf16[4,320,128]{2,1,0:T(8,128)(2,1)S(1)}, u32[]{:S(2)}, u32[]{:S(2)}) collective-permute-start(bf16[4,320,128]{2,1,0:T(8,128)(2,1)S(1)} %pad_maximum_fusion.3), channel_id=1, source_target_pairs={{0,6},{1,7},{2,0},{3,1},{4,2},{5,3},{6,4},{7,5},{8,14},{9,15},{10,... | collective-permute-start | bytes 983048 | tf_op jit(solution)/shard_map/ppermute | solution.py:23
  18.7 9.5 %all-to-all-done.here = bf16[8,208,128]{2,1,0:T(8,128)(2,1)S(1)} async-done(((bf16[8,208,128]{2,1,0:T(8,128)(2,1)}), bf16[8,208,128]{2,1,0:T(8,128)(2,1)S(1)}, u32[]{:S(2)}, u32[]{:S(2)}) %all-to-all-start) | async-done | bytes 426016 | tf_op jit(solution)/shard_map/all_to_all | solution.py:258
  28.3 1.2 collective-permute-start
  29.5 1.5 %collective-permute-start.1 = (bf16[8,208,128]{2,1,0:T(8,128)(2,1)S(1)}, bf16[8,208,128]{2,1,0:T(8,128)(2,1)S(1)}, u32[]{:S(2)}, u32[]{:S(2)}) collective-permute-start(bf16[8,208,128]{2,1,0:T(8,128)(2,1)S(1)} %all-to-all-done.here), channel_id=1, source_target_pairs={{0,24},{1,25},{2,26},{3,27},{4,28},{5,29},{6,30},{7,31},{8,0},{9,1... | collective-permute-start | bytes 1277960 | tf_op jit(solution)/shard_map/ppermute | solution.py:23
  30.9 0.4 collective-permute-done.4
  31.3 0.2 pad_maximum_fusion.own
  31.5 8.0 %collective-permute-done.below = bf16[8,208,128]{2,1,0:T(8,128)(2,1)S(1)} collective-permute-done((bf16[8,208,128]{2,1,0:T(8,128)(2,1)S(1)}, bf16[8,208,128]{2,1,0:T(8,128)(2,1)S(1)}, u32[]{:S(2)}, u32[]{:S(2)}) %collective-permute-start) | collective-permute-done | bytes 426016 | tf_op jit(solution)/shard_map/ppermute | solution.py:23
  39.5 2.2 %collective-permute-start.5 = (bf16[4,4,320,128]{3,2,1,0:T(8,128)(2,1)S(1)}, bf16[4,4,320,128]{3,2,1,0:T(8,128)(2,1)S(1)}, u32[]{:S(2)}, u32[]{:S(2)}) collective-permute-start(bf16[4,4,320,128]{3,2,1,0:T(8,128)(2,1)S(1)} %pad_maximum_fusion.own), channel_id=1, source_target_pairs={{0,1},{1,0},{2,3},{3,2},{4,5},{5,4},{6,7},{7,6},{8,9},{9,8},{10,11... | collective-permute-start | bytes 3932168 | tf_op jit(solution)/shard_map/ppermute | solution.py:23
  41.7 0.7 slice.33
  42.4 1.2 collective-permute-start.6
  43.6 0.7 slice.34
  44.3 1.5 %collective-permute-start.7 = (bf16[4,208,128]{2,1,0:T(8,128)(2,1)}, bf16[4,208,128]{2,1,0:T(8,128)(2,1)}, u32[]{:S(2)}, u32[]{:S(2)}) collective-permute-start(bf16[4,208,128]{2,1,0:T(8,128)(2,1)} %slice.34), channel_id=1, source_target_pairs={{0,24},{1,25},{2,26},{3,27},{4,28},{5,29},{6,30},{7,31},{8,0},{9,1... | collective-permute-start | bytes 638984 | tf_op jit(solution)/shard_map/ppermute | solution.py:23
  45.9 1.0 shard_map.60
  46.9 3.9 %collective-permute-done.6.first = bf16[4,208,128]{2,1,0:T(8,128)(2,1)} collective-permute-done((bf16[4,208,128]{2,1,0:T(8,128)(2,1)}, bf16[4,208,128]{2,1,0:T(8,128)(2,1)}, u32[]{:S(2)}, u32[]{:S(2)}) %collective-permute-start.6) | collective-permute-done | bytes 213024 | tf_op jit(solution)/shard_map/ppermute | solution.py:23
  50.8 0.4 collective-permute-done.7.second
  51.1 2.8 %shard_map.61 = bf16[2,320,128]{2,1,0:T(8,128)(2,1)} custom-call(s32[6]{0:T(128)S(1)} %stack.78.place, bf16[4,256,640]{2,1,0:T(8,128)(2,1)S(1)} %get-tuple-element.16.full, bf16[256,384]{1,0:T(8,128)(2,1)S(1)} %get-tuple-element.17.mine, bf16[8,208,128]{2,1,0:T(8,128)(2,1)S(1)} %all-to-all-done.here, bf16[8,208,128]{2,1,0:T(8,128)(2,1)S(1)} %copy-done.1, ...), custom_call_target="tpu_custom_call" | custom-call | flops 500000000 | bytes 4000000 | tf_op jit(solution)/shard_map/pallas_call | solution.py:158
  53.9 2.7 %collective-permute-start.8 = (bf16[2,320,128]{2,1,0:T(8,128)(2,1)}, bf16[2,320,128]{2,1,0:T(8,128)(2,1)S(1)}, u32[]{:S(2)}, u32[]{:S(2)}) collective-permute-start(bf16[2,320,128]{2,1,0:T(8,128)(2,1)} %shard_map.61), channel_id=1, source_target_pairs={{0,6},{1,7},{2,0},{3,1},{4,2},{5,3},{6,4},{7,5},{8,14},{9,15},{10,... | collective-permute-start | bytes 491528 | tf_op jit(solution)/shard_map/ppermute | solution.py:23
  56.6 0.3 collective-permute-start.9
  57.0 0.7 collective-permute-start.10
  57.7 1.9 %collective-permute-start.11 = (bf16[2,320,128]{2,1,0:T(8,128)(2,1)}, bf16[2,320,128]{2,1,0:T(8,128)(2,1)S(1)}, u32[]{:S(2)}, u32[]{:S(2)}) collective-permute-start(bf16[2,320,128]{2,1,0:T(8,128)(2,1)} %shard_map.61), channel_id=1, source_target_pairs={{0,192},{1,193},{2,224},{3,225},{4,0},{5,1},{6,32},{7,33},{8,208},... | collective-permute-start | bytes 491528 | tf_op jit(solution)/shard_map/ppermute | solution.py:23
  59.6 1.2 collective-permute-done.8
  60.8 1.8 %collective-permute-done.9 = bf16[2,320,128]{2,1,0:T(8,128)(2,1)S(1)} collective-permute-done((bf16[2,320,128]{2,1,0:T(8,128)(2,1)}, bf16[2,320,128]{2,1,0:T(8,128)(2,1)S(1)}, u32[]{:S(2)}, u32[]{:S(2)}) %collective-permute-start.9) | collective-permute-done | bytes 163872 | tf_op jit(solution)/shard_map/ppermute | solution.py:23
  62.6 6.7 %collective-permute-done.10 = bf16[2,320,128]{2,1,0:T(8,128)(2,1)S(1)} collective-permute-done((bf16[2,320,128]{2,1,0:T(8,128)(2,1)}, bf16[2,320,128]{2,1,0:T(8,128)(2,1)S(1)}, u32[]{:S(2)}, u32[]{:S(2)}) %collective-permute-start.10) | collective-permute-done | bytes 163872 | tf_op jit(solution)/shard_map/ppermute | solution.py:23
  69.3 1.0 pad_maximum_fusion.1.refs_0_
  70.3 0.1 collective-permute-start.13
  70.4 3.6 %collective-permute-start.12 = (bf16[4,2,320,128]{3,2,1,0:T(8,128)(2,1)S(1)}, bf16[4,2,320,128]{3,2,1,0:T(8,128)(2,1)S(1)}, u32[]{:S(2)}, u32[]{:S(2)}) collective-permute-start(bf16[4,2,320,128]{3,2,1,0:T(8,128)(2,1)S(1)} %pad_maximum_fusion.1.refs_0_), channel_id=1, source_target_pairs={{0,24},{1,25},{2,26},{3,27},{4,28},{5,29},{6,30},{7,31},{8,0},{9,1... | collective-permute-start | bytes 1966088 | tf_op jit(solution)/shard_map/ppermute | solution.py:23
  74.0 2.7 %collective-permute-start.16 = (bf16[2,320,128]{2,1,0:T(8,128)(2,1)S(1)}, bf16[2,320,128]{2,1,0:T(8,128)(2,1)S(1)}, u32[]{:S(2)}, u32[]{:S(2)}) collective-permute-start(bf16[2,320,128]{2,1,0:T(8,128)(2,1)S(1)} %collective-permute-done.11.refs_4_), channel_id=1, source_target_pairs={{0,224},{1,225},{2,226},{3,227},{4,228},{5,229},{6,230},{7,231},{8... | collective-permute-start | bytes 491528 | tf_op jit(solution)/shard_map/ppermute | solution.py:23
  76.7 0.7 copy-done.7
  77.3 2.3 %collective-permute-done.19.refs_11_ = bf16[2,320,128]{2,1,0:T(8,128)(2,1)S(1)} collective-permute-done((bf16[2,320,128]{2,1,0:T(8,128)(2,1)S(1)}, bf16[2,320,128]{2,1,0:T(8,128)(2,1)S(1)}, u32[]{:S(2)}, u32[]{:S(2)}) %collective-permute-start.19) | collective-permute-done | bytes 163872 | tf_op jit(solution)/shard_map/ppermute | solution.py:23
  79.7 0.7 copy-done.9
  80.4 2.7 %collective-permute-start.17 = (bf16[2,320,128]{2,1,0:T(8,128)(2,1)S(1)}, bf16[2,320,128]{2,1,0:T(8,128)(2,1)}, u32[]{:S(2)}, u32[]{:S(2)}) collective-permute-start(bf16[2,320,128]{2,1,0:T(8,128)(2,1)S(1)} %collective-permute-done.16.refs_5_), channel_id=1, source_target_pairs={{0,224},{1,225},{2,226},{3,227},{4,228},{5,229},{6,230},{7,231},{8... | collective-permute-start | bytes 491528 | tf_op jit(solution)/shard_map/ppermute | solution.py:23
  83.0 0.7 copy-done.11
  83.7 1.7 %collective-permute-done.20.refs_10_ = bf16[2,320,128]{2,1,0:T(8,128)(2,1)} collective-permute-done((bf16[2,320,128]{2,1,0:T(8,128)(2,1)S(1)}, bf16[2,320,128]{2,1,0:T(8,128)(2,1)}, u32[]{:S(2)}, u32[]{:S(2)}) %collective-permute-start.20) | collective-permute-done | bytes 163872 | tf_op jit(solution)/shard_map/ppermute | solution.py:23
  85.4 3.2 %collective-permute-start.18 = (bf16[2,320,128]{2,1,0:T(8,128)(2,1)}, bf16[2,320,128]{2,1,0:T(8,128)(2,1)}, u32[]{:S(2)}, u32[]{:S(2)}) collective-permute-start(bf16[2,320,128]{2,1,0:T(8,128)(2,1)} %collective-permute-done.17.refs_6_), channel_id=1, source_target_pairs={{0,224},{1,225},{2,226},{3,227},{4,228},{5,229},{6,230},{7,231},{8... | collective-permute-start | bytes 491528 | tf_op jit(solution)/shard_map/ppermute | solution.py:23
  88.5 0.8 slice.43
  89.3 0.9 collective-permute-start.14
  90.2 0.8 slice.44
  91.0 0.2 copy-done.4
  91.2 1.8 %collective-permute-start.15 = (bf16[2,2,320,128]{3,2,1,0:T(8,128)(2,1)}, bf16[2,2,320,128]{3,2,1,0:T(8,128)(2,1)}, u32[]{:S(2)}, u32[]{:S(2)}) collective-permute-start(bf16[2,2,320,128]{3,2,1,0:T(8,128)(2,1)} %slice.44), channel_id=1, source_target_pairs={{0,24},{1,25},{2,26},{3,27},{4,28},{5,29},{6,30},{7,31},{8,0},{9,1... | collective-permute-start | bytes 983048 | tf_op jit(solution)/shard_map/ppermute | solution.py:23
  93.0 0.1 collective-permute-start.22
  93.1 1.0 slice.46
  94.1 2.5 %collective-permute-start.23 = (bf16[2,160,128]{2,1,0:T(8,128)(2,1)S(1)}, bf16[2,160,128]{2,1,0:T(8,128)(2,1)S(1)}, u32[]{:S(2)}, u32[]{:S(2)}) collective-permute-start(bf16[2,160,128]{2,1,0:T(8,128)(2,1)S(1)} %slice.46), channel_id=1, source_target_pairs={{0,224},{1,225},{2,226},{3,227},{4,228},{5,229},{6,230},{7,231},{8... | collective-permute-start | bytes 245768 | tf_op jit(solution)/shard_map/ppermute | solution.py:23
  96.7 0.9 collective-permute-done.22
  97.6 0.6 collective-permute-done.23
  98.2 1.1 pad_maximum_fusion.2.refs_2_
  99.4 2.9 %shard_map.63 = (f32[4,256,256]{2,1,0:T(8,128)S(1)}, f32[4,256,256]{2,1,0:T(8,128)S(1)}) custom-call(s32[3]{0:T(128)S(1)} %pad_add_fusion.1.place, bf16[4,2,320,128]{3,2,1,0:T(8,128)(2,1)S(1)} %pad_maximum_fusion.1.refs_0_, bf16[4,2,320,128]{3,2,1,0:T(8,128)(2,1)S(1)} %copy-done.5, bf16[4,2,320,128]{3,2,1,0:T(8,128)(2,1)S(1)} %pad_maximum_fusion.2.refs_2_, ...), custom_call_target="tpu_custom_call" | custom-call | flops 1400000000 | bytes 6000000 | tf_op jit(solution)/shard_map/pallas_call | solution.py:98
  102.2 6.0 %collective-permute-start.24 = (f32[4,256,256]{2,1,0:T(8,128)S(1)}, f32[4,256,256]{2,1,0:T(8,128)S(1)}, u32[]{:S(2)}, u32[]{:S(2)}) collective-permute-start(f32[4,256,256]{2,1,0:T(8,128)S(1)} %get-tuple-element.23), channel_id=1, source_target_pairs={{0,1},{1,0},{2,3},{3,2},{4,5},{5,4},{6,7},{7,6},{8,9},{9,8},{10,11... | collective-permute-start | bytes 3145736 | tf_op jit(solution)/shard_map/ppermute | solution.py:23
  108.2 2.3 %collective-permute-done.24 = f32[4,256,256]{2,1,0:T(8,128)S(1)} collective-permute-done((f32[4,256,256]{2,1,0:T(8,128)S(1)}, f32[4,256,256]{2,1,0:T(8,128)S(1)}, u32[]{:S(2)}, u32[]{:S(2)}) %collective-permute-start.24) | collective-permute-done | bytes 1048608 | tf_op jit(solution)/shard_map/ppermute | solution.py:23
  110.5 0.2 add_convert_fusion
  110.7 1.1 collective-permute-start.27
  111.8 1.5 %collective-permute-start.26 = (bf16[256,256]{1,0:T(8,128)(2,1)S(1)}, bf16[256,256]{1,0:T(8,128)(2,1)S(1)}, u32[]{:S(2)}, u32[]{:S(2)}) collective-permute-start(bf16[256,256]{1,0:T(8,128)(2,1)S(1)} %get-tuple-element.26), channel_id=1, source_target_pairs={{0,8},{1,9},{2,10},{3,11},{4,12},{5,13},{6,14},{7,15},{8,16},{9,17... | collective-permute-start | bytes 393224 | tf_op jit(solution)/shard_map/ppermute | solution.py:23
  113.4 1.1 collective-permute-start.25
  114.5 1.0 shard_map.62.left
  115.5 1.8 %shard_map.64.refs_1_ = bf16[2,1,8,128,2560]{4,3,2,1,0:T(8,128)(2,1)} custom-call(s32[1]{0:T(128)} %bitcast.24.place, bf16[2,128,2560]{2,1,0:T(8,128)(2,1)S(1)} %shard_map.62.left, bf16[256,256]{1,0:T(8,128)(2,1)S(1)} %get-tuple-element.24.refs_0_), custom_call_target="tpu_custom_call" | custom-call | flops 350000000 | bytes 4000000 | tf_op jit(solution)/shard_map/pallas_call | solution.py:140
  117.3 1.8 %shard_map.65.refs_1_ = bf16[2,1,8,128,2560]{4,3,2,1,0:T(8,128)(2,1)} custom-call(s32[1]{0:T(128)} %bitcast.22.place, bf16[2,128,2560]{2,1,0:T(8,128)(2,1)S(1)} %shard_map.62.left, bf16[256,256]{1,0:T(8,128)(2,1)S(1)} %collective-permute-done.27.refs_0_, bf16[2,1,8,128,2560]{4,3,2,1,0:T(8,128)(2,1)} %shard_map.64.refs_1_), custom_call_target="tpu_custom_call", output_to_operand_aliasing={{}: (3, {})} | custom-call | flops 350000000 | bytes 4000000 | tf_op jit(solution)/shard_map/pallas_call | solution.py:140
  119.1 1.5 %collective-permute-done.26.refs_0_ = bf16[256,256]{1,0:T(8,128)(2,1)S(1)} collective-permute-done((bf16[256,256]{1,0:T(8,128)(2,1)S(1)}, bf16[256,256]{1,0:T(8,128)(2,1)S(1)}, u32[]{:S(2)}, u32[]{:S(2)}) %collective-permute-start.26) | collective-permute-done | bytes 131104 | tf_op jit(solution)/shard_map/ppermute | solution.py:23
  120.6 1.8 %shard_map.66.refs_1_ = bf16[2,1,8,128,2560]{4,3,2,1,0:T(8,128)(2,1)} custom-call(s32[1]{0:T(128)} %bitcast.20.place, bf16[2,128,2560]{2,1,0:T(8,128)(2,1)S(1)} %shard_map.62.left, bf16[256,256]{1,0:T(8,128)(2,1)S(1)} %collective-permute-done.26.refs_0_, bf16[2,1,8,128,2560]{4,3,2,1,0:T(8,128)(2,1)} %shard_map.65.refs_1_), custom_call_target="tpu_custom_call", output_to_operand_aliasing={{}: (3, {})} | custom-call | flops 350000000 | bytes 4000000 | tf_op jit(solution)/shard_map/pallas_call | solution.py:140
  122.4 1.8 %shard_map.67 = bf16[2,1,8,128,2560]{4,3,2,1,0:T(8,128)(2,1)} custom-call(s32[1]{0:T(128)} %bitcast.13.place, bf16[2,128,2560]{2,1,0:T(8,128)(2,1)S(1)} %shard_map.62.left, bf16[256,256]{1,0:T(8,128)(2,1)S(1)} %collective-permute-done.25.refs_0_, bf16[2,1,8,128,2560]{4,3,2,1,0:T(8,128)(2,1)} %shard_map.66.refs_1_), custom_call_target="tpu_custom_call", output_to_operand_aliasing={{}: (3, {})} | custom-call | flops 350000000 | bytes 4000000 | tf_op jit(solution)/shard_map/pallas_call | solution.py:140
  (47 shorter events, 0.4 us)
Async XLA Ops:
  0.7 0.9 copy-start.6
  4.1 24.1 %all-to-all-start = ((bf16[8,208,128]{2,1,0:T(8,128)(2,1)}), bf16[8,208,128]{2,1,0:T(8,128)(2,1)S(1)}, u32[]{:S(2)}, u32[]{:S(2)}) async-start(bf16[8,208,128]{2,1,0:T(8,128)(2,1)} %shard_map.59), calls=%async_computation | async-start | bytes 851968 | tf_op jit(solution)/shard_map/all_to_all | solution.py:258
  13.2 17.8 %collective-permute-start.3 = (bf16[4,320,128]{2,1,0:T(8,128)(2,1)S(1)}, bf16[4,320,128]{2,1,0:T(8,128)(2,1)S(1)}, u32[]{:S(2)}, u32[]{:S(2)}) collective-permute-start(bf16[4,320,128]{2,1,0:T(8,128)(2,1)S(1)} %pad_maximum_fusion.3), channel_id=1, source_target_pairs={{0,4},{1,5},{2,6},{3,7},{4,0},{5,1},{6,2},{7,3},{8,12},{9,13},{10,... | collective-permute-start | bytes 983048 | tf_op jit(solution)/shard_map/ppermute | solution.py:23
  16.1 15.2 %collective-permute-start.4 = (bf16[4,320,128]{2,1,0:T(8,128)(2,1)S(1)}, bf16[4,320,128]{2,1,0:T(8,128)(2,1)S(1)}, u32[]{:S(2)}, u32[]{:S(2)}) collective-permute-start(bf16[4,320,128]{2,1,0:T(8,128)(2,1)S(1)} %pad_maximum_fusion.3), channel_id=1, source_target_pairs={{0,2},{1,3},{2,4},{3,5},{4,6},{5,7},{6,0},{7,1},{8,10},{9,11},{10,... | collective-permute-start | bytes 983048 | tf_op jit(solution)/shard_map/ppermute | solution.py:23
  16.5 14.8 %collective-permute-start.2 = (bf16[4,320,128]{2,1,0:T(8,128)(2,1)S(1)}, bf16[4,320,128]{2,1,0:T(8,128)(2,1)S(1)}, u32[]{:S(2)}, u32[]{:S(2)}) collective-permute-start(bf16[4,320,128]{2,1,0:T(8,128)(2,1)S(1)} %pad_maximum_fusion.3), channel_id=1, source_target_pairs={{0,6},{1,7},{2,0},{3,1},{4,2},{5,3},{6,4},{7,5},{8,14},{9,15},{10,... | collective-permute-start | bytes 983048 | tf_op jit(solution)/shard_map/ppermute | solution.py:23
  28.3 11.3 %collective-permute-start = (bf16[8,208,128]{2,1,0:T(8,128)(2,1)S(1)}, bf16[8,208,128]{2,1,0:T(8,128)(2,1)S(1)}, u32[]{:S(2)}, u32[]{:S(2)}) collective-permute-start(bf16[8,208,128]{2,1,0:T(8,128)(2,1)S(1)} %all-to-all-done.here), channel_id=1, source_target_pairs={{0,8},{1,9},{2,10},{3,11},{4,12},{5,13},{6,14},{7,15},{8,16},{9,17... | collective-permute-start | bytes 1277960 | tf_op jit(solution)/shard_map/ppermute | solution.py:23
  29.5 10.1 %collective-permute-start.1 = (bf16[8,208,128]{2,1,0:T(8,128)(2,1)S(1)}, bf16[8,208,128]{2,1,0:T(8,128)(2,1)S(1)}, u32[]{:S(2)}, u32[]{:S(2)}) collective-permute-start(bf16[8,208,128]{2,1,0:T(8,128)(2,1)S(1)} %all-to-all-done.here), channel_id=1, source_target_pairs={{0,24},{1,25},{2,26},{3,27},{4,28},{5,29},{6,30},{7,31},{8,0},{9,1... | collective-permute-start | bytes 1277960 | tf_op jit(solution)/shard_map/ppermute | solution.py:23
  31.3 14.5 %copy-start.13 = (s32[2]{0:T(128)S(1)}, s32[2]{0:T(128)}, u32[]{:S(2)}) copy-start(s32[2]{0:T(128)} %param.6) | copy-start | bytes 28
  39.5 4.1 %copy-start = (bf16[8,208,128]{2,1,0:T(8,128)(2,1)}, bf16[8,208,128]{2,1,0:T(8,128)(2,1)S(1)}, u32[]{:S(2)}) copy-start(bf16[8,208,128]{2,1,0:T(8,128)(2,1)S(1)} %collective-permute-done.1.above) | copy-start | bytes 1277956
  39.5 6.3 %collective-permute-start.5 = (bf16[4,4,320,128]{3,2,1,0:T(8,128)(2,1)S(1)}, bf16[4,4,320,128]{3,2,1,0:T(8,128)(2,1)S(1)}, u32[]{:S(2)}, u32[]{:S(2)}) collective-permute-start(bf16[4,4,320,128]{3,2,1,0:T(8,128)(2,1)S(1)} %pad_maximum_fusion.own), channel_id=1, source_target_pairs={{0,1},{1,0},{2,3},{3,2},{4,5},{5,4},{6,7},{7,6},{8,9},{9,8},{10,11... | collective-permute-start | bytes 3932168 | tf_op jit(solution)/shard_map/ppermute | solution.py:23
  42.4 8.4 %collective-permute-start.6 = (bf16[4,208,128]{2,1,0:T(8,128)(2,1)}, bf16[4,208,128]{2,1,0:T(8,128)(2,1)}, u32[]{:S(2)}, u32[]{:S(2)}) collective-permute-start(bf16[4,208,128]{2,1,0:T(8,128)(2,1)} %slice.33), channel_id=1, source_target_pairs={{0,8},{1,9},{2,10},{3,11},{4,12},{5,13},{6,14},{7,15},{8,16},{9,17... | collective-permute-start | bytes 638984 | tf_op jit(solution)/shard_map/ppermute | solution.py:23
  44.3 6.8 %collective-permute-start.7 = (bf16[4,208,128]{2,1,0:T(8,128)(2,1)}, bf16[4,208,128]{2,1,0:T(8,128)(2,1)}, u32[]{:S(2)}, u32[]{:S(2)}) collective-permute-start(bf16[4,208,128]{2,1,0:T(8,128)(2,1)} %slice.34), channel_id=1, source_target_pairs={{0,24},{1,25},{2,26},{3,27},{4,28},{5,29},{6,30},{7,31},{8,0},{9,1... | collective-permute-start | bytes 638984 | tf_op jit(solution)/shard_map/ppermute | solution.py:23
  45.9 5.3 %copy-start.1 = (bf16[8,208,128]{2,1,0:T(8,128)(2,1)S(1)}, bf16[8,208,128]{2,1,0:T(8,128)(2,1)}, u32[]{:S(2)}) copy-start(bf16[8,208,128]{2,1,0:T(8,128)(2,1)} %copy-done) | copy-start | bytes 1277956
  53.9 6.9 %collective-permute-start.8 = (bf16[2,320,128]{2,1,0:T(8,128)(2,1)}, bf16[2,320,128]{2,1,0:T(8,128)(2,1)S(1)}, u32[]{:S(2)}, u32[]{:S(2)}) collective-permute-start(bf16[2,320,128]{2,1,0:T(8,128)(2,1)} %shard_map.61), channel_id=1, source_target_pairs={{0,6},{1,7},{2,0},{3,1},{4,2},{5,3},{6,4},{7,5},{8,14},{9,15},{10,... | collective-permute-start | bytes 491528 | tf_op jit(solution)/shard_map/ppermute | solution.py:23
  56.6 6.0 %collective-permute-start.9 = (bf16[2,320,128]{2,1,0:T(8,128)(2,1)}, bf16[2,320,128]{2,1,0:T(8,128)(2,1)S(1)}, u32[]{:S(2)}, u32[]{:S(2)}) collective-permute-start(bf16[2,320,128]{2,1,0:T(8,128)(2,1)} %shard_map.61), channel_id=1, source_target_pairs={{0,4},{1,5},{2,6},{3,7},{4,0},{5,1},{6,2},{7,3},{8,12},{9,13},{10,... | collective-permute-start | bytes 491528 | tf_op jit(solution)/shard_map/ppermute | solution.py:23
  57.0 12.3 %collective-permute-start.10 = (bf16[2,320,128]{2,1,0:T(8,128)(2,1)}, bf16[2,320,128]{2,1,0:T(8,128)(2,1)S(1)}, u32[]{:S(2)}, u32[]{:S(2)}) collective-permute-start(bf16[2,320,128]{2,1,0:T(8,128)(2,1)} %shard_map.61), channel_id=1, source_target_pairs={{0,2},{1,3},{2,4},{3,5},{4,6},{5,7},{6,0},{7,1},{8,10},{9,11},{10,... | collective-permute-start | bytes 491528 | tf_op jit(solution)/shard_map/ppermute | solution.py:23
  57.7 12.6 %collective-permute-start.11 = (bf16[2,320,128]{2,1,0:T(8,128)(2,1)}, bf16[2,320,128]{2,1,0:T(8,128)(2,1)S(1)}, u32[]{:S(2)}, u32[]{:S(2)}) collective-permute-start(bf16[2,320,128]{2,1,0:T(8,128)(2,1)} %shard_map.61), channel_id=1, source_target_pairs={{0,192},{1,193},{2,224},{3,225},{4,0},{5,1},{6,32},{7,33},{8,208},... | collective-permute-start | bytes 491528 | tf_op jit(solution)/shard_map/ppermute | solution.py:23
  70.3 18.2 %collective-permute-start.13 = (bf16[4,2,320,128]{3,2,1,0:T(8,128)(2,1)S(1)}, bf16[4,2,320,128]{3,2,1,0:T(8,128)(2,1)S(1)}, u32[]{:S(2)}, u32[]{:S(2)}) collective-permute-start(bf16[4,2,320,128]{3,2,1,0:T(8,128)(2,1)S(1)} %pad_maximum_fusion.1.refs_0_), channel_id=1, source_target_pairs={{0,8},{1,9},{2,10},{3,11},{4,12},{5,13},{6,14},{7,15},{8,16},{9,17... | collective-permute-start | bytes 1966088 | tf_op jit(solution)/shard_map/ppermute | solution.py:23
  70.4 19.8 %collective-permute-start.12 = (bf16[4,2,320,128]{3,2,1,0:T(8,128)(2,1)S(1)}, bf16[4,2,320,128]{3,2,1,0:T(8,128)(2,1)S(1)}, u32[]{:S(2)}, u32[]{:S(2)}) collective-permute-start(bf16[4,2,320,128]{3,2,1,0:T(8,128)(2,1)S(1)} %pad_maximum_fusion.1.refs_0_), channel_id=1, source_target_pairs={{0,24},{1,25},{2,26},{3,27},{4,28},{5,29},{6,30},{7,31},{8,0},{9,1... | collective-permute-start | bytes 1966088 | tf_op jit(solution)/shard_map/ppermute | solution.py:23
  74.0 5.7 %collective-permute-start.19 = (bf16[2,320,128]{2,1,0:T(8,128)(2,1)S(1)}, bf16[2,320,128]{2,1,0:T(8,128)(2,1)S(1)}, u32[]{:S(2)}, u32[]{:S(2)}) collective-permute-start(bf16[2,320,128]{2,1,0:T(8,128)(2,1)S(1)} %collective-permute-done.11.refs_4_), channel_id=1, source_target_pairs={{0,32},{1,33},{2,34},{3,35},{4,36},{5,37},{6,38},{7,39},{8,40},{9,... | collective-permute-start | bytes 491528 | tf_op jit(solution)/shard_map/ppermute | solution.py:23
  74.0 6.4 %collective-permute-start.16 = (bf16[2,320,128]{2,1,0:T(8,128)(2,1)S(1)}, bf16[2,320,128]{2,1,0:T(8,128)(2,1)S(1)}, u32[]{:S(2)}, u32[]{:S(2)}) collective-permute-start(bf16[2,320,128]{2,1,0:T(8,128)(2,1)S(1)} %collective-permute-done.11.refs_4_), channel_id=1, source_target_pairs={{0,224},{1,225},{2,226},{3,227},{4,228},{5,229},{6,230},{7,231},{8... | collective-permute-start | bytes 491528 | tf_op jit(solution)/shard_map/ppermute | solution.py:23
  76.7 0.7 copy-start.7
  79.7 5.7 %collective-permute-start.20 = (bf16[2,320,128]{2,1,0:T(8,128)(2,1)S(1)}, bf16[2,320,128]{2,1,0:T(8,128)(2,1)}, u32[]{:S(2)}, u32[]{:S(2)}) collective-permute-start(bf16[2,320,128]{2,1,0:T(8,128)(2,1)S(1)} %collective-permute-done.19.refs_11_), channel_id=1, source_target_pairs={{0,32},{1,33},{2,34},{3,35},{4,36},{5,37},{6,38},{7,39},{8,40},{9,... | collective-permute-start | bytes 491528 | tf_op jit(solution)/shard_map/ppermute | solution.py:23
  79.7 0.7 copy-start.9
  80.4 5.0 %collective-permute-start.17 = (bf16[2,320,128]{2,1,0:T(8,128)(2,1)S(1)}, bf16[2,320,128]{2,1,0:T(8,128)(2,1)}, u32[]{:S(2)}, u32[]{:S(2)}) collective-permute-start(bf16[2,320,128]{2,1,0:T(8,128)(2,1)S(1)} %collective-permute-done.16.refs_5_), channel_id=1, source_target_pairs={{0,224},{1,225},{2,226},{3,227},{4,228},{5,229},{6,230},{7,231},{8... | collective-permute-start | bytes 491528 | tf_op jit(solution)/shard_map/ppermute | solution.py:23
  83.0 0.7 copy-start.11
  85.3 7.6 %collective-permute-start.21 = (bf16[2,320,128]{2,1,0:T(8,128)(2,1)}, bf16[2,320,128]{2,1,0:T(8,128)(2,1)S(1)}, u32[]{:S(2)}, u32[]{:S(2)}) collective-permute-start(bf16[2,320,128]{2,1,0:T(8,128)(2,1)} %collective-permute-done.20.refs_10_), channel_id=1, source_target_pairs={{0,32},{1,33},{2,34},{3,35},{4,36},{5,37},{6,38},{7,39},{8,40},{9,... | collective-permute-start | bytes 491528 | tf_op jit(solution)/shard_map/ppermute | solution.py:23
  85.4 7.8 %collective-permute-start.18 = (bf16[2,320,128]{2,1,0:T(8,128)(2,1)}, bf16[2,320,128]{2,1,0:T(8,128)(2,1)}, u32[]{:S(2)}, u32[]{:S(2)}) collective-permute-start(bf16[2,320,128]{2,1,0:T(8,128)(2,1)} %collective-permute-done.17.refs_6_), channel_id=1, source_target_pairs={{0,224},{1,225},{2,226},{3,227},{4,228},{5,229},{6,230},{7,231},{8... | collective-permute-start | bytes 491528 | tf_op jit(solution)/shard_map/ppermute | solution.py:23
  88.5 1.7 %copy-start.2 = (bf16[4,2,320,128]{3,2,1,0:T(8,128)(2,1)}, bf16[4,2,320,128]{3,2,1,0:T(8,128)(2,1)S(1)}, u32[]{:S(2)}) copy-start(bf16[4,2,320,128]{3,2,1,0:T(8,128)(2,1)S(1)} %collective-permute-done.13.refs_3_) | copy-start | bytes 1966084
  89.3 8.8 %collective-permute-start.14 = (bf16[2,2,320,128]{3,2,1,0:T(8,128)(2,1)}, bf16[2,2,320,128]{3,2,1,0:T(8,128)(2,1)}, u32[]{:S(2)}, u32[]{:S(2)}) collective-permute-start(bf16[2,2,320,128]{3,2,1,0:T(8,128)(2,1)} %slice.43), channel_id=1, source_target_pairs={{0,8},{1,9},{2,10},{3,11},{4,12},{5,13},{6,14},{7,15},{8,16},{9,17... | collective-permute-start | bytes 983048 | tf_op jit(solution)/shard_map/ppermute | solution.py:23
  90.2 0.9 copy-start.4
  91.2 7.0 %collective-permute-start.15 = (bf16[2,2,320,128]{3,2,1,0:T(8,128)(2,1)}, bf16[2,2,320,128]{3,2,1,0:T(8,128)(2,1)}, u32[]{:S(2)}, u32[]{:S(2)}) collective-permute-start(bf16[2,2,320,128]{3,2,1,0:T(8,128)(2,1)} %slice.44), channel_id=1, source_target_pairs={{0,24},{1,25},{2,26},{3,27},{4,28},{5,29},{6,30},{7,31},{8,0},{9,1... | collective-permute-start | bytes 983048 | tf_op jit(solution)/shard_map/ppermute | solution.py:23
  93.0 6.4 %copy-start.3 = (bf16[4,2,320,128]{3,2,1,0:T(8,128)(2,1)S(1)}, bf16[4,2,320,128]{3,2,1,0:T(8,128)(2,1)}, u32[]{:S(2)}) copy-start(bf16[4,2,320,128]{3,2,1,0:T(8,128)(2,1)} %copy-done.2) | copy-start | bytes 1966084
  93.0 6.4 %copy-start.5 = (bf16[4,2,320,128]{3,2,1,0:T(8,128)(2,1)S(1)}, bf16[4,2,320,128]{3,2,1,0:T(8,128)(2,1)}, u32[]{:S(2)}) copy-start(bf16[4,2,320,128]{3,2,1,0:T(8,128)(2,1)} %copy-done.4) | copy-start | bytes 1966084
  93.0 6.4 %copy-start.8 = (bf16[2,320,128]{2,1,0:T(8,128)(2,1)S(1)}, bf16[2,320,128]{2,1,0:T(8,128)(2,1)}, u32[]{:S(2)}) copy-start(bf16[2,320,128]{2,1,0:T(8,128)(2,1)} %copy-done.7) | copy-start | bytes 491524
  93.0 6.4 %copy-start.10 = (bf16[2,320,128]{2,1,0:T(8,128)(2,1)S(1)}, bf16[2,320,128]{2,1,0:T(8,128)(2,1)}, u32[]{:S(2)}) copy-start(bf16[2,320,128]{2,1,0:T(8,128)(2,1)} %copy-done.9) | copy-start | bytes 491524
  93.0 6.4 %copy-start.12 = (bf16[2,320,128]{2,1,0:T(8,128)(2,1)S(1)}, bf16[2,320,128]{2,1,0:T(8,128)(2,1)}, u32[]{:S(2)}) copy-start(bf16[2,320,128]{2,1,0:T(8,128)(2,1)} %copy-done.11) | copy-start | bytes 491524
  93.0 4.6 %collective-permute-start.22 = (bf16[2,160,128]{2,1,0:T(8,128)(2,1)S(1)}, bf16[2,160,128]{2,1,0:T(8,128)(2,1)S(1)}, u32[]{:S(2)}, u32[]{:S(2)}) collective-permute-start(bf16[2,160,128]{2,1,0:T(8,128)(2,1)S(1)} %slice.45), channel_id=1, source_target_pairs={{0,32},{1,33},{2,34},{3,35},{4,36},{5,37},{6,38},{7,39},{8,40},{9,... | collective-permute-start | bytes 245768 | tf_op jit(solution)/shard_map/ppermute | solution.py:23
  94.1 4.0 %collective-permute-start.23 = (bf16[2,160,128]{2,1,0:T(8,128)(2,1)S(1)}, bf16[2,160,128]{2,1,0:T(8,128)(2,1)S(1)}, u32[]{:S(2)}, u32[]{:S(2)}) collective-permute-start(bf16[2,160,128]{2,1,0:T(8,128)(2,1)S(1)} %slice.46), channel_id=1, source_target_pairs={{0,224},{1,225},{2,226},{3,227},{4,228},{5,229},{6,230},{7,231},{8... | collective-permute-start | bytes 245768 | tf_op jit(solution)/shard_map/ppermute | solution.py:23
  102.2 8.3 %collective-permute-start.24 = (f32[4,256,256]{2,1,0:T(8,128)S(1)}, f32[4,256,256]{2,1,0:T(8,128)S(1)}, u32[]{:S(2)}, u32[]{:S(2)}) collective-permute-start(f32[4,256,256]{2,1,0:T(8,128)S(1)} %get-tuple-element.23), channel_id=1, source_target_pairs={{0,1},{1,0},{2,3},{3,2},{4,5},{5,4},{6,7},{7,6},{8,9},{9,8},{10,11... | collective-permute-start | bytes 3145736 | tf_op jit(solution)/shard_map/ppermute | solution.py:23
  110.7 6.5 %collective-permute-start.27 = (bf16[256,256]{1,0:T(8,128)(2,1)S(1)}, bf16[256,256]{1,0:T(8,128)(2,1)S(1)}, u32[]{:S(2)}, u32[]{:S(2)}) collective-permute-start(bf16[256,256]{1,0:T(8,128)(2,1)S(1)} %get-tuple-element.25), channel_id=1, source_target_pairs={{0,16},{1,17},{2,18},{3,19},{4,20},{5,21},{6,22},{7,23},{8,24},{9,... | collective-permute-start | bytes 393224 | tf_op jit(solution)/shard_map/ppermute | solution.py:23
  111.8 8.7 %collective-permute-start.26 = (bf16[256,256]{1,0:T(8,128)(2,1)S(1)}, bf16[256,256]{1,0:T(8,128)(2,1)S(1)}, u32[]{:S(2)}, u32[]{:S(2)}) collective-permute-start(bf16[256,256]{1,0:T(8,128)(2,1)S(1)} %get-tuple-element.26), channel_id=1, source_target_pairs={{0,8},{1,9},{2,10},{3,11},{4,12},{5,13},{6,14},{7,15},{8,16},{9,17... | collective-permute-start | bytes 393224 | tf_op jit(solution)/shard_map/ppermute | solution.py:23
  113.4 9.0 %collective-permute-start.25 = (bf16[256,256]{1,0:T(8,128)(2,1)S(1)}, bf16[256,256]{1,0:T(8,128)(2,1)S(1)}, u32[]{:S(2)}, u32[]{:S(2)}) collective-permute-start(bf16[256,256]{1,0:T(8,128)(2,1)S(1)} %get-tuple-element.27), channel_id=1, source_target_pairs={{0,24},{1,25},{2,26},{3,27},{4,28},{5,29},{6,30},{7,31},{8,0},{9,1... | collective-permute-start | bytes 393224 | tf_op jit(solution)/shard_map/ppermute | solution.py:23
